TPU v7x, 32 devices: a whole 2x2x4 slice. The times are simulated.
32 devices in a mesh: dp: 4 (over x, core), ctx: 8 (over z, y).
Axes of the slice: x: 2, y: 2, z: 4, core: 2. Of those that a mesh axis runs over, the one named last changes fastest.
Arguments:
- tokens: bfloat16 [4096, 1536], P(('dp', 'ctx')), may hold values from -6 to 6
- cotangent: bfloat16 [4096, 1536], P(('dp', 'ctx')), may hold values from -6 to 6
- gain_attn: bfloat16 [1536], P(('dp', 'ctx')), may hold values from 0.5 to 1.5
- w_query: bfloat16 [1536, 1536], P(('dp', 'ctx')), may hold values from -0.1875 to 0.1875
- key_weight: bfloat16 [1536, 768], P(('dp', 'ctx')), may hold values from -0.1875 to 0.1875
- value_weight: bfloat16 [1536, 768], P(('dp', 'ctx')), may hold values from -0.15625 to 0.15625
- w_out: bfloat16 [1536, 1536], P(('dp', 'ctx')), may hold values from -2.5 to 2.5
- gain_ffn: bfloat16 [1536], P(('dp', 'ctx')), may hold values from 0.29882812 to 3
- w_gate: bfloat16 [1536, 4096], P(('dp', 'ctx')), may hold values from -0.15625 to 0.15625
- w_up: bfloat16 [1536, 4096], P(('dp', 'ctx')), may hold values from -0.15625 to 0.15625
- w_down: bfloat16 [4096, 1536], P(('dp', 'ctx')), may hold values from -0.1875 to 0.1875
Outputs:
- output: bfloat16 [4096, 1536], P(('dp', 'ctx'))
- grad_tokens: float32 [4096, 1536], P(('dp', 'ctx'))
- grad_gain_attn: float32 [1536], P(('dp', 'ctx'))
- grad_w_query: float32 [1536, 1536], P(('dp', 'ctx'))
- grad_w_key: float32 [1536, 768], P(('dp', 'ctx'))
- grad_w_value: float32 [1536, 768], P(('dp', 'ctx'))
- grad_w_out: float32 [1536, 1536], P(('dp', 'ctx'))
- grad_gain_ffn: float32 [1536], P(('dp', 'ctx'))
- grad_w_gate: float32 [1536, 4096], P(('dp', 'ctx'))
- grad_w_up: float32 [1536, 4096], P(('dp', 'ctx'))
- grad_w_down: float32 [4096, 1536], P(('dp', 'ctx'))
All inputs are finite; a program needn't handle non-finite values.
Results may differ from a plain program's by a relative error of at most 0.028.
Values may be sent and summed in bfloat16 or wider, within the bound.
A program may use at most 320 MiB of HBM per device.

v0:
```python
import jax
import jax.numpy as jnp
from jax import lax
from jax.sharding import PartitionSpec as P

QUERY_HEADS = 16
KEY_VALUE_HEADS = 8
HEAD_SIZE = 96


NORM_EPS = 1e-05
ROPE_THETA = 100000.0
MASK_FILL = -1e30


def passed_along(value, axis, by):
    peers = lax.axis_size(axis)
    pairs = [(i, i + by) for i in range(peers) if 0 <= i + by < peers]
    return lax.ppermute(value, axis, pairs)


def shifted(block, axis, distance):
    devices = range(lax.axis_size(axis))
    route = [((i - distance) % len(devices), i) for i in devices]
    return lax.ppermute(block, axis, route)


def rope_tables(first_row, block_count):
    half_dim = HEAD_SIZE // 2
    positions = (first_row + jnp.arange(block_count, dtype=jnp.int32)).astype(jnp.float32)
    frequency = ROPE_THETA ** (-jnp.arange(half_dim, dtype=jnp.float32) * 2.0 / HEAD_SIZE)
    angles = positions[:, None] * frequency[None, :]
    return (jnp.cos(angles)[:, None, :], jnp.sin(angles)[:, None, :])


def apply_rotary(value_rows, cosine_table, sine_values, direction):
    half_dim = HEAD_SIZE // 2
    first_half = value_rows[..., :half_dim]
    second_half = value_rows[..., half_dim:]
    return jnp.concatenate(
        [
            first_half * cosine_table - direction * second_half * sine_values,
            second_half * cosine_table + direction * first_half * sine_values,
        ],
        axis=-1,
    )


def norm_back(grad_normed, inputs, inv_root, gain):
    grad_gain = jnp.sum(grad_normed * inputs * inv_root, axis=0)
    scaled = grad_normed * gain.astype(jnp.float32)
    grad_inputs = inv_root * (
        scaled - inputs * inv_root * inv_root * jnp.mean(scaled * inputs, axis=-1, keepdims=True)
    )
    return (grad_gain, grad_inputs)


def row_product(left, right):
    return jnp.einsum("tc,tf->cf", left, right, preferred_element_type=jnp.float32)


def per_device(
    tokens,
    cotangent,
    gain_attn,
    w_query,
    key_weight,
    value_weight,
    w_out,
    gain_ffn,
    w_gate,
    w_up,
    w_down,
):
    token_rows = tokens.shape[0]
    head_group = QUERY_HEADS // KEY_VALUE_HEADS
    key_value_width = KEY_VALUE_HEADS * HEAD_SIZE
    query_width = QUERY_HEADS * HEAD_SIZE
    score_scale = HEAD_SIZE ** (-0.5)
    ctx_count = lax.axis_size("ctx")
    ctx_rank = lax.axis_index("ctx")
    first_row = ctx_rank * token_rows
    query_pos = first_row + jnp.arange(token_rows, dtype=jnp.int32)
    attn_full = (
        lax.all_gather(gain_attn, ("dp", "ctx"), axis=0, tiled=True),
        lax.all_gather(w_query, ("dp", "ctx"), axis=0, tiled=True),
        lax.all_gather(key_weight, ("dp", "ctx"), axis=0, tiled=True),
        lax.all_gather(value_weight, ("dp", "ctx"), axis=0, tiled=True),
        lax.all_gather(w_out, ("dp", "ctx"), axis=0, tiled=True),
    )
    gain_one, query_full, key_full, value_full, out_full = attn_full
    inputs = tokens.astype(jnp.float32)
    inv_one = lax.rsqrt(jnp.mean(inputs * inputs, axis=-1, keepdims=True) + NORM_EPS)
    first_normed = (inputs * inv_one * gain_one.astype(jnp.float32)).astype(jnp.bfloat16)
    query_unrotated = jnp.dot(first_normed, query_full, preferred_element_type=jnp.float32).reshape(
        token_rows, QUERY_HEADS, HEAD_SIZE
    )
    key_unrotated = jnp.dot(first_normed, key_full, preferred_element_type=jnp.float32).reshape(
        token_rows, KEY_VALUE_HEADS, HEAD_SIZE
    )
    value_raw = jnp.dot(first_normed, value_full, preferred_element_type=jnp.float32)
    cosine_table, sine_values = rope_tables(first_row, token_rows)
    query_rows = (
        apply_rotary(query_unrotated, cosine_table, sine_values, 1.0)
        .astype(jnp.bfloat16)
        .reshape(token_rows, KEY_VALUE_HEADS, head_group, HEAD_SIZE)
    )
    keys_rot = (
        apply_rotary(key_unrotated, cosine_table, sine_values, 1.0)
        .astype(jnp.bfloat16)
        .reshape(token_rows, key_value_width)
    )
    kv_local = jnp.concatenate([keys_rot, value_raw.astype(jnp.bfloat16)], axis=1)
    starting = (
        jnp.full((KEY_VALUE_HEADS, head_group, token_rows), MASK_FILL, jnp.float32),
        jnp.zeros((KEY_VALUE_HEADS, head_group, token_rows), jnp.float32),
        jnp.zeros((token_rows, KEY_VALUE_HEADS, head_group, HEAD_SIZE), jnp.float32),
    )
    sequence_portion = lax.all_gather(kv_local, "ctx", axis=0, tiled=True)

    def update(state):
        run_max, run_sum, run_acc = state
        block_count = sequence_portion.shape[0]
        key_portion = sequence_portion[:, :key_value_width].reshape(
            block_count, KEY_VALUE_HEADS, HEAD_SIZE
        )
        value_portion = sequence_portion[:, key_value_width:].reshape(
            block_count, KEY_VALUE_HEADS, HEAD_SIZE
        )
        scores = (
            jnp.einsum(
                "tkgd,skd->kgts", query_rows, key_portion, preferred_element_type=jnp.float32
            )
            * score_scale
        )
        key_pos = jnp.arange(block_count, dtype=jnp.int32)
        allowed = key_pos[None, :] <= query_pos[:, None]
        scores = jnp.where(allowed, scores, MASK_FILL)
        new_max = jnp.maximum(run_max, jnp.max(scores, axis=-1))
        expo = jnp.exp(scores - new_max[..., None])
        new_sum = jnp.sum(expo, axis=-1)
        added = jnp.einsum(
            "kgts,skd->tkgd",
            expo.astype(jnp.bfloat16),
            value_portion,
            preferred_element_type=jnp.float32,
        )
        return (new_max, new_sum, added)

    def unchanged(state):
        return state

    run_max, run_sum, run_acc = lax.cond(
        jnp.int32(0) <= first_row + token_rows - 1, update, unchanged, starting
    )
    attn_four = run_acc / jnp.transpose(run_sum, (2, 0, 1))[..., None]
    log_total = run_max + jnp.log(run_sum)
    attn_out = attn_four.reshape(token_rows, query_width)
    attn_low = attn_out.astype(jnp.bfloat16)
    middle = inputs + jnp.dot(attn_low, out_full, preferred_element_type=jnp.float32)
    mlp_full = (
        lax.all_gather(gain_ffn, ("dp", "ctx"), axis=0, tiled=True),
        lax.all_gather(w_gate, ("dp", "ctx"), axis=0, tiled=True),
        lax.all_gather(w_up, ("dp", "ctx"), axis=0, tiled=True),
        lax.all_gather(w_down, ("dp", "ctx"), axis=0, tiled=True),
    )
    gain_two, gate_full, up_full, down_full = mlp_full
    inv_two = lax.rsqrt(jnp.mean(middle * middle, axis=-1, keepdims=True) + NORM_EPS)
    normed_two = (middle * inv_two * gain_two.astype(jnp.float32)).astype(jnp.bfloat16)
    gate_value = jnp.dot(normed_two, gate_full, preferred_element_type=jnp.float32)
    up_value = jnp.dot(normed_two, up_full, preferred_element_type=jnp.float32)
    sigmoid_gate = jax.nn.sigmoid(gate_value)
    silu_gate = gate_value * sigmoid_gate
    hidden = (silu_gate * up_value).astype(jnp.bfloat16)
    output = (middle + jnp.dot(hidden, down_full, preferred_element_type=jnp.float32)).astype(
        jnp.bfloat16
    )
    mlp_back = (
        lax.all_gather(gain_ffn, ("dp", "ctx"), axis=0, tiled=True),
        lax.all_gather(w_gate, ("dp", "ctx"), axis=0, tiled=True),
        lax.all_gather(w_up, ("dp", "ctx"), axis=0, tiled=True),
        lax.all_gather(w_down, ("dp", "ctx"), axis=0, tiled=True),
    )
    gain_two_back, gate_back, up_back, down_back = mlp_back
    grad_out = cotangent.astype(jnp.float32)
    grad_hidden = jnp.einsum("td,fd->tf", cotangent, down_back, preferred_element_type=jnp.float32)
    grad_gate = (
        grad_hidden * up_value * sigmoid_gate * (1.0 + gate_value * (1.0 - sigmoid_gate))
    ).astype(jnp.bfloat16)
    grad_up = (grad_hidden * silu_gate).astype(jnp.bfloat16)
    grad_normed_two = jnp.einsum(
        "tf,cf->tc", grad_gate, gate_back, preferred_element_type=jnp.float32
    ) + jnp.einsum("tf,cf->tc", grad_up, up_back, preferred_element_type=jnp.float32)
    grad_gain_two, grad_middle_norm = norm_back(grad_normed_two, middle, inv_two, gain_two_back)
    grad_middle = grad_out + grad_middle_norm
    gate_up_pair = jnp.concatenate([grad_gate, grad_up], axis=1)
    gate_up_sum = lax.psum_scatter(
        row_product(normed_two, gate_up_pair), ("dp", "ctx"), scatter_dimension=0, tiled=True
    )
    grad_down_sum = lax.psum_scatter(
        row_product(hidden, cotangent), ("dp", "ctx"), scatter_dimension=0, tiled=True
    )
    attn_back = (
        lax.all_gather(gain_attn, ("dp", "ctx"), axis=0, tiled=True),
        lax.all_gather(w_query, ("dp", "ctx"), axis=0, tiled=True),
        lax.all_gather(key_weight, ("dp", "ctx"), axis=0, tiled=True),
        lax.all_gather(value_weight, ("dp", "ctx"), axis=0, tiled=True),
        lax.all_gather(w_out, ("dp", "ctx"), axis=0, tiled=True),
    )
    gain_one_back, query_back, key_back, value_back, out_back = attn_back
    grad_branch = grad_middle.astype(jnp.bfloat16)
    attention_gradient = jnp.einsum(
        "td,cd->tc", grad_branch, out_back, preferred_element_type=jnp.float32
    ).astype(jnp.bfloat16)
    gradient_quad = attention_gradient.reshape(token_rows, KEY_VALUE_HEADS, head_group, HEAD_SIZE)
    delta_rows = jnp.transpose(
        jnp.sum(gradient_quad.astype(jnp.float32) * attn_four, axis=-1), (1, 2, 0)
    )

    def pair_terms(key_value_block, key_first):
        block_count = key_value_block.shape[0]
        key_portion = key_value_block[:, :key_value_width].reshape(
            block_count, KEY_VALUE_HEADS, HEAD_SIZE
        )
        value_portion = key_value_block[:, key_value_width:].reshape(
            block_count, KEY_VALUE_HEADS, HEAD_SIZE
        )
        scores = (
            jnp.einsum(
                "tkgd,skd->kgts", query_rows, key_portion, preferred_element_type=jnp.float32
            )
            * score_scale
        )
        key_pos = key_first + jnp.arange(block_count, dtype=jnp.int32)
        allowed = key_pos[None, :] <= query_pos[:, None]
        scores = jnp.where(allowed, scores, MASK_FILL)
        probs = jnp.exp(scores - log_total[..., None])
        grad_probs = jnp.einsum(
            "tkgd,skd->kgts", gradient_quad, value_portion, preferred_element_type=jnp.float32
        )
        grad_scores = (probs * (grad_probs - delta_rows[..., None])).astype(jnp.bfloat16)
        grad_query = (
            jnp.einsum(
                "kgts,skd->tkgd", grad_scores, key_portion, preferred_element_type=jnp.float32
            )
            * score_scale
        )
        grad_keys = (
            jnp.einsum(
                "kgts,tkgd->skd", grad_scores, query_rows, preferred_element_type=jnp.float32
            )
            * score_scale
        )
        grad_values = jnp.einsum(
            "kgts,tkgd->skd",
            probs.astype(jnp.bfloat16),
            gradient_quad,
            preferred_element_type=jnp.float32,
        )
        return (
            grad_query,
            jnp.concatenate(
                [
                    grad_keys.reshape(block_count, key_value_width),
                    grad_values.reshape(block_count, key_value_width),
                ],
                axis=1,
            ),
        )

    def add_pair(operands):
        kv_use, key_first, grad_query, grad_now = operands
        more_query, more_kv = pair_terms(kv_use, key_first)
        return (grad_query + more_query, grad_now + more_kv)

    def keep_pair(operands):
        return (operands[2], operands[3])

    def cycle_step(step, state):
        kv_now, grad_now, grad_query = state
        owner = (ctx_rank - step + ctx_count) % ctx_count
        kv_next = passed_along(kv_now, "ctx", 1)
        grad_query, grad_now = lax.cond(
            owner <= ctx_rank,
            add_pair,
            keep_pair,
            (kv_now, owner * token_rows, grad_query, grad_now),
        )
        grad_next = shifted(grad_now.astype(jnp.bfloat16), "ctx", 1).astype(grad_now.dtype)
        return (kv_next, grad_next, grad_query)

    cycle_start = (
        kv_local,
        jnp.zeros((token_rows, 2 * key_value_width), jnp.float32),
        jnp.zeros((token_rows, KEY_VALUE_HEADS, head_group, HEAD_SIZE), jnp.float32),
    )
    kv_final, key_value_gradient, grad_query = lax.fori_loop(0, ctx_count, cycle_step, cycle_start)
    grad_query_raw = (
        apply_rotary(
            grad_query.reshape(token_rows, QUERY_HEADS, HEAD_SIZE), cosine_table, sine_values, -1.0
        )
        .reshape(token_rows, query_width)
        .astype(jnp.bfloat16)
    )
    grad_key_raw = (
        apply_rotary(
            key_value_gradient[:, :key_value_width].reshape(token_rows, KEY_VALUE_HEADS, HEAD_SIZE),
            cosine_table,
            sine_values,
            -1.0,
        )
        .reshape(token_rows, key_value_width)
        .astype(jnp.bfloat16)
    )
    grad_value_raw = key_value_gradient[:, key_value_width:].astype(jnp.bfloat16)
    grad_normed_one = (
        jnp.einsum("tq,cq->tc", grad_query_raw, query_back, preferred_element_type=jnp.float32)
        + jnp.einsum("tq,cq->tc", grad_key_raw, key_back, preferred_element_type=jnp.float32)
        + jnp.einsum("tq,cq->tc", grad_value_raw, value_back, preferred_element_type=jnp.float32)
    )
    grad_gain_one, grad_input_norm = norm_back(grad_normed_one, inputs, inv_one, gain_one_back)
    grad_tokens = grad_middle + grad_input_norm
    projection_grads = jnp.concatenate([grad_query_raw, grad_key_raw, grad_value_raw], axis=1)
    qkv_sum = lax.psum_scatter(
        row_product(first_normed, projection_grads), ("dp", "ctx"), scatter_dimension=0, tiled=True
    )
    grad_out_sum = lax.psum_scatter(
        row_product(attn_low, grad_branch), ("dp", "ctx"), scatter_dimension=0, tiled=True
    )
    gain_sums = (
        lax.psum_scatter(grad_gain_one, ("dp", "ctx"), scatter_dimension=0, tiled=True),
        lax.psum_scatter(grad_gain_two, ("dp", "ctx"), scatter_dimension=0, tiled=True),
    )
    ff_width = w_gate.shape[1]
    return (
        output,
        grad_tokens,
        gain_sums[0],
        qkv_sum[:, :query_width],
        qkv_sum[:, query_width : query_width + key_value_width],
        qkv_sum[:, query_width + key_value_width :],
        grad_out_sum,
        gain_sums[1],
        gate_up_sum[:, :ff_width],
        gate_up_sum[:, ff_width:],
        grad_down_sum,
    )


def solution(mesh):
    return jax.shard_map(
        per_device,
        mesh=mesh,
        in_specs=(
            P(("dp", "ctx"), None),
            P(("dp", "ctx"), None),
            P(("dp", "ctx")),
            P(("dp", "ctx"), None),
            P(("dp", "ctx"), None),
            P(("dp", "ctx"), None),
            P(("dp", "ctx"), None),
            P(("dp", "ctx")),
            P(("dp", "ctx"), None),
            P(("dp", "ctx"), None),
            P(("dp", "ctx"), None),
        ),
        out_specs=(
            P(("dp", "ctx"), None),
            P(("dp", "ctx"), None),
            P(("dp", "ctx")),
            P(("dp", "ctx"), None),
            P(("dp", "ctx"), None),
            P(("dp", "ctx"), None),
            P(("dp", "ctx"), None),
            P(("dp", "ctx")),
            P(("dp", "ctx"), None),
            P(("dp", "ctx"), None),
            P(("dp", "ctx"), None),
        ),
        check_vma=False,
    )
```

profile of v0, /device:TPU:0, one launch (start us, length us, event | category | flops | bytes accessed | tf_op | source)
XLA Modules:
  0.0 1890.8 jit_solution(12456435151676652126)
XLA Ops:
  11.2 42.1 %all-reduce.5 = (bf16[1536]{0:T(1024)(128)(2,1)S(1)}, bf16[1536]{0:T(1024)(128)(2,1)S(1)}) all-reduce(bf16[1536]{0:T(1024)(128)(2,1)S(1)} %dynamic-update-slice, bf16[1536]{0:T(1024)(128)(2,1)S(1)} %dynamic-update-slice.1), channel_id=1, replica_groups=mesh['dp'=4,'ctx'=8] {'dp','ctx'}, use_global_device_ids=true, to_apply=%add | all-reduce | flops 3072 | bytes 12288
  54.6 16.4 all-gather.9.cloned.1.call-done
  71.0 2.9 fusion.59
  74.1 56.0 %all-gather.11.cloned.1.call-done = bf16[1536,768]{1,0:T(8,128)(2,1)} async-done(((bf16[48,768]{1,0:T(8,128)(2,1)}), bf16[1536,768]{1,0:T(8,128)(2,1)}) %all-gather.11.cloned.1.call-update) | async-done | bytes 2359312 | tf_op jit(solution)/shard_map/all_gather | solution.py:88
  130.2 2.2 convolution_convert_fusion.1
  135.9 1.9 copy.56
  137.8 57.9 %all-gather.15.cloned.1.call-done = bf16[1536,1536]{1,0:T(8,128)(2,1)} async-done(((bf16[48,1536]{1,0:T(8,128)(2,1)}), bf16[1536,1536]{1,0:T(8,128)(2,1)}) %all-gather.15.cloned.1.call-update) | async-done | bytes 4718608 | tf_op jit(solution)/shard_map/all_gather | solution.py:86
  195.7 4.3 fusion.56
  200.2 57.4 %all-gather.13.cloned.1.call-done = bf16[1024,1536]{1,0:T(8,128)(2,1)} async-done(((bf16[128,1536]{1,0:T(8,128)(2,1)}), bf16[1024,1536]{1,0:T(8,128)(2,1)}) %all-gather.13.cloned.1.call-update) | async-done | bytes 3145744 | tf_op jit(solution)/shard_map/all_gather | solution.py:119
  257.6 15.7 conditional.2
  257.7 4.8 copy.54
  262.5 2.2 fusion.61
  266.9 3.0 fusion.3
  269.9 2.7 fusion.8
  274.8 47.9 %all-gather.17.cloned.1.call-done = bf16[1536,1536]{1,0:T(8,128)(2,1)} async-done(((bf16[48,1536]{1,0:T(8,128)(2,1)}), bf16[1536,1536]{1,0:T(8,128)(2,1)}) %all-gather.17.cloned.1.call-update) | async-done | bytes 4718608 | tf_op jit(solution)/shard_map/all_gather | solution.py:89
  322.7 3.2 multiply_reduce_fusion.3
  326.1 94.2 %all-gather.19.cloned.1.call-done = bf16[1536,4096]{1,0:T(8,128)(2,1)} async-done(((bf16[48,4096]{1,0:T(8,128)(2,1)}), bf16[1536,4096]{1,0:T(8,128)(2,1)}) %all-gather.19.cloned.1.call-update) | async-done | bytes 12582928 | tf_op jit(solution)/shard_map/all_gather | solution.py:163
  420.3 7.7 fusion.66
  428.0 89.5 %all-gather.21.cloned.1.call-done = bf16[1536,4096]{1,0:T(8,128)(2,1)} async-done(((bf16[48,4096]{1,0:T(8,128)(2,1)}), bf16[1536,4096]{1,0:T(8,128)(2,1)}) %all-gather.21.cloned.1.call-update) | async-done | bytes 12582928 | tf_op jit(solution)/shard_map/all_gather | solution.py:164
  517.5 7.7 fusion.67
  525.2 89.5 %all-gather.23.cloned.1.call-done = bf16[4096,1536]{1,0:T(8,128)(2,1)} async-done(((bf16[128,1536]{1,0:T(8,128)(2,1)}), bf16[4096,1536]{1,0:T(8,128)(2,1)}) %all-gather.23.cloned.1.call-update) | async-done | bytes 12582928 | tf_op jit(solution)/shard_map/all_gather | solution.py:165
  614.7 11.9 multiply_convert_fusion
  626.6 10.2 fusion.68
  636.8 6.7 multiply_reduce_fusion
  645.8 4.1 convolution_convert_fusion
  651.0 178.5 %while.20 = (s32[]{:T(128)}, bf16[128,1536]{0,1:T(8,128)(2,1)S(1)}, f32[128,1536]{0,1:T(8,128)}, f32[128,8,2,96]{0,3,2,1:T(8,128)S(1)}, s32[]{:T(128)}, /*index=...) while((s32[]{:T(128)}, bf16[128,1536]{0,1:T(8,128)(2,1)S(1)}, ...), condition=%wide.region_11.12_spmd.clone, body=%wide.region_8.11_spmd.clone.sunk | while | flops 254984464 | bytes 20303356 | solution.py:297
  651.2 3.6 conditional.5
  657.1 2.8 collective-permute-start
  659.9 9.9 collective-permute-done.1
  670.7 3.8 collective-permute-done
  676.6 6.1 collective-permute-start.1
  682.7 3.7 collective-permute-start
  686.4 6.2 collective-permute-done.1
  693.5 5.8 collective-permute-done
  701.3 2.5 collective-permute-start.1
  703.8 8.2 collective-permute-start
  712.0 4.4 collective-permute-done.1
  717.4 2.1 collective-permute-done
  721.6 6.3 collective-permute-start.1
  727.9 5.3 collective-permute-start
  733.2 7.1 collective-permute-done.1
  744.7 3.4 collective-permute-start.1
  748.1 5.3 collective-permute-start
  753.4 9.8 collective-permute-done.1
  767.6 5.3 collective-permute-start
  772.9 12.7 collective-permute-done.1
  788.6 6.1 collective-permute-start
  794.7 12.8 collective-permute-done.1
  810.6 2.6 collective-permute-start
  813.2 15.4 collective-permute-done.1
  832.5 9.4 fusion.42
  843.6 23.0 %fusion.26 = f32[1536,8192]{1,0:T(8,128)} fusion(bf16[128,1536]{1,0:T(8,128)(2,1)S(1)} %copy-done.10, bf16[128,4096]{1,0:T(8,128)(2,1)S(1)} %copy-done.16, bf16[128,4096]{1,0:T(8,128)(2,1)S(1)} %copy-done.17), kind=kOutput, calls=%fused_computation.41 | convolution fusion | flops 3225419776 | bytes 52822016 | tf_op jit(solution)/shard_map/tc,tf->cf/dot_general | solution.py:59
  867.9 5.3 fusion.49
  874.6 11.9 fusion.70
  886.6 4.6 fusion.69
  891.2 2.8 convolution_add_fusion.1
  895.9 46.5 %all-reduce.4 = (f32[1536]{0:T(1024)S(1)}, f32[1536]{0:T(1024)S(1)}) all-reduce(f32[1536]{0:T(1024)S(1)} %get-tuple-element.415, f32[1536]{0:T(1024)S(1)} %get-tuple-element.413), channel_id=2, replica_groups=mesh['dp'=4,'ctx'=8] {'dp','ctx'}, use_global_device_ids=true, to_apply=%region_14.15.clone | all-reduce | flops 3072 | bytes 24576
  943.6 2.3 fusion.37
  945.9 7.3 fusion.25
  953.2 100.3 %reduce-scatter.5.cloned.1.call-done = f32[48,3072]{1,0:T(8,128)} async-done(((f32[1536,3072]{1,0:T(8,128)}), f32[48,3072]{1,0:T(8,128)}) %reduce-scatter.5.cloned.1.call-update) | async-done | bytes 589840 | tf_op jit(solution)/shard_map/reduce_scatter | solution.py:324
  1056.9 433.4 %reduce-scatter.9.cloned.1.call-done = f32[48,8192]{1,0:T(8,128)} async-done(((f32[1536,8192]{1,0:T(8,128)}), f32[48,8192]{1,0:T(8,128)}) %reduce-scatter.9.cloned.1.call-update) | async-done | bytes 1572880 | tf_op jit(solution)/shard_map/reduce_scatter | solution.py:197
  1490.2 2.6 fusion.63
  1492.9 138.5 %reduce-scatter.7.cloned.1.call-done = f32[48,1536]{1,0:T(8,128)} async-done(((f32[1536,1536]{1,0:T(8,128)}), f32[48,1536]{1,0:T(8,128)}) %reduce-scatter.7.cloned.1.call-update) | async-done | bytes 294928 | tf_op jit(solution)/shard_map/reduce_scatter | solution.py:327
  1631.4 252.4 %reduce-scatter.11.cloned.1.call-done = f32[128,1536]{1,0:T(8,128)} async-done(((f32[4096,1536]{1,0:T(8,128)}), f32[128,1536]{1,0:T(8,128)}) %reduce-scatter.11.cloned.1.call-update) | async-done | bytes 786448 | tf_op jit(solution)/shard_map/reduce_scatter | solution.py:200
  (179 shorter events, 61.4 us)
Async XLA Ops:
  7.2 123.0 %copy-start.2 = (bf16[128,1536]{1,0:T(8,128)(2,1)S(1)}, bf16[128,1536]{1,0:T(8,128)(2,1)}, u32[]{:S(2)}) copy-start(bf16[128,1536]{1,0:T(8,128)(2,1)} %param.17) | copy-start | bytes 1179652
  7.2 63.8 %all-gather.9.cloned.1.call-start = ((), (), s32[]{:S(2)}) async-start(), calls=%async_computation.4 | async-start | bytes 2433024 | tf_op jit(solution)/shard_map/all_gather | solution.py:87
  7.9 122.3 %all-gather.11.cloned.1.call-start = ((), (), s32[]{:S(2)}) async-start(), calls=%async_computation.5 | async-start | bytes 2433024 | tf_op jit(solution)/shard_map/all_gather | solution.py:88
  8.7 187.0 %all-gather.15.cloned.1.call-start = ((), (), s32[]{:S(2)}) async-start(), calls=%async_computation.7 | async-start | bytes 4866048 | tf_op jit(solution)/shard_map/all_gather | solution.py:86
  9.4 248.2 %all-gather.13.cloned.1.call-start = ((), (), s32[]{:S(2)}) async-start(), calls=%async_computation.6 | async-start | bytes 3538944 | tf_op jit(solution)/shard_map/all_gather | solution.py:119
  133.2 189.5 %all-gather.17.cloned.1.call-start = ((), (), s32[]{:S(2)}) async-start(), calls=%async_computation.8 | async-start | bytes 4866048 | tf_op jit(solution)/shard_map/all_gather | solution.py:89
  133.8 286.5 %all-gather.19.cloned.1.call-start = ((), (), s32[]{:S(2)}) async-start(), calls=%async_computation.9 | async-start | bytes 12976128 | tf_op jit(solution)/shard_map/all_gather | solution.py:163
  134.3 383.1 %all-gather.21.cloned.1.call-start = ((), (), s32[]{:S(2)}) async-start(), calls=%async_computation.10 | async-start | bytes 12976128 | tf_op jit(solution)/shard_map/all_gather | solution.py:164
  135.1 479.6 %all-gather.23.cloned.1.call-start = ((), (), s32[]{:S(2)}) async-start(), calls=%async_computation.11 | async-start | bytes 12976128 | tf_op jit(solution)/shard_map/all_gather | solution.py:165
  135.8 917.6 %reduce-scatter.5.cloned.1.call-start = ((), (), s32[]{:S(2)}) async-start(), calls=%async_computation.12 | async-start | bytes 19464192 | tf_op jit(solution)/shard_map/reduce_scatter | solution.py:324
  273.3 49.4 %copy-start.11 = (f32[128,8,2,96]{0,3,2,1:T(8,128)}, f32[128,8,2,96]{0,3,2,1:T(8,128)S(1)}, u32[]{:S(2)}) copy-start(f32[128,8,2,96]{0,3,2,1:T(8,128)S(1)} %get-tuple-element.327) | copy-start | bytes 2359300
  274.8 51.2 %copy-start.14 = (bf16[128,8,2,96]{0,3,2,1:T(8,128)(2,1)}, bf16[128,8,2,96]{0,3,2,1:T(8,128)(2,1)S(1)}, u32[]{:S(2)}) copy-start(bf16[128,8,2,96]{0,3,2,1:T(8,128)(2,1)S(1)} %fusion.48) | copy-start | bytes 1179652
  325.9 317.6 %copy-start.3 = (f32[128,1536]{1,0:T(8,128)}, f32[128,1536]{1,0:T(8,128)S(1)}, u32[]{:S(2)}) copy-start(f32[128,1536]{1,0:T(8,128)S(1)} %get-tuple-element.468) | copy-start | bytes 2359300
  326.1 191.4 %copy-start.9 = (bf16[128,1536]{1,0:T(8,128)(2,1)}, bf16[128,1536]{1,0:T(8,128)(2,1)S(1)}, u32[]{:S(2)}) copy-start(bf16[128,1536]{1,0:T(8,128)(2,1)S(1)} %multiply_convert_fusion.3) | copy-start | bytes 1179652
  428.0 186.7 %copy-start.20 = (bf16[128,1536]{1,0:T(8,128)(2,1)S(1)}, bf16[128,1536]{1,0:T(8,128)(2,1)}, u32[]{:S(2)}) copy-start(bf16[128,1536]{1,0:T(8,128)(2,1)} %param.18) | copy-start | bytes 1179652
  626.6 10.2 copy-start
  636.8 6.7 copy-start.21
  644.9 0.9 copy-start.6
  645.8 4.3 copy-start.12
  645.8 5.2 copy-start.5
  655.6 14.2 collective-permute-start.1
  657.1 17.4 collective-permute-start
  676.6 16.0 collective-permute-start.1
  682.7 16.6 collective-permute-start
  701.3 15.1 collective-permute-start.1
  703.8 15.7 collective-permute-start
  721.6 18.7 collective-permute-start.1
  727.9 14.8 collective-permute-start
  744.7 18.4 collective-permute-start.1
  748.1 16.0 collective-permute-start
  766.2 19.4 %collective-permute-start.1 = (bf16[128,1536]{0,1:T(8,128)(2,1)}, bf16[128,1536]{0,1:T(8,128)(2,1)S(1)}, u32[]{:S(2)}, u32[]{:S(2)}) collective-permute-start(bf16[128,1536]{0,1:T(8,128)(2,1)} %convert_element_type.203), channel_id=1, source_target_pairs={{7,0},{0,1},{1,2},{2,3},{3,4},{4,5},{5,6},{6,7},{15,8},{8,9},{9,10... | collective-permute-start | bytes 1179656 | tf_op jit(solution)/shard_map/while/body/eval_jaxpr/ppermute | solution.py:25
  767.6 18.9 %collective-permute-start = (bf16[128,1536]{0,1:T(8,128)(2,1)S(1)}, bf16[128,1536]{0,1:T(8,128)(2,1)S(1)}, u32[]{:S(2)}, u32[]{:S(2)}) collective-permute-start(bf16[128,1536]{0,1:T(8,128)(2,1)S(1)} %copy.88), channel_id=1, source_target_pairs={{0,1},{1,2},{2,3},{3,4},{4,5},{5,6},{6,7},{8,9},{9,10},{10,11},{11... | collective-permute-start | bytes 1179656 | tf_op jit(solution)/shard_map/while/body/eval_jaxpr/ppermute | solution.py:19
  788.6 19.0 %collective-permute-start.1 = (bf16[128,1536]{0,1:T(8,128)(2,1)}, bf16[128,1536]{0,1:T(8,128)(2,1)S(1)}, u32[]{:S(2)}, u32[]{:S(2)}) collective-permute-start(bf16[128,1536]{0,1:T(8,128)(2,1)} %convert_element_type.203), channel_id=1, source_target_pairs={{7,0},{0,1},{1,2},{2,3},{3,4},{4,5},{5,6},{6,7},{15,8},{8,9},{9,10... | collective-permute-start | bytes 1179656 | tf_op jit(solution)/shard_map/while/body/eval_jaxpr/ppermute | solution.py:25
  788.6 19.9 %collective-permute-start = (bf16[128,1536]{0,1:T(8,128)(2,1)S(1)}, bf16[128,1536]{0,1:T(8,128)(2,1)S(1)}, u32[]{:S(2)}, u32[]{:S(2)}) collective-permute-start(bf16[128,1536]{0,1:T(8,128)(2,1)S(1)} %copy.88), channel_id=1, source_target_pairs={{0,1},{1,2},{2,3},{3,4},{4,5},{5,6},{6,7},{8,9},{9,10},{10,11},{11... | collective-permute-start | bytes 1179656 | tf_op jit(solution)/shard_map/while/body/eval_jaxpr/ppermute | solution.py:19
  810.6 18.1 collective-permute-start.1
  810.6 19.0 %collective-permute-start = (bf16[128,1536]{0,1:T(8,128)(2,1)S(1)}, bf16[128,1536]{0,1:T(8,128)(2,1)S(1)}, u32[]{:S(2)}, u32[]{:S(2)}) collective-permute-start(bf16[128,1536]{0,1:T(8,128)(2,1)S(1)} %copy.88), channel_id=1, source_target_pairs={{0,1},{1,2},{2,3},{3,4},{4,5},{5,6},{6,7},{8,9},{9,10},{10,11},{11... | collective-permute-start | bytes 1179656 | tf_op jit(solution)/shard_map/while/body/eval_jaxpr/ppermute | solution.py:19
  831.9 0.7 copy-start.18
  841.9 1.0 copy-start.10
  841.9 1.3 copy-start.16
  841.9 1.7 copy-start.17
  841.9 648.3 %reduce-scatter.9.cloned.1.call-start = ((), (), s32[]{:S(2)}) async-start(), calls=%async_computation.14 | async-start | bytes 51904512 | tf_op jit(solution)/shard_map/reduce_scatter | solution.py:197
  866.5 1.2 copy-start.7
  866.5 1.3 copy-start.15
  866.6 764.8 %reduce-scatter.7.cloned.1.call-start = ((), (), s32[]{:S(2)}) async-start(), calls=%async_computation.13 | async-start | bytes 9732096 | tf_op jit(solution)/shard_map/reduce_scatter | solution.py:327
  873.2 1.3 copy-start.13
  873.2 1.4 copy-start.22
  873.2 1010.5 %reduce-scatter.11.cloned.1.call-start = ((), (), s32[]{:S(2)}) async-start(), calls=%async_computation.15 | async-start | bytes 25952256 | tf_op jit(solution)/shard_map/reduce_scatter | solution.py:200
  886.6 4.6 copy-start.19
  886.6 7.4 copy-start.1
  886.6 7.4 copy-start.8
  894.0 51.9 %copy-start.4 = (f32[128,1536]{1,0:T(8,128)S(1)}, f32[128,1536]{1,0:T(8,128)}, u32[]{:S(2)}) copy-start(f32[128,1536]{1,0:T(8,128)} %copy-done.3) | copy-start | bytes 2359300
Sparse Core Ops, SparseCore 0:
  10.9 60.0 all-gather.8
  73.9 56.2 all-gather.10
  133.1 62.5 all-gather.14
  198.3 59.2 all-gather.12
  260.4 62.2 all-gather.16
  325.4 94.8 all-gather.18
  423.2 94.2 all-gather.20
  520.4 94.2 all-gather.22
  842.1 211.3 reduce-scatter.4
  1059.8 430.4 reduce-scatter.8
  1496.7 134.5 reduce-scatter.6
  1639.3 244.3 reduce-scatter.10
where the time goes:
time: 1900 us; the launch traced here: 1890 us
  waiting for transfers between devices  1530 us (81%)
  matrix products  134 us (7%)
  blocking collectives  88.6 us (5%)
  starting transfers between devices  60.9 us (3%)
  other arithmetic  34.8 us (2%)
  local copies, waits for them, and re-layouts  27.7 us (1%)
    reduce_scatter x1, waiting for transfers between devices, per_device(): lax.psum_scatter(row_product(normed_two, gate_up_pair), ('dp', 'ctx'), sc...  433 us
    reduce_scatter x1, waiting for transfers between devices, per_device(): lax.psum_scatter(row_product(hidden, cotangent), ('dp', 'ctx'), scatter_d...  252 us
    reduce_scatter x1, waiting for transfers between devices, per_device(): lax.psum_scatter(row_product(attn_low, grad_branch), ('dp', 'ctx'), scatt...  139 us
    reduce_scatter x1, waiting for transfers between devices, per_device(): lax.psum_scatter(row_product(first_normed, projection_grads), ('dp', 'ctx...  100 us
    all_gather x1, waiting for transfers between devices, per_device(): lax.all_gather(w_gate, ('dp', 'ctx'), axis=0, tiled=True)  94.2 us
    all_gather x1, waiting for transfers between devices, per_device(): lax.all_gather(w_up, ('dp', 'ctx'), axis=0, tiled=True)  89.5 us
    all_gather x1, waiting for transfers between devices, per_device(): lax.all_gather(w_down, ('dp', 'ctx'), axis=0, tiled=True)  89.5 us
    unnamed x2, blocking collectives  88.6 us
  transfers between devices with their start and end apart: 28, of which 24 were waited for; matrix products, arithmetic and copies ran while one was open for 7% of the time, Pallas kernels for 0%

commit v1 on v0

--- a/solution.py
+++ b/solution.py
@@ -59,7 +59,7 @@
     return jnp.einsum("tc,tf->cf", left, right, preferred_element_type=jnp.float32)
 
 
-def per_device(
+def blockwise_layer(
     tokens,
     cotangent,
     gain_attn,
@@ -347,9 +347,190 @@
     )
 
 
+def weight_columns(weight, chunk_of, row_count):
+    by_share = lax.all_to_all(chunk_of(weight), "ctx", split_axis=0, concat_axis=0, tiled=True)
+    rows = by_share.reshape(-1, by_share.shape[-1])
+    return lax.all_gather(rows, "dp", axis=0, tiled=True)
+
+
+def gradient_rows(partial, ctx_count):
+    mine = lax.psum_scatter(partial.astype(jnp.bfloat16), "dp", scatter_dimension=0, tiled=True)
+    blocks = mine.reshape(ctx_count, -1, mine.shape[-1])
+    return lax.all_to_all(blocks, "ctx", split_axis=0, concat_axis=0, tiled=True).astype(jnp.float32)
+
+
+def normed(rows, gain):
+    inv_root = lax.rsqrt(jnp.mean(rows * rows, axis=-1, keepdims=True) + NORM_EPS)
+    return inv_root, (rows * inv_root * gain.astype(jnp.float32)).astype(jnp.bfloat16)
+
+
+def split_layer(
+    tokens,
+    cotangent,
+    gain_attn,
+    w_query,
+    key_weight,
+    value_weight,
+    w_out,
+    gain_ffn,
+    w_gate,
+    w_up,
+    w_down,
+):
+    ctx_count = lax.axis_size("ctx")
+    dp_count = lax.axis_size("dp")
+    ctx_rank = lax.axis_index("ctx")
+    block_rows, width = tokens.shape
+    weight_rows = w_query.shape[0]
+    head_group = QUERY_HEADS // KEY_VALUE_HEADS
+    score_scale = HEAD_SIZE ** (-0.5)
+    query_share = head_group * HEAD_SIZE
+    first_row = ctx_rank * block_rows
+    seq_rows = block_rows * ctx_count
+    ff_width = w_gate.shape[1]
+    down_rows = w_down.shape[0]
+    ff_share = dp_count * down_rows
+
+    def own(rows):
+        return lax.dynamic_slice_in_dim(rows, first_row, block_rows, 0)
+
+    gain_one = lax.all_gather(gain_attn, ("dp", "ctx"), axis=0, tiled=True)
+    gain_two = lax.all_gather(gain_ffn, ("dp", "ctx"), axis=0, tiled=True)
+    x_all = lax.all_gather(tokens, "ctx", axis=0, tiled=True)
+    ct_all = lax.all_gather(cotangent, "ctx", axis=0, tiled=True)
+
+    def qkv_chunks(_):
+        q = w_query.reshape(weight_rows, ctx_count, -1)
+        k = key_weight.reshape(weight_rows, ctx_count, -1)
+        v = value_weight.reshape(weight_rows, ctx_count, -1)
+        return jnp.transpose(jnp.concatenate([q, k, v], axis=2), (1, 0, 2))
+
+    def ff_chunks(weight):
+        cut = weight.reshape(weight_rows, dp_count, ctx_count, down_rows)
+        return jnp.transpose(cut, (2, 0, 1, 3)).reshape(ctx_count, weight_rows, ff_share)
+
+    w_qkv = weight_columns(None, qkv_chunks, width)
+    out_full = lax.all_gather(w_out, ("dp", "ctx"), axis=0, tiled=True)
+    w_g = weight_columns(w_gate, ff_chunks, width)
+    w_u = weight_columns(w_up, ff_chunks, width)
+    w_d = lax.all_gather(w_down, "dp", axis=0, tiled=True)
+
+    inputs = x_all.astype(jnp.float32)
+    inv_one, h1 = normed(inputs, gain_one)
+    qkv = jnp.dot(h1, w_qkv, preferred_element_type=jnp.float32)
+    cosine_table, sine_values = rope_tables(0, seq_rows)
+    q = apply_rotary(
+        qkv[:, :query_share].reshape(seq_rows, head_group, HEAD_SIZE), cosine_table, sine_values, 1.0
+    ).astype(jnp.bfloat16)
+    k = apply_rotary(
+        qkv[:, query_share : query_share + HEAD_SIZE].reshape(seq_rows, 1, HEAD_SIZE),
+        cosine_table,
+        sine_values,
+        1.0,
+    ).astype(jnp.bfloat16)[:, 0]
+    v = qkv[:, query_share + HEAD_SIZE :].astype(jnp.bfloat16)
+    scores = jnp.einsum("tgd,sd->gts", q, k, preferred_element_type=jnp.float32) * score_scale
+    positions = jnp.arange(seq_rows, dtype=jnp.int32)
+    allowed = positions[None, :] <= positions[:, None]
+    scores = jnp.where(allowed, scores, MASK_FILL)
+    top = jnp.max(scores, axis=-1)
+    expo = jnp.exp(scores - top[..., None])
+    total = jnp.sum(expo, axis=-1)
+    attn = jnp.einsum("gts,sd->tgd", expo.astype(jnp.bfloat16), v, preferred_element_type=jnp.float32)
+    attn = attn / jnp.transpose(total)[..., None]
+    log_total = top + jnp.log(total)
+    ob = attn.reshape(seq_rows, query_share).astype(jnp.bfloat16)
+    ob_all = lax.all_gather(ob, "ctx", axis=1, tiled=True)
+
+    middle = inputs + jnp.dot(ob_all, out_full, preferred_element_type=jnp.float32)
+    inv_two, h2 = normed(middle, gain_two)
+    gate = jnp.dot(h2, w_g, preferred_element_type=jnp.float32)
+    up = jnp.dot(h2, w_u, preferred_element_type=jnp.float32)
+    sig = jax.nn.sigmoid(gate)
+    silu = gate * sig
+    hidden = (silu * up).astype(jnp.bfloat16)
+    out_part = jnp.dot(hidden, w_d, preferred_element_type=jnp.float32).astype(jnp.bfloat16)
+    out_sum = lax.psum_scatter(out_part, "ctx", scatter_dimension=0, tiled=True)
+    middle_own = own(middle)
+    output = (middle_own + out_sum.astype(jnp.float32)).astype(jnp.bfloat16)
+
+    d_hidden = jnp.einsum("td,fd->tf", ct_all, w_d, preferred_element_type=jnp.float32)
+    d_gate = (d_hidden * up * sig * (1.0 + gate * (1.0 - sig))).astype(jnp.bfloat16)
+    d_up = (d_hidden * silu).astype(jnp.bfloat16)
+    dh2_part = jnp.einsum("tf,cf->tc", d_gate, w_g, preferred_element_type=jnp.float32) + jnp.einsum(
+        "tf,cf->tc", d_up, w_u, preferred_element_type=jnp.float32
+    )
+    dh2 = lax.psum_scatter(
+        dh2_part.astype(jnp.bfloat16), "ctx", scatter_dimension=0, tiled=True
+    ).astype(jnp.float32)
+    grad_gain_two, back = norm_back(dh2, middle_own, own(inv_two), gain_two)
+    d_middle = cotangent.astype(jnp.float32) + back
+
+    grad_down = lax.psum_scatter(
+        row_product(hidden, ct_all).astype(jnp.bfloat16), "dp", scatter_dimension=0, tiled=True
+    ).astype(jnp.float32)
+    gate_rows = gradient_rows(row_product(h2, d_gate), ctx_count)
+    up_rows = gradient_rows(row_product(h2, d_up), ctx_count)
+
+    da = d_middle.astype(jnp.bfloat16)
+    do_rows = jnp.einsum("td,cd->tc", da, out_full, preferred_element_type=jnp.float32).astype(
+        jnp.bfloat16
+    )
+
+    def to_columns(rows):
+        blocks = jnp.transpose(rows.reshape(block_rows, ctx_count, -1), (1, 0, 2))
+        return lax.all_to_all(blocks, "ctx", split_axis=0, concat_axis=0, tiled=True).reshape(
+            seq_rows, -1
+        )
+
+    do = to_columns(do_rows).reshape(seq_rows, head_group, HEAD_SIZE)
+    da_columns = to_columns(da)
+    out_rows = gradient_rows(row_product(ob_all, da_columns), ctx_count)
+
+    delta = jnp.transpose(jnp.sum(do.astype(jnp.float32) * attn, axis=-1))
+    probs = jnp.exp(scores - log_total[..., None])
+    d_probs = jnp.einsum("tgd,sd->gts", do, v, preferred_element_type=jnp.float32)
+    d_scores = (probs * (d_probs - delta[..., None])).astype(jnp.bfloat16)
+    dq = jnp.einsum("gts,sd->tgd", d_scores, k, preferred_element_type=jnp.float32) * score_scale
+    dk = jnp.einsum("gts,tgd->sd", d_scores, q, preferred_element_type=jnp.float32) * score_scale
+    dv = jnp.einsum("gts,tgd->sd", probs.astype(jnp.bfloat16), do, preferred_element_type=jnp.float32)
+    dq = apply_rotary(dq, cosine_table, sine_values, -1.0).reshape(seq_rows, query_share)
+    dk = apply_rotary(dk[:, None], cosine_table, sine_values, -1.0)[:, 0]
+    d_qkv = jnp.concatenate([dq, dk, dv], axis=1).astype(jnp.bfloat16)
+    qkv_rows = gradient_rows(row_product(h1, d_qkv), ctx_count)
+    dh1_part = jnp.einsum("tq,cq->tc", d_qkv, w_qkv, preferred_element_type=jnp.float32)
+    dh1 = lax.psum_scatter(
+        dh1_part.astype(jnp.bfloat16), "ctx", scatter_dimension=0, tiled=True
+    ).astype(jnp.float32)
+    grad_gain_one, back = norm_back(dh1, own(inputs), own(inv_one), gain_one)
+    grad_tokens = d_middle + back
+
+    def joined(blocks):
+        return jnp.transpose(blocks, (1, 0, 2)).reshape(blocks.shape[1], -1)
+
+    def ff_joined(blocks):
+        cut = blocks.reshape(ctx_count, weight_rows, dp_count, down_rows)
+        return jnp.transpose(cut, (1, 2, 0, 3)).reshape(weight_rows, ff_width)
+
+    return (
+        output,
+        grad_tokens,
+        lax.psum_scatter(grad_gain_one, ("dp", "ctx"), scatter_dimension=0, tiled=True),
+        joined(qkv_rows[:, :, :query_share]),
+        joined(qkv_rows[:, :, query_share : query_share + HEAD_SIZE]),
+        joined(qkv_rows[:, :, query_share + HEAD_SIZE :]),
+        joined(out_rows),
+        lax.psum_scatter(grad_gain_two, ("dp", "ctx"), scatter_dimension=0, tiled=True),
+        ff_joined(gate_rows),
+        ff_joined(up_rows),
+        grad_down,
+    )
+
+
 def solution(mesh):
+    heads_split = mesh.shape["ctx"] == KEY_VALUE_HEADS
     return jax.shard_map(
-        per_device,
+        split_layer if heads_split else blockwise_layer,
         mesh=mesh,
         in_specs=(
             P(("dp", "ctx"), None),

time: 1900 us -> 759 us (0.40)
  waiting for transfers between devices: 1530 us -> 375 us
  blocking collectives: 88.6 us -> 170 us
  matrix products: 134 us -> 89.9 us
  starting transfers between devices: 60.9 us -> 30.6 us
    reduce_scatter x4 -> x8, waiting for transfers between devices: 925 us -> 159 us  [the longest x1 57.1 us: split_layer(): lax.psum_scatter(dh1_part.astype(jnp.bfloat16), 'ctx', scatter_dimension=...]
    all_gather x8, waiting for transfers between devices: 509 us -> 190 us  [the longest x1 62.7 us: split_layer(): ct_all = lax.all_gather(cotangent, 'ctx', axis=0, tiled=True)]
    ppermute x16 -> x0, waiting for transfers between devices: 91.5 us -> none  [the longest x8 78.3 us: shifted(): return lax.ppermute(block, axis, route)]
    all_to_all x0 -> x5, blocking collectives: none -> 88.6 us  [the longest x3 57.6 us: weight_columns(): lax.all_to_all(chunk_of(weight), 'ctx', split_axis=0, concat_axis=0, tile...]
    ppermute x16 -> x0, starting transfers between devices: 60.5 us -> none  [the longest x8 39.3 us: passed_along(): return lax.ppermute(value, axis, pairs)]
    dot_general x4 -> x5, matrix products: 49.6 us -> 22.7 us  [row_product(): jnp.einsum('tc,tf->cf', left, right, preferred_element_type=jnp.float32)]
    all_to_all x0 -> x4, waiting for transfers between devices: none -> 22.8 us  [the longest x3 19 us: gradient_rows(): lax.all_to_all(blocks, 'ctx', split_axis=0, concat_axis=0, tiled=True)]
    dot_general x21 -> x16, matrix products: 84.3 us -> 67.2 us  [the longest x1 8.5 us: split_layer(): jnp.dot(ob_all, out_full, preferred_element_type=jnp.float32)]
  transfers between devices with their start and end apart: 28 -> 20, of which waited for: 24 -> 14; matrix products, arithmetic and copies ran while one was open for 7% -> 18% of each run, Pallas kernels for 0% -> 0%
where the time goes in v1:
time: 759 us; the launch traced here: 749 us
  waiting for transfers between devices  375 us (49%)
  blocking collectives  170 us (22%)
  matrix products  89.9 us (12%)
  local copies, waits for them, and re-layouts  37.4 us (5%)
  other arithmetic  31.3 us (4%)
  starting transfers between devices  30.6 us (4%)
  between operations  15.2 us (2%)
    unnamed x2, blocking collectives  81.6 us
    all_gather x1, waiting for transfers between devices, split_layer(): ct_all = lax.all_gather(cotangent, 'ctx', axis=0, tiled=True)  62.7 us
    all_gather x1, waiting for transfers between devices, split_layer(): ob_all = lax.all_gather(ob, 'ctx', axis=1, tiled=True)  61.9 us
    all_to_all x3, blocking collectives, weight_columns(): lax.all_to_all(chunk_of(weight), 'ctx', split_axis=0, concat_axis=0, tile...  57.6 us
    reduce_scatter x1, waiting for transfers between devices, split_layer(): lax.psum_scatter(dh1_part.astype(jnp.bfloat16), 'ctx', scatter_dimension=...  57.1 us
    reduce_scatter x1, waiting for transfers between devices, split_layer(): lax.psum_scatter(dh2_part.astype(jnp.bfloat16), 'ctx', scatter_dimension=...  49.6 us
    all_gather x3, waiting for transfers between devices, weight_columns(): return lax.all_gather(rows, 'dp', axis=0, tiled=True)  34.4 us
    reduce_scatter x1, waiting for transfers between devices, split_layer(): out_sum = lax.psum_scatter(out_part, 'ctx', scatter_dimension=0, tiled=True)  34.2 us
  transfers between devices with their start and end apart: 20, of which 14 were waited for; matrix products, arithmetic and copies ran while one was open for 18% of the time, Pallas kernels for 0%

profile of v1, /device:TPU:0, one launch (start us, length us, event | category | flops | bytes accessed | tf_op | source)
XLA Modules:
  0.0 749.3 jit_solution(9929601551640094548)
XLA Ops:
  11.4 23.0 %all_to_all.45 = bf16[8,48,384]{2,1,0:T(8,128)(2,1)} all-to-all(bf16[8,48,384]{2,1,0:T(8,128)(2,1)S(1)} %copy.67), channel_id=1, replica_groups=mesh['dp'=4,'ctx'=8] {'ctx'}, dimensions={0} | all-to-all | bytes 589824 | tf_op jit(solution)/shard_map/all_to_all | solution.py:351
  35.7 39.9 %all-reduce.5 = (bf16[1536]{0:T(1024)(128)(2,1)S(1)}, bf16[1536]{0:T(1024)(128)(2,1)}) all-reduce(bf16[1536]{0:T(1024)(128)(2,1)S(1)} %dynamic-update-slice, bf16[1536]{0:T(1024)(128)(2,1)S(1)} %dynamic-update-slice.1), channel_id=1, replica_groups=mesh['dp'=4,'ctx'=8] {'dp','ctx'}, use_global_device_ids=true, to_apply=%add | all-reduce | flops 3072 | bytes 12288
  77.0 1.4 broadcast_multiply_fusion
  78.5 2.7 multiply_reduce_fusion.1
  81.8 12.5 %all-gather.11.cloned.1.call-done = bf16[1536,384]{1,0:T(8,128)(2,1)} async-done(((bf16[384,384]{1,0:T(8,128)(2,1)}), bf16[1536,384]{1,0:T(8,128)(2,1)}) %all-gather.11.cloned.1.call-update) | async-done | bytes 1179664 | tf_op jit(solution)/shard_map/all_gather | solution.py:353
  94.3 2.8 fusion.32
  98.9 1.9 fusion.5
  100.9 2.0 fusion.2
  104.2 3.5 fusion.77
  108.9 18.3 %all_to_all.46 = bf16[8,48,512]{2,1,0:T(8,128)(2,1)} all-to-all(bf16[8,48,512]{2,1,0:T(8,128)(2,1)} %reshape.308), channel_id=1, replica_groups=mesh['dp'=4,'ctx'=8] {'ctx'}, dimensions={0} | all-to-all | bytes 786432 | tf_op jit(solution)/shard_map/all_to_all | solution.py:351
  129.7 16.3 %all_to_all.47 = bf16[8,48,512]{2,1,0:T(8,128)(2,1)} all-to-all(bf16[8,48,512]{2,1,0:T(8,128)(2,1)} %reshape.311), channel_id=1, replica_groups=mesh['dp'=4,'ctx'=8] {'ctx'}, dimensions={0} | all-to-all | bytes 786432 | tf_op jit(solution)/shard_map/all_to_all | solution.py:351
  148.2 15.3 %all-gather.15.cloned.1.call-done = bf16[1536,1536]{1,0:T(8,128)(2,1)} async-done(((bf16[48,1536]{1,0:T(8,128)(2,1)}), bf16[1536,1536]{1,0:T(8,128)(2,1)}) %all-gather.15.cloned.1.call-update) | async-done | bytes 4718608 | tf_op jit(solution)/shard_map/all_gather | solution.py:413
  163.5 61.9 %all-gather.13.cloned.1.call-done = bf16[1024,1536]{0,1:T(8,128)(2,1)} async-done(((bf16[1024,192]{0,1:T(8,128)(2,1)}), bf16[1024,1536]{0,1:T(8,128)(2,1)}) %all-gather.13.cloned.1.call-update) | async-done | bytes 3145744 | tf_op jit(solution)/shard_map/all_gather | solution.py:443
  225.4 8.5 %multiply_reduce_fusion = (f32[1024]{0:T(1024)S(1)}, f32[1024,1536]{1,0:T(8,128)S(1)}) fusion(bf16[1024,1536]{0,1:T(8,128)(2,1)} %all-gather.13.cloned.1.call-done, bf16[1536,1536]{1,0:T(8,128)(2,1)} %all-gather.15.cloned.1.call-done, bf16[1024,1536]{1,0:T(8,128)(2,1)S(1)} %copy-done), kind=kOutput, calls=%fused_computation.11 | convolution fusion | flops 4838128640 | bytes 17305600 | tf_op jit(solution)/shard_map/dot_general | solution.py:445
  233.9 2.7 copy-done.1
  236.6 2.3 multiply_convert_fusion
  238.9 6.2 all-gather.17.cloned.1.call-done
  245.1 5.5 fusion.78
  250.6 15.7 %all-gather.19.cloned.1.call-done = bf16[1536,512]{1,0:T(8,128)(2,1)} async-done(((bf16[384,512]{1,0:T(8,128)(2,1)}), bf16[1536,512]{1,0:T(8,128)(2,1)}) %all-gather.19.cloned.1.call-update) | async-done | bytes 1572880 | tf_op jit(solution)/shard_map/all_gather | solution.py:353
  266.2 5.5 fusion.79
  271.7 15.8 %all-gather.21.cloned.1.call-done = bf16[512,1536]{1,0:T(8,128)(2,1)} async-done(((bf16[128,1536]{1,0:T(8,128)(2,1)}), bf16[512,1536]{1,0:T(8,128)(2,1)}) %all-gather.21.cloned.1.call-update) | async-done | bytes 1572880 | tf_op jit(solution)/shard_map/all_gather | solution.py:416
  287.5 62.7 %all-gather.23.cloned.1.call-done = bf16[1024,1536]{1,0:T(8,128)(2,1)} async-done(((bf16[128,1536]{1,0:T(8,128)(2,1)}), bf16[1024,1536]{1,0:T(8,128)(2,1)}) %all-gather.23.cloned.1.call-update) | async-done | bytes 3145744 | tf_op jit(solution)/shard_map/all_gather | solution.py:400
  350.1 7.3 multiply_convert_fusion.2
  357.5 1.8 fusion.80
  359.7 3.5 add_convert_fusion
  363.2 5.1 convolution_convert_fusion.4
  368.4 11.8 %reduce-scatter.21.cloned.1.call-start = ((), (), s32[]{:S(2)}) async-start(), calls=%async_computation.30 | async-start | bytes 1966080 | tf_op jit(solution)/shard_map/reduce_scatter | solution.py:357
  380.2 5.2 convolution_convert_fusion.3
  386.7 49.6 %reduce-scatter.13.cloned.1.call-done = bf16[128,1536]{1,0:T(8,128)(2,1)} async-done(((bf16[1024,1536]{1,0:T(8,128)(2,1)}), bf16[128,1536]{1,0:T(8,128)(2,1)}) %reduce-scatter.13.cloned.1.call-update) | async-done | bytes 393232 | tf_op jit(solution)/shard_map/reduce_scatter | solution.py:463
  436.3 2.1 fusion.40
  439.0 2.3 fusion.76
  441.3 1.9 copy.79
  443.2 15.7 %all_to_all.48 = bf16[8,128,192]{1,2,0:T(8,128)(2,1)S(1)} all-to-all(bf16[8,128,192]{1,2,0:T(8,128)(2,1)} %bitcast.169), channel_id=1, replica_groups=mesh['dp'=4,'ctx'=8] {'ctx'}, dimensions={0} | all-to-all | bytes 786432 | tf_op jit(solution)/shard_map/all_to_all | solution.py:482
  458.9 3.9 convolution_convert_fusion.6
  462.9 2.2 copy.89
  465.1 4.9 convolution_convert_fusion.7
  470.0 1.9 copy.71
  471.9 4.1 all-to-all-start.3
  477.4 5.3 convolution_convert_fusion.2
  482.7 3.8 all-to-all-done.3
  486.5 2.0 copy.72
  488.5 1.9 reshape_reshape.3
  490.4 1.4 multiply_reduce_fusion.2
  491.8 6.9 fusion.1
  498.8 1.4 fusion.21
  503.9 2.6 fusion.22
  507.2 3.2 convolution_convert_fusion.5
  510.7 5.1 convolution_convert_fusion
  515.9 5.2 convolution_convert_fusion.1
  521.1 4.1 all-to-all-start.7
  525.3 10.6 %all-to-all-done.7 = bf16[8,48,512]{2,1,0:T(8,128)(2,1)} async-done(((bf16[8,48,512]{2,1,0:T(8,128)(2,1)}), bf16[8,48,512]{2,1,0:T(8,128)(2,1)}, u32[]{:S(2)}, u32[]{:S(2)}) %all-to-all-start.7) | async-done | bytes 393248 | tf_op jit(solution)/shard_map/all_to_all | solution.py:359
  535.9 15.3 %all_to_all.49 = bf16[8,48,512]{2,1,0:T(8,128)(2,1)} all-to-all(bf16[8,48,512]{2,1,0:T(8,128)(2,1)} %bitcast.174), channel_id=1, replica_groups=mesh['dp'=4,'ctx'=8] {'ctx'}, dimensions={0} | all-to-all | bytes 786432 | tf_op jit(solution)/shard_map/all_to_all | solution.py:359
  551.1 4.0 all-to-all-start.6
  556.4 3.5 convert_element_type.142
  560.0 2.0 convert_element_type.173
  564.4 18.0 %reduce-scatter.17.cloned.1.call-done = bf16[384,384]{1,0:T(8,128)(2,1)} async-done(((bf16[1536,384]{1,0:T(8,128)(2,1)}), bf16[384,384]{1,0:T(8,128)(2,1)}) %reduce-scatter.17.cloned.1.call-update) | async-done | bytes 294928 | tf_op jit(solution)/shard_map/reduce_scatter | solution.py:357
  582.4 5.5 all-to-all-start.4
  587.9 2.2 copy_bitcast_fusion
  592.2 8.4 %all-to-all-done.4 = bf16[8,48,384]{2,1,0:T(8,128)(2,1)S(1)} async-done(((bf16[8,48,384]{2,1,0:T(8,128)(2,1)}), bf16[8,48,384]{2,1,0:T(8,128)(2,1)S(1)}, u32[]{:S(2)}, u32[]{:S(2)}) %all-to-all-start.4) | async-done | bytes 294944 | tf_op jit(solution)/shard_map/all_to_all | solution.py:359
  603.6 57.1 %reduce-scatter.15.cloned.1.call-done = bf16[128,1536]{1,0:T(8,128)(2,1)} async-done(((bf16[1024,1536]{1,0:T(8,128)(2,1)}), bf16[128,1536]{1,0:T(8,128)(2,1)}) %reduce-scatter.15.cloned.1.call-update) | async-done | bytes 393232 | tf_op jit(solution)/shard_map/reduce_scatter | solution.py:502
  660.7 1.5 fusion.42
  662.2 41.7 %all-reduce.4 = (f32[1536]{0:T(1024)S(1)}, f32[1536]{0:T(1024)S(1)}) all-reduce(f32[1536]{0:T(1024)S(1)} %get-tuple-element.13, f32[1536]{0:T(1024)S(1)} %copy-done.30), channel_id=5, replica_groups=mesh['dp'=4,'ctx'=8] {'dp','ctx'}, use_global_device_ids=true, to_apply=%region_11.12.clone | all-reduce | flops 3072 | bytes 24576
  705.1 34.2 %reduce-scatter.11.cloned.1.call-done = bf16[128,1536]{1,0:T(8,128)(2,1)} async-done(((bf16[1024,1536]{1,0:T(8,128)(2,1)}), bf16[128,1536]{1,0:T(8,128)(2,1)}) %reduce-scatter.11.cloned.1.call-update) | async-done | bytes 393232 | tf_op jit(solution)/shard_map/reduce_scatter | solution.py:453
  739.4 3.0 fusion.35
  (187 shorter events, 34.5 us)
Async XLA Ops:
  7.2 28.1 %copy-start.42 = (bf16[48]{0:T(256)(128)(2,1)S(1)}, bf16[48]{0:T(256)(128)(2,1)}, u32[]{:S(2)}) copy-start(bf16[48]{0:T(256)(128)(2,1)} %param.13) | copy-start | bytes 292
  7.2 28.3 %copy-start.43 = (bf16[48]{0:T(256)(128)(2,1)S(1)}, bf16[48]{0:T(256)(128)(2,1)}, u32[]{:S(2)}) copy-start(bf16[48]{0:T(256)(128)(2,1)} %param.18) | copy-start | bytes 292
  7.2 71.3 %all-gather.9.cloned.1.call-start = ((), (), s32[]{:S(2)}) async-start(), calls=%async_computation.17 | async-start | bytes 3538944 | tf_op jit(solution)/shard_map/all_gather | solution.py:399
  7.9 86.4 %all-gather.11.cloned.1.call-start = ((), (), s32[]{:S(2)}) async-start(), calls=%async_computation.18 | async-start | bytes 1474560 | tf_op jit(solution)/shard_map/all_gather | solution.py:353
  34.4 129.1 %all-gather.15.cloned.1.call-start = ((), (), s32[]{:S(2)}) async-start(), calls=%async_computation.20 | async-start | bytes 4866048 | tf_op jit(solution)/shard_map/all_gather | solution.py:413
  35.2 190.2 %all-gather.13.cloned.1.call-start = ((), (), s32[]{:S(2)}) async-start(), calls=%async_computation.19 | async-start | bytes 3538944 | tf_op jit(solution)/shard_map/all_gather | solution.py:443
  75.6 2.8 copy-start.34
  75.7 21.6 %copy-start.26 = (f32[1024]{0:T(1024)}, f32[1024]{0:T(1024)S(1)}, u32[]{:S(2)}) copy-start(f32[1024]{0:T(1024)S(1)} %iota_convert_fusion) | copy-start | bytes 12292
  78.5 19.6 %copy-start.7 = (f32[1024,48]{0,1:T(8,128)}, f32[1024,48]{0,1:T(8,128)S(1)}, u32[]{:S(2)}) copy-start(f32[1024,48]{0,1:T(8,128)S(1)} %get-tuple-element.36) | copy-start | bytes 589828
  78.5 15.8 %copy-start = (bf16[1024,1536]{1,0:T(8,128)(2,1)S(1)}, bf16[1024,1536]{1,0:T(8,128)(2,1)}, u32[]{:S(2)}) copy-start(bf16[1024,1536]{1,0:T(8,128)(2,1)} %all-gather.9.cloned.1.call-done) | copy-start | bytes 9437188
  81.8 15.5 %copy-start.35 = (f32[48]{0:T(128)S(1)}, f32[48]{0:T(128)}, u32[]{:S(2)}) copy-start(f32[48]{0:T(128)} %copy-done.34) | copy-start | bytes 580
  97.1 5.8 copy-start.13
  97.2 1.8 copy-start.3
  98.1 2.8 copy-start.17
  98.1 2.8 copy-start.19
  98.2 2.7 copy-start.21
  98.3 2.7 copy-start.23
  100.9 3.3 copy-start.2
  100.9 3.3 copy-start.28
  102.9 4.8 copy-start.29
  104.2 3.6 copy-start.15
  107.7 137.4 %all-gather.17.cloned.1.call-start = ((), (), s32[]{:S(2)}) async-start(), calls=%async_computation.21 | async-start | bytes 1966080 | tf_op jit(solution)/shard_map/all_gather | solution.py:353
  127.3 139.0 %all-gather.19.cloned.1.call-start = ((), (), s32[]{:S(2)}) async-start(), calls=%async_computation.22 | async-start | bytes 1966080 | tf_op jit(solution)/shard_map/all_gather | solution.py:353
  146.0 141.5 %all-gather.21.cloned.1.call-start = ((), (), s32[]{:S(2)}) async-start(), calls=%async_computation.23 | async-start | bytes 1966080 | tf_op jit(solution)/shard_map/all_gather | solution.py:416
  146.7 203.4 %all-gather.23.cloned.1.call-start = ((), (), s32[]{:S(2)}) async-start(), calls=%async_computation.25 | async-start | bytes 3538944 | tf_op jit(solution)/shard_map/all_gather | solution.py:400
  147.5 288.8 %reduce-scatter.13.cloned.1.call-start = ((), (), s32[]{:S(2)}) async-start(), calls=%async_computation.26 | async-start | bytes 3538944 | tf_op jit(solution)/shard_map/reduce_scatter | solution.py:463
  233.9 2.7 copy-start.1
  233.9 2.7 copy-start.31
  350.1 7.3 copy-start.41
  357.5 1.9 copy-start.44
  357.5 1.9 copy-start.12
  357.5 2.2 copy-start.11
  363.1 158.0 %reduce-scatter.19.cloned.1.call-start = ((), (), s32[]{:S(2)}) async-start(), calls=%async_computation.29 | async-start | bytes 1966080 | tf_op jit(solution)/shard_map/reduce_scatter | solution.py:357
  368.4 70.6 %copy-start.6 = (bf16[128,1536]{1,0:T(8,128)(2,1)S(1)}, bf16[128,1536]{1,0:T(8,128)(2,1)}, u32[]{:S(2)}) copy-start(bf16[128,1536]{1,0:T(8,128)(2,1)} %param.12) | copy-start | bytes 1179652
  368.4 156.9 %reduce-scatter.21.cloned.1.call-start = ((), (), s32[]{:S(2)}) async-start(), calls=%async_computation.30 | async-start | bytes 1966080 | tf_op jit(solution)/shard_map/reduce_scatter | solution.py:357
  385.4 165.7 %reduce-scatter.25.cloned.1.call-start = ((), (), s32[]{:S(2)}) async-start(), calls=%async_computation.32 | async-start | bytes 983040 | tf_op jit(solution)/shard_map/reduce_scatter | solution.py:357
  471.9 14.6 %all-to-all-start.3 = ((bf16[8,128,192]{1,2,0:T(8,128)(2,1)}), bf16[8,128,192]{1,2,0:T(8,128)(2,1)}, u32[]{:S(2)}, u32[]{:S(2)}) async-start(bf16[8,128,192]{1,2,0:T(8,128)(2,1)} %bitcast.164), calls=%async_computation.5 | async-start | bytes 786432 | tf_op jit(solution)/shard_map/all_to_all | solution.py:482
  476.0 83.9 %reduce-scatter.23.cloned.1.call-start = ((), (), s32[]{:S(2)}) async-start(), calls=%async_computation.31 | async-start | bytes 1966080 | tf_op jit(solution)/shard_map/reduce_scatter | solution.py:469
  482.7 99.7 %reduce-scatter.17.cloned.1.call-start = ((), (), s32[]{:S(2)}) async-start(), calls=%async_computation.28 | async-start | bytes 1474560 | tf_op jit(solution)/shard_map/reduce_scatter | solution.py:357
  491.8 6.9 copy-start.22
  491.8 6.9 copy-start.24
  498.8 1.5 copy-start.27
  498.8 1.5 copy-start.36
  498.8 2.4 copy-start.18
  498.8 2.4 copy-start.20
  498.8 3.5 slice-start
  501.1 5.4 copy-start.25
  501.2 2.4 slice-start.1
  501.2 2.7 copy-start.4
  501.2 2.7 copy-start.9
  501.2 2.7 copy-start.32
  503.9 2.6 copy-start.16
  503.9 3.3 copy-start.37
  510.4 150.3 %reduce-scatter.15.cloned.1.call-start = ((), (), s32[]{:S(2)}) async-start(), calls=%async_computation.27 | async-start | bytes 3538944 | tf_op jit(solution)/shard_map/reduce_scatter | solution.py:502
  515.8 223.6 %reduce-scatter.11.cloned.1.call-start = ((), (), s32[]{:S(2)}) async-start(), calls=%async_computation.24 | async-start | bytes 3538944 | tf_op jit(solution)/shard_map/reduce_scatter | solution.py:453
  521.1 14.8 %all-to-all-start.7 = ((bf16[8,48,512]{2,1,0:T(8,128)(2,1)}), bf16[8,48,512]{2,1,0:T(8,128)(2,1)}, u32[]{:S(2)}, u32[]{:S(2)}) async-start(bf16[8,48,512]{2,1,0:T(8,128)(2,1)} %bitcast.173), calls=%async_computation.12 | async-start | bytes 786432 | tf_op jit(solution)/shard_map/all_to_all | solution.py:359
  551.1 13.3 %all-to-all-start.6 = ((bf16[8,48,192]{2,1,0:T(8,128)(2,1)}), bf16[8,48,192]{2,1,0:T(8,128)(2,1)}, u32[]{:S(2)}, u32[]{:S(2)}) async-start(bf16[8,48,192]{2,1,0:T(8,128)(2,1)} %bitcast.179), calls=%async_computation.10 | async-start | bytes 393216 | tf_op jit(solution)/shard_map/all_to_all | solution.py:359
  560.0 3.7 copy-start.10
  582.4 18.2 %all-to-all-start.4 = ((bf16[8,48,384]{2,1,0:T(8,128)(2,1)}), bf16[8,48,384]{2,1,0:T(8,128)(2,1)S(1)}, u32[]{:S(2)}, u32[]{:S(2)}) async-start(bf16[8,48,384]{2,1,0:T(8,128)(2,1)} %bitcast.178), calls=%async_computation.8 | async-start | bytes 589824 | tf_op jit(solution)/shard_map/all_to_all | solution.py:359
  591.4 69.3 %copy-start.38 = (f32[128]{0:T(128)S(1)}, f32[128]{0:T(128)}, u32[]{:S(2)}) copy-start(f32[128]{0:T(128)} %dynamic-slice.7) | copy-start | bytes 1540
  592.2 70.0 %copy-start.30 = (f32[1536]{0:T(1024)S(1)}, f32[1536]{0:T(1024)}, u32[]{:S(2)}) copy-start(f32[1536]{0:T(1024)} %get-tuple-element.11) | copy-start | bytes 18436
  592.2 147.1 %copy-start.5 = (bf16[128,1536]{1,0:T(8,128)(2,1)S(1)}, bf16[128,1536]{1,0:T(8,128)(2,1)}, u32[]{:S(2)}) copy-start(bf16[128,1536]{1,0:T(8,128)(2,1)} %reduce-scatter.13.cloned.1.call-done) | copy-start | bytes 1179652
  592.2 147.1 %copy-start.33 = (f32[128]{0:T(128)S(1)}, f32[128]{0:T(128)}, u32[]{:S(2)}) copy-start(f32[128]{0:T(128)} %dynamic-slice.6) | copy-start | bytes 1540
  592.2 147.1 %copy-start.40 = (f32[128]{0:T(128)S(1)}, f32[128]{0:T(128)}, u32[]{:S(2)}) copy-start(f32[128]{0:T(128)} %copy-done.39) | copy-start | bytes 1540
  (4 other events, 3.3 us)
Sparse Core Ops, SparseCore 0:
  10.2 66.3 all-gather.8
  78.2 16.0 all-gather.10
  97.2 66.2 all-gather.14
  166.1 59.2 all-gather.12
  226.8 18.2 all-gather.16
  246.5 19.6 all-gather.18
  267.8 19.6 all-gather.20
  289.6 60.4 all-gather.22
  363.3 73.0 reduce-scatter.12
  438.7 27.4 reduce-scatter.18
  468.9 28.1 reduce-scatter.20
  500.1 23.2 reduce-scatter.24
  526.0 28.1 reduce-scatter.22
  556.7 25.6 reduce-scatter.16
  586.3 74.3 reduce-scatter.14
  664.6 74.7 reduce-scatter.10

commit v2 on v0

--- a/solution.py
+++ b/solution.py
@@ -1,6 +1,10 @@
+import functools
+
 import jax
 import jax.numpy as jnp
 from jax import lax
+from jax.experimental import pallas as pl
+from jax.experimental.pallas import tpu as pltpu
 from jax.sharding import PartitionSpec as P
 
 QUERY_HEADS = 16
@@ -59,7 +63,7 @@
     return jnp.einsum("tc,tf->cf", left, right, preferred_element_type=jnp.float32)
 
 
-def per_device(
+def blockwise_layer(
     tokens,
     cotangent,
     gain_attn,
@@ -347,9 +351,683 @@
     )
 
 
+DP = 4
+CTX = 8
+STEPS = CTX - 1
+HEAD_LANES = 128
+HALF_LANES = 64
+SHARE = 4 * HEAD_LANES
+RIGHT, LEFT = 1, -1
+F32 = jnp.float32
+BF16 = jnp.bfloat16
+
+
+def ring_place(rank):
+    return jnp.where(lax.rem(rank, 2) == 0, rank // 2, CTX - 1 - rank // 2)
+
+
+def ring_rank(place):
+    place = lax.rem(place + 2 * CTX, CTX)
+    return jnp.where(place < CTX // 2, 2 * place, 2 * CTX - 1 - 2 * place)
+
+
+class Here:
+    def __init__(self):
+        self.dp = lax.axis_index("dp")
+        self.ctx = lax.axis_index("ctx")
+        self.place = ring_place(self.ctx)
+        self.row = self.dp // 2
+        self.core = lax.rem(self.dp, 2)
+        self.next = {
+            RIGHT: (self.dp, ring_rank(self.place + 1)),
+            LEFT: (self.dp, ring_rank(self.place - 1)),
+        }
+        self.sibling_dp = self.row * 2 + 1 - self.core
+        self.across_dp = (1 - self.row) * 2 + self.core
+        self.sibling = (self.sibling_dp, self.ctx)
+        self.across = (self.across_dp, self.ctx)
+
+    def peer(self, ahead):
+        return lax.rem(self.ctx + ahead, CTX)
+
+    def greet(self, partners):
+        barrier = pltpu.get_barrier_semaphore()
+        for partner in partners:
+            pl.semaphore_signal(
+                barrier, inc=1, device_id=partner, device_id_type=pl.DeviceIdType.MESH
+            )
+        pl.semaphore_wait(barrier, len(partners))
+
+    def peers(self):
+        return [(self.dp, self.peer(ahead)) for ahead in range(1, CTX)]
+
+
+def send(source, target, sems, device):
+    copy = pltpu.make_async_remote_copy(
+        src_ref=source,
+        dst_ref=target,
+        send_sem=sems[0],
+        recv_sem=sems[1],
+        device_id=device,
+        device_id_type=pl.DeviceIdType.MESH,
+    )
+    copy.start()
+    return copy
+
+
+class Sems:
+    def __init__(self, sent, received):
+        self.sent, self.received, self.used = sent, received, 0
+
+    def __call__(self):
+        pair = (self.sent.at[self.used], self.received.at[self.used])
+        self.used += 1
+        return pair
+
+
+def gather_ring(here, streams, sems):
+    flying = [[] for _ in streams]
+    for step in range(STEPS):
+        for index, (own, place_of, way) in enumerate(streams):
+            rank = ring_rank(here.place - way * step)
+            if step > 0:
+                flying[index][-1].wait_recv()
+            source = own if step == 0 else place_of(rank)
+            flying[index].append(send(source, place_of(rank), sems(), here.next[way]))
+        yield
+    for copies in flying:
+        copies[-1].wait_recv()
+    yield
+    for copies in flying:
+        for copy in copies:
+            copy.wait_send()
+
+
+def run_all(*generators):
+    live = list(generators)
+    while live:
+        for one in list(live):
+            try:
+                next(one)
+            except StopIteration:
+                live.remove(one)
+
+
+def spread_over_dp(here, place_of, sems, ready=()):
+    for copy in ready:
+        copy.wait()
+    first = send(place_of(here.dp), place_of(here.dp), sems(), here.across)
+    beside = send(place_of(here.dp), place_of(here.dp), sems(), here.sibling)
+    yield
+    first.wait_recv()
+    last = send(place_of(here.across_dp), place_of(here.across_dp), sems(), here.sibling)
+    yield
+    beside.wait_recv()
+    last.wait_recv()
+    for copy in (first, beside, last):
+        copy.wait_send()
+
+
+def gather_columns(here, chunks, target, local_sem, sems):
+    mine = here.dp * CTX + here.ctx
+    local = pltpu.make_async_copy(chunks.at[here.ctx], target.at[mine], local_sem)
+    local.start()
+    copies = []
+    for ahead in range(1, CTX):
+        peer = here.peer(ahead)
+        copies.append(send(chunks.at[peer], target.at[mine], sems(), (here.dp, peer)))
+    yield
+    yield
+    yield
+    yield from spread_over_dp(
+        here, lambda dp: target.at[pl.ds(dp * CTX, CTX)], sems, copies + [local]
+    )
+
+
+def gather_kernel(
+    tokens, cotangent, qkv, gate_up, down, out, x_all, ct_all, w_qkv, w_gu, w_d, w_o, local, sent, got
+):
+    here = Here()
+    sems = Sems(sent, got)
+    here.greet(here.peers() + [here.sibling, here.across])
+    kept = [
+        pltpu.make_async_copy(tokens, x_all.at[here.ctx], local.at[0]),
+        pltpu.make_async_copy(cotangent, ct_all.at[here.ctx], local.at[1]),
+        pltpu.make_async_copy(down, w_d.at[here.dp], local.at[2]),
+        pltpu.make_async_copy(out, w_o.at[here.dp * CTX + here.ctx], local.at[3]),
+    ]
+    for copy in kept:
+        copy.start()
+
+    def rings(own, target, count, base=0):
+        width = own.shape[1] // count
+        for index in range(count):
+            columns = pl.ds(index * width, width)
+            yield (
+                own.at[:, columns],
+                lambda rank, columns=columns: target.at[base + rank, :, columns],
+                RIGHT if index < count // 2 else LEFT,
+            )
+
+    def out_gather():
+        yield from gather_ring(here, list(rings(out, w_o, 2, here.dp * CTX)), sems)
+        kept[3].wait()
+        yield from spread_over_dp(here, lambda dp: w_o.at[pl.ds(dp * CTX, CTX)], sems)
+
+    run_all(
+        gather_ring(here, list(rings(tokens, x_all, 4)), sems),
+        gather_columns(here, qkv, w_qkv, local.at[4], sems),
+        gather_columns(here, gate_up, w_gu, local.at[5], sems),
+        out_gather(),
+        gather_ring(here, list(rings(cotangent, ct_all, 4)), sems),
+        spread_over_dp(here, lambda dp: w_d.at[dp], sems, [kept[2]]),
+    )
+    for copy in kept[:2]:
+        copy.wait()
+
+
+ANY = pl.BlockSpec(memory_space=pltpu.MemorySpace.HBM)
+VMEM = pl.BlockSpec(memory_space=pltpu.MemorySpace.VMEM)
+VMEM_BYTES = 56 * 2**20
+
+
+def params(collective_id):
+    return pltpu.CompilerParams(
+        collective_id=collective_id, has_side_effects=True, vmem_limit_bytes=VMEM_BYTES
+    )
+
+
+def dma_sems(count):
+    return [pltpu.SemaphoreType.DMA((count,)), pltpu.SemaphoreType.DMA((count,))]
+
+
+def gather_all(tokens, cotangent, qkv, gate_up, down, out):
+    rows, width = tokens.shape
+    shape = lambda *dims: jax.ShapeDtypeStruct(dims, BF16)
+    return pl.pallas_call(
+        gather_kernel,
+        out_shape=(
+            shape(CTX, rows, width),
+            shape(CTX, rows, width),
+            shape(DP * CTX, *qkv.shape[1:]),
+            shape(DP * CTX, *gate_up.shape[1:]),
+            shape(DP, *down.shape),
+            shape(DP * CTX, *out.shape),
+        ),
+        in_specs=[ANY] * 6,
+        out_specs=(ANY,) * 6,
+        scratch_shapes=[pltpu.SemaphoreType.DMA((6,))] + dma_sems(96),
+        compiler_params=params(1),
+        name="gather_inputs",
+    )(tokens, cotangent, qkv, gate_up, down, out)
+
+
+def heads_kernel(mine, every, local, sent, got):
+    here = Here()
+    sems = Sems(sent, got)
+    here.greet([here.next[RIGHT], here.next[LEFT]])
+    kept = pltpu.make_async_copy(mine, every.at[here.ctx], local)
+    kept.start()
+    width = mine.shape[1] // 4
+    streams = []
+    for index in range(4):
+        lanes = pl.ds(index * width, width)
+        streams.append(
+            (
+                mine.at[:, lanes],
+                lambda rank, lanes=lanes: every.at[rank, :, lanes],
+                RIGHT if index < 2 else LEFT,
+            )
+        )
+    run_all(gather_ring(here, streams, sems))
+    kept.wait()
+
+
+def gather_heads(mine):
+    return pl.pallas_call(
+        heads_kernel,
+        out_shape=jax.ShapeDtypeStruct((CTX, *mine.shape), BF16),
+        in_specs=[ANY],
+        out_specs=ANY,
+        scratch_shapes=[pltpu.SemaphoreType.DMA] + dma_sems(4 * STEPS),
+        compiler_params=params(2),
+        name="gather_heads",
+    )(mine)
+
+
+def reduce_ring(here, part, slots, out, sems):
+    width = part.shape[2] // 4
+    flying = [[] for _ in range(4)]
+    for step in range(STEPS):
+        for index in range(4):
+            columns = pl.ds(index * width, width)
+            way = RIGHT if index < 2 else LEFT
+            rank = ring_rank(here.place - way * (1 + step))
+            if step == 0:
+                source = part.at[rank, :, columns]
+            else:
+                flying[index][-1].wait_recv()
+                source = slots.at[step - 1, :, columns]
+                source[...] = (source[...].astype(F32) + part[rank, :, columns].astype(F32)).astype(
+                    BF16
+                )
+            flying[index].append(
+                send(source, slots.at[step, :, columns], sems(), here.next[way])
+            )
+        yield
+    for index in range(4):
+        columns = pl.ds(index * width, width)
+        flying[index][-1].wait_recv()
+        out[:, columns] = slots[STEPS - 1, :, columns].astype(F32) + part[
+            here.ctx, :, columns
+        ].astype(F32)
+    yield
+    for copies in flying:
+        for copy in copies:
+            copy.wait_send()
+
+
+def add_rows(total, more, piece):
+    def body(index, carry):
+        rows = pl.ds(pl.multiple_of(index * piece, piece), piece)
+        total[rows, :] = (total[rows, :].astype(F32) + more[rows, :].astype(F32)).astype(BF16)
+        return carry
+
+    lax.fori_loop(0, total.shape[0] // piece, body, 0)
+
+
+def reduce_over_dp(here, part, beside, across, sems, piece):
+    row, far = here.row, 1 - here.row
+    first = send(part.at[far * 2 + 1 - here.core], beside.at[0], sems(), here.sibling)
+    second = send(part.at[row * 2 + 1 - here.core], beside.at[1], sems(), here.sibling)
+    yield
+    first.wait_recv()
+    add_rows(part.at[here.across_dp], beside.at[0], piece)
+    third = send(part.at[here.across_dp], across, sems(), here.across)
+    second.wait_recv()
+    add_rows(part.at[here.dp], beside.at[1], piece)
+    yield
+    yield
+    yield
+    third.wait_recv()
+    add_rows(part.at[here.dp], across, piece)
+    for copy in (first, second, third):
+        copy.wait_send()
+
+
+def scatter_columns(here, part, beside, across, out, local_sem, sems, rows):
+    yield from reduce_over_dp(here, part, beside, across, sems, rows)
+    source = lambda rank: part.at[here.dp, pl.ds(rank * rows, rows), :]
+    local = pltpu.make_async_copy(source(here.ctx), out.at[here.ctx], local_sem)
+    local.start()
+    copies = []
+    for ahead in range(1, CTX):
+        peer = here.peer(ahead)
+        copies.append(send(source(peer), out.at[here.ctx], sems(), (here.dp, peer)))
+    yield
+    for copy in copies + [local]:
+        copy.wait()
+
+
+def ff_back_kernel(
+    dh2_part, out_part, gu_part, down_part,
+    dh2, out, gu_rows, down_sum,
+    dh2_slots, out_slots, gu_beside, gu_across, down_beside, down_across, local, sent, got,
+):
+    here = Here()
+    sems = Sems(sent, got)
+    here.greet(here.peers() + [here.sibling, here.across])
+
+    def down_reduce():
+        yield from reduce_over_dp(here, down_part, down_beside, down_across, sems, 32)
+        down_sum[...] = down_part[here.dp].astype(F32)
+
+    run_all(
+        reduce_ring(here, dh2_part, dh2_slots, dh2, sems),
+        scatter_columns(
+            here, gu_part, gu_beside, gu_across, gu_rows, local, sems, gu_rows.shape[1]
+        ),
+        down_reduce(),
+        reduce_ring(here, out_part, out_slots, out, sems),
+    )
+
+
+def ff_back(dh2_part, out_part, gu_part, down_part):
+    rows, width = dh2_part.shape[1:]
+    gu_block, down_block = gu_part.shape[1:], down_part.shape[1:]
+    own = jax.ShapeDtypeStruct((rows, width), F32)
+    return pl.pallas_call(
+        ff_back_kernel,
+        out_shape=(
+            own,
+            own,
+            jax.ShapeDtypeStruct((CTX, gu_block[0] // CTX, gu_block[1]), BF16),
+            jax.ShapeDtypeStruct(down_block, F32),
+        ),
+        in_specs=[VMEM] * 4,
+        out_specs=(VMEM,) * 4,
+        scratch_shapes=[
+            pltpu.VMEM((STEPS, rows, width), BF16),
+            pltpu.VMEM((STEPS, rows, width), BF16),
+            pltpu.VMEM((2, *gu_block), BF16),
+            pltpu.VMEM(gu_block, BF16),
+            pltpu.VMEM((2, *down_block), BF16),
+            pltpu.VMEM(down_block, BF16),
+            pltpu.SemaphoreType.DMA,
+        ]
+        + dma_sems(80),
+        compiler_params=params(3),
+        name="ff_back",
+    )(dh2_part, out_part, gu_part, down_part)
+
+
+def columns_kernel(blocks, every, local, sent, got):
+    here = Here()
+    sems = Sems(sent, got)
+    here.greet(here.peers())
+    rows = blocks.shape[3]
+    place = lambda rank: every.at[:, :, pl.ds(pl.multiple_of(rank * rows, rows), rows)]
+    kept = pltpu.make_async_copy(blocks.at[here.ctx], place(here.ctx), local)
+    kept.start()
+    copies = []
+    for ahead in range(1, CTX):
+        peer = here.peer(ahead)
+        copies.append(send(blocks.at[peer], place(here.ctx), sems(), (here.dp, peer)))
+    for copy in copies:
+        copy.wait()
+    kept.wait()
+
+
+def to_columns(blocks):
+    _, pair, share, rows = blocks.shape
+    return pl.pallas_call(
+        columns_kernel,
+        out_shape=jax.ShapeDtypeStruct((pair, share, CTX * rows), BF16),
+        in_specs=[ANY],
+        out_specs=ANY,
+        scratch_shapes=[pltpu.SemaphoreType.DMA] + dma_sems(STEPS),
+        compiler_params=params(4),
+        name="to_columns",
+    )(blocks)
+
+
+def attn_back_kernel(
+    dh1_part, qkv_part, out_part,
+    dh1, qkv_rows, out_rows,
+    slots, qkv_beside, qkv_across, out_beside, out_across, local, sent, got,
+):
+    here = Here()
+    sems = Sems(sent, got)
+    here.greet(here.peers() + [here.sibling, here.across])
+    rows = qkv_rows.shape[1]
+    run_all(
+        reduce_ring(here, dh1_part, slots, dh1, sems),
+        scatter_columns(
+            here, out_part, out_beside, out_across, out_rows, local.at[0], sems, rows
+        ),
+        scatter_columns(
+            here, qkv_part, qkv_beside, qkv_across, qkv_rows, local.at[1], sems, rows
+        ),
+    )
+
+
+def attn_back(dh1_part, qkv_part, out_part):
+    rows, width = dh1_part.shape[1:]
+    qkv_block, out_block = qkv_part.shape[1:], out_part.shape[1:]
+    by_owner = lambda block: jax.ShapeDtypeStruct((CTX, block[0] // CTX, block[1]), BF16)
+    return pl.pallas_call(
+        attn_back_kernel,
+        out_shape=(
+            jax.ShapeDtypeStruct((rows, width), F32),
+            by_owner(qkv_block),
+            by_owner(out_block),
+        ),
+        in_specs=[VMEM] * 3,
+        out_specs=(VMEM,) * 3,
+        scratch_shapes=[
+            pltpu.VMEM((STEPS, rows, width), BF16),
+            pltpu.VMEM((2, *qkv_block), BF16),
+            pltpu.VMEM(qkv_block, BF16),
+            pltpu.VMEM((2, *out_block), BF16),
+            pltpu.VMEM(out_block, BF16),
+            pltpu.SemaphoreType.DMA((2,)),
+        ]
+        + dma_sems(60),
+        compiler_params=params(5),
+        name="attn_back",
+    )(dh1_part, qkv_part, out_part)
+
+
+def gains_kernel(parts, total, every, sent, got):
+    here = Here()
+    sems = Sems(sent, got)
+    mine = here.dp * CTX + here.ctx
+    others = []
+    for ahead in range(1, DP * CTX):
+        rank = lax.rem(mine + ahead, DP * CTX)
+        others.append((rank // CTX, lax.rem(rank, CTX)))
+    here.greet(others)
+    every[mine] = parts[mine]
+    copies = []
+    for other in others:
+        copies.append(send(parts.at[other[0] * CTX + other[1]], every.at[mine], sems(), other))
+    for copy in copies:
+        copy.wait()
+    total[...] = jnp.sum(every[...], axis=0)
+
+
+def sum_gains(parts):
+    return pl.pallas_call(
+        gains_kernel,
+        out_shape=jax.ShapeDtypeStruct(parts.shape[1:], F32),
+        in_specs=[VMEM],
+        out_specs=VMEM,
+        scratch_shapes=[pltpu.VMEM(parts.shape, F32)] + dma_sems(DP * CTX - 1),
+        compiler_params=params(6),
+        name="sum_gains",
+    )(parts)
+
+
+def normed(rows, gain):
+    inv_root = lax.rsqrt(jnp.mean(rows * rows, axis=-1, keepdims=True) + NORM_EPS)
+    return inv_root, (rows * inv_root * gain.astype(F32)).astype(BF16)
+
+
+def spaced_head(weight):
+    half = HEAD_SIZE // 2
+    cut = weight.reshape(*weight.shape[:-1], 2, half)
+    cut = jnp.pad(cut, [(0, 0)] * (cut.ndim - 1) + [(0, HALF_LANES - half)])
+    return cut.reshape(*weight.shape[:-1], HEAD_LANES)
+
+
+def packed_head(spaced):
+    half = HEAD_SIZE // 2
+    cut = spaced.reshape(*spaced.shape[:-1], 2, HALF_LANES)[..., :half]
+    return cut.reshape(*spaced.shape[:-1], HEAD_SIZE)
+
+
+def spaced_tables(row_count):
+    half = HEAD_SIZE // 2
+    cosine, sine = rope_tables(0, row_count)
+    pad = ((0, 0), (0, HALF_LANES - half))
+    cosine = jnp.pad(cosine[:, 0], pad)
+    sine = jnp.pad(sine[:, 0], pad)
+    return jnp.concatenate([cosine, cosine], axis=1), jnp.concatenate([-sine, sine], axis=1)
+
+
+def split_layer(
+    tokens,
+    cotangent,
+    gain_attn,
+    w_query,
+    key_weight,
+    value_weight,
+    w_out,
+    gain_ffn,
+    w_gate,
+    w_up,
+    w_down,
+):
+    ctx_rank = lax.axis_index("ctx")
+    block_rows, width = tokens.shape
+    weight_rows = w_query.shape[0]
+    head_group = QUERY_HEADS // KEY_VALUE_HEADS
+    score_scale = HEAD_SIZE ** (-0.5)
+    query_share = head_group * HEAD_SIZE
+    seq_rows = block_rows * CTX
+    ff_width = w_gate.shape[1]
+    down_rows = w_down.shape[0]
+    ff_share = DP * down_rows
+
+    def own(rows):
+        return lax.dynamic_slice_in_dim(rows, ctx_rank * block_rows, block_rows, 0)
+
+    q_cut = spaced_head(w_query.reshape(weight_rows, CTX, head_group, HEAD_SIZE))
+    k_cut = spaced_head(key_weight.reshape(weight_rows, CTX, HEAD_SIZE))
+    gains = jnp.stack([gain_attn, gain_ffn], axis=1)[:, None, :]
+    v_cut = jnp.concatenate(
+        [
+            value_weight.reshape(weight_rows, CTX, HEAD_SIZE),
+            jnp.broadcast_to(gains, (weight_rows, CTX, 2)),
+            jnp.zeros((weight_rows, CTX, HEAD_LANES - HEAD_SIZE - 2), BF16),
+        ],
+        axis=2,
+    )
+    qkv_chunks = jnp.transpose(
+        jnp.concatenate([q_cut.reshape(weight_rows, CTX, -1), k_cut, v_cut], axis=2), (1, 0, 2)
+    )
+
+    def ff_chunks(weight):
+        cut = weight.reshape(weight_rows, DP, CTX, down_rows)
+        return jnp.transpose(cut, (2, 0, 1, 3)).reshape(CTX, weight_rows, ff_share)
+
+    gu_chunks = jnp.concatenate([ff_chunks(w_gate), ff_chunks(w_up)], axis=2)
+    x_all, ct_all, w_qkv, w_gu, w_d, w_o = gather_all(
+        tokens, cotangent, qkv_chunks, gu_chunks, w_down, w_out
+    )
+    x_all = x_all.reshape(seq_rows, width)
+    ct_all = ct_all.reshape(seq_rows, width)
+    w_qkv = w_qkv.reshape(width, SHARE)
+    w_gu = w_gu.reshape(width, 2 * ff_share)
+    w_d = w_d.reshape(ff_share, width)
+    w_o = w_o.reshape(width, width)
+    gain_lane = 3 * HEAD_LANES + HEAD_SIZE
+    gain_one = w_qkv[:, gain_lane]
+    gain_two = w_qkv[:, gain_lane + 1]
+
+    inputs = x_all.astype(F32)
+    inv_one, h1 = normed(inputs, gain_one)
+    qkv = jnp.dot(h1, w_qkv, preferred_element_type=F32).reshape(seq_rows, 4, HEAD_LANES)
+    cosine, sine = spaced_tables(seq_rows)
+    rotated = qkv[:, :3] * cosine[:, None] + jnp.roll(qkv[:, :3], HALF_LANES, axis=-1) * sine[:, None]
+    rotated = rotated.astype(BF16)
+    q, k = rotated[:, :head_group], rotated[:, head_group]
+    v = qkv[:, 3].astype(BF16)
+    scores = jnp.einsum("tgd,sd->gts", q, k, preferred_element_type=F32) * score_scale
+    positions = jnp.arange(seq_rows, dtype=jnp.int32)
+    allowed = positions[None, :] <= positions[:, None]
+    scores = jnp.where(allowed, scores, MASK_FILL)
+    top = jnp.max(scores, axis=-1)
+    expo = jnp.exp(scores - top[..., None])
+    total = jnp.sum(expo, axis=-1)
+    attn = jnp.einsum("gts,sd->tgd", expo.astype(BF16), v, preferred_element_type=F32)
+    attn = (attn / jnp.transpose(total)[..., None])[..., :HEAD_SIZE]
+    log_total = top + jnp.log(total)
+    ob_t = jnp.transpose(attn.reshape(seq_rows, query_share).astype(BF16))
+    ob_all = gather_heads(ob_t).reshape(width, seq_rows)
+
+    middle = inputs + jnp.einsum("ct,cd->td", ob_all, w_o, preferred_element_type=F32)
+    inv_two, h2 = normed(middle, gain_two)
+    gate_up = jnp.dot(h2, w_gu, preferred_element_type=F32)
+    gate, up = gate_up[:, :ff_share], gate_up[:, ff_share:]
+    sig = jax.nn.sigmoid(gate)
+    silu = gate * sig
+    hidden = (silu * up).astype(BF16)
+    out_part = jnp.dot(hidden, w_d, preferred_element_type=F32).astype(BF16)
+    d_hidden = jnp.einsum("td,fd->tf", ct_all, w_d, preferred_element_type=F32)
+    d_gate = (d_hidden * up * sig * (1.0 + gate * (1.0 - sig))).astype(BF16)
+    d_up = (d_hidden * silu).astype(BF16)
+    d_gu = jnp.concatenate([d_gate, d_up], axis=1)
+    dh2_part = jnp.einsum("tf,cf->tc", d_gu, w_gu, preferred_element_type=F32).astype(BF16)
+    gu_part = row_product(h2, d_gu).astype(BF16)
+    down_part = row_product(hidden, ct_all).astype(BF16)
+    dh2, out_sum, gu_rows, grad_down = ff_back(
+        dh2_part.reshape(CTX, block_rows, width),
+        out_part.reshape(CTX, block_rows, width),
+        gu_part.reshape(DP, CTX * weight_rows, 2 * ff_share),
+        down_part.reshape(DP, down_rows, width),
+    )
+    middle_own = own(middle)
+    output = (middle_own + out_sum).astype(BF16)
+    grad_gain_two, back = norm_back(dh2, middle_own, own(inv_two), gain_two)
+    d_middle = cotangent.astype(F32) + back
+
+    da = d_middle.astype(BF16)
+    do_t = jnp.einsum("cd,td->ct", w_o, da, preferred_element_type=F32).astype(BF16)
+    pair = jnp.stack(
+        [
+            do_t.reshape(CTX, query_share, block_rows),
+            jnp.transpose(da).reshape(CTX, query_share, block_rows),
+        ],
+        axis=1,
+    )
+    do_da = to_columns(pair)
+    do = jnp.transpose(do_da[0]).reshape(seq_rows, head_group, HEAD_SIZE)
+    out_part = jnp.einsum("ct,et->ce", ob_all, do_da[1], preferred_element_type=F32).astype(BF16)
+    out_part = jnp.pad(out_part, ((0, 0), (0, 2 * HEAD_LANES - query_share)))
+
+    delta = jnp.transpose(jnp.sum(do.astype(F32) * attn, axis=-1))
+    do = jnp.pad(do, ((0, 0), (0, 0), (0, HEAD_LANES - HEAD_SIZE)))
+    probs = jnp.exp(scores - log_total[..., None])
+    d_probs = jnp.einsum("tgd,sd->gts", do, v, preferred_element_type=F32)
+    d_scores = (probs * (d_probs - delta[..., None])).astype(BF16)
+    dq = jnp.einsum("gts,sd->tgd", d_scores, k, preferred_element_type=F32) * score_scale
+    dk = jnp.einsum("gts,tgd->sd", d_scores, q, preferred_element_type=F32) * score_scale
+    dv = jnp.einsum("gts,tgd->sd", probs.astype(BF16), do, preferred_element_type=F32)
+    d_qk = jnp.concatenate([dq, dk[:, None]], axis=1)
+    d_qk = d_qk * cosine[:, None] - jnp.roll(d_qk, HALF_LANES, axis=-1) * sine[:, None]
+    d_qkv = jnp.concatenate([d_qk.reshape(seq_rows, -1), dv], axis=1).astype(BF16)
+    qkv_part = row_product(h1, d_qkv).astype(BF16)
+    dh1_part = jnp.einsum("tq,cq->tc", d_qkv, w_qkv, preferred_element_type=F32).astype(BF16)
+    dh1, qkv_rows, out_rows = attn_back(
+        dh1_part.reshape(CTX, block_rows, width),
+        qkv_part.reshape(DP, CTX * weight_rows, SHARE),
+        out_part.reshape(DP, CTX * weight_rows, 2 * HEAD_LANES),
+    )
+    grad_gain_one, back = norm_back(dh1, own(inputs), own(inv_one), gain_one)
+    grad_tokens = d_middle + back
+    gain_parts = jnp.stack([grad_gain_one, grad_gain_two]).reshape(2, DP * CTX, weight_rows)
+    gain_parts = jnp.pad(
+        jnp.transpose(gain_parts, (1, 0, 2)), ((0, 0), (0, 6), (0, HEAD_LANES - weight_rows))
+    )
+    gain_sums = sum_gains(gain_parts)[:2, :weight_rows]
+
+    qkv_rows = jnp.transpose(qkv_rows.astype(F32), (1, 0, 2)).reshape(weight_rows, CTX, 4, HEAD_LANES)
+    out_rows = jnp.transpose(out_rows.astype(F32), (1, 0, 2))[..., :query_share]
+
+    def ff_joined(blocks):
+        cut = blocks.astype(F32).reshape(CTX, weight_rows, DP, down_rows)
+        return jnp.transpose(cut, (1, 2, 0, 3)).reshape(weight_rows, ff_width)
+
+    return (
+        output,
+        grad_tokens,
+        gain_sums[0],
+        packed_head(qkv_rows[:, :, :head_group]).reshape(weight_rows, -1),
+        packed_head(qkv_rows[:, :, head_group]).reshape(weight_rows, -1),
+        qkv_rows[:, :, 3, :HEAD_SIZE].reshape(weight_rows, -1),
+        out_rows.reshape(weight_rows, width),
+        gain_sums[1],
+        ff_joined(gu_rows[:, :, :ff_share]),
+        ff_joined(gu_rows[:, :, ff_share:]),
+        grad_down,
+    )
+
+
 def solution(mesh):
+    heads_split = mesh.shape["dp"] == 4 and mesh.shape["ctx"] == KEY_VALUE_HEADS
     return jax.shard_map(
-        per_device,
+        split_layer if heads_split else blockwise_layer,
         mesh=mesh,
         in_specs=(
             P(("dp", "ctx"), None),

time: 1900 us -> 492 us (0.26)
  waiting for transfers between devices: 1530 us -> 0 us
  Pallas kernels: 0 us -> 348 us
  blocking collectives: 88.6 us -> 0 us
  matrix products: 134 us -> 72 us
  starting transfers between devices: 60.9 us -> 0 us
    reduce_scatter x4 -> x0, waiting for transfers between devices: 925 us -> none  [the longest x1 433 us: per_device(): lax.psum_scatter(row_product(normed_two, gate_up_pair), ('dp', 'ctx'), sc...]
    all_gather x8 -> x0, waiting for transfers between devices: 509 us -> none  [the longest x1 94.2 us: per_device(): lax.all_gather(w_gate, ('dp', 'ctx'), axis=0, tiled=True)]
    pallas_call x0 -> x6, Pallas kernels: none -> 348 us  [the longest x1 138 us: gather_all(): pl.pallas_call(gather_kernel, out_shape=(shape(CTX, rows, width), shape(C...]
    ppermute x16 -> x0, waiting for transfers between devices: 91.5 us -> none  [the longest x8 78.3 us: shifted(): return lax.ppermute(block, axis, route)]
    unnamed x2 -> x0, blocking collectives: 88.6 us -> none
    ppermute x16 -> x0, starting transfers between devices: 60.5 us -> none  [the longest x8 39.3 us: passed_along(): return lax.ppermute(value, axis, pairs)]
    dot_general x4 -> x3, matrix products: 49.6 us -> 12.6 us  [row_product(): jnp.einsum('tc,tf->cf', left, right, preferred_element_type=jnp.float32)]
    dot_general x21 -> x15, matrix products: 84.3 us -> 59.4 us  [the longest x1 10 us: split_layer(): jnp.einsum('ct,cd->td', ob_all, w_o, preferred_element_type=F32)]
  transfers between devices with their start and end apart: 28 -> 0, of which waited for: 24 -> 0; matrix products, arithmetic and copies ran while one was open for 7% -> 0% of each run, Pallas kernels for 0% -> 0%
where the time goes in v2:
time: 492 us; the launch traced here: 486 us
  Pallas kernels  348 us (71%)
  matrix products  72 us (15%)
  local copies, waits for them, and re-layouts  40.2 us (8%)
  other arithmetic  23.9 us (5%)
    pallas_call x1, Pallas kernels, gather_all(): pl.pallas_call(gather_kernel, out_shape=(shape(CTX, rows, width), shape(C...  138 us
    pallas_call x1, Pallas kernels, ff_back(): pl.pallas_call(ff_back_kernel, out_shape=(own, own, jax.ShapeDtypeStruct(...  85.3 us
    pallas_call x1, Pallas kernels, attn_back(): pl.pallas_call(attn_back_kernel, out_shape=(jax.ShapeDtypeStruct((rows, w...  61.3 us
    pallas_call x1, Pallas kernels, gather_heads(): pl.pallas_call(heads_kernel, out_shape=jax.ShapeDtypeStruct((CTX, *mine.s...  38.4 us
    unnamed x100, local copies, waits for them, and re-layouts  12.9 us
    pallas_call x1, Pallas kernels, sum_gains(): pl.pallas_call(gains_kernel, out_shape=jax.ShapeDtypeStruct(parts.shape[1...  12.8 us
    pallas_call x1, Pallas kernels, to_columns(): pl.pallas_call(columns_kernel, out_shape=jax.ShapeDtypeStruct((pair, shar...  12.6 us
    dot_general x3, matrix products, row_product(): jnp.einsum('tc,tf->cf', left, right, preferred_element_type=jnp.float32)  12.6 us

profile of v2, /device:TPU:0, one launch (start us, length us, event | category | flops | bytes accessed | tf_op | source)
XLA Modules:
  0.0 485.9 jit_solution(11680244851106844870)
XLA Ops:
  0.7 1.4 reshape_reshape.15
  3.0 1.1 reshape_reshape.17
  5.0 0.9 concatenate.30
  6.7 1.0 pad_maximum_fusion.5.gate_up
  7.7 137.5 %gather_inputs.1 = (bf16[8,128,1536]{2,1,0:T(8,128)(2,1)}, bf16[8,128,1536]{2,1,0:T(8,128)(2,1)}, bf16[32,48,512]{2,1,0:T(8,128)(2,1)}, bf16[32,48,1024]{2,1,0:T...) custom-call(bf16[128,1536]{1,0:T(8,128)(2,1)} %tokens.1, bf16[128,1536]{1,0:T(8,128)(2,1)} %cotangent.1, ...), custom_call_target="tpu_custom_call" | custom-call | tf_op jit(solution)/shard_map/gather_inputs/pallas_call | solution.py:547
  145.3 1.3 iota_compare_fusion
  146.6 2.2 fusion.62
  148.8 1.2 copy.79
  150.0 2.6 multiply_reduce_fusion.1
  153.2 2.5 multiply_convert_fusion.2
  155.6 2.8 copy.50
  158.4 4.2 fusion.64
  162.7 0.8 multiply_cosine_fusion
  163.7 0.8 copy-done.3
  165.2 1.9 fusion.5
  167.1 2.0 fusion.2
  169.1 1.2 copy-done.1
  170.5 2.6 fusion.22
  173.1 1.0 copy-done.13
  174.1 0.8 fusion.43
  174.9 38.4 %gather_heads.1 = bf16[8,192,1024]{2,1,0:T(8,128)(2,1)} custom-call(bf16[192,1024]{1,0:T(8,128)(2,1)} %bitcast.206), custom_call_target="tpu_custom_call" | custom-call | tf_op jit(solution)/shard_map/gather_heads/pallas_call | solution.py:587
  213.3 10.0 %multiply_reduce_fusion = (f32[1024]{0:T(1024)}, f32[1024,1536]{1,0:T(8,128)}) fusion(bf16[1536,1024]{1,0:T(8,128)(2,1)} %bitcast.185, bf16[1536,1536]{1,0:T(8,128)(2,1)S(1)} %bitcast.181, bf16[1024,1536]{1,0:T(8,128)(2,1)S(1)} %bitcast.173), kind=kOutput, calls=%fused_computation.11 | convolution fusion | flops 4838128640 | bytes 17305600 | tf_op jit(solution)/shard_map/ct,cd->td/dot_general | solution.py:939
  223.4 0.8 copy.80
  224.1 0.7 convert_reduce_fusion
  224.9 0.7 add_rsqrt_fusion
  225.6 7.3 %fusion.60 = f32[1024,1024]{0,1:T(8,128)S(1)} fusion(bf16[1536,1024]{1,0:T(8,128)(2,1)} %bitcast.228, f32[1024,1536]{1,0:T(8,128)} %get-tuple-element.66, f32[1536]{0:T(1024)S(1)} %convert_reduce_fusion, f32[1024]{0:T(1024)S(1)} %add_rsqrt_fusion), kind=kOutput, calls=%fused_computation.126 | convolution fusion | flops 3225944064 | bytes 13641728 | tf_op jit(solution)/shard_map/dot_general | solution.py:941
  232.9 2.5 multiply_convert_fusion.8
  235.5 5.0 %convolution_convert_fusion.3 = bf16[1024,1536]{1,0:T(8,128)(2,1)} fusion(bf16[1536,1024]{1,0:T(8,128)(2,1)S(1)} %bitcast.229, bf16[1024,512]{0,1:T(8,128)(2,1)S(1)} %get-tuple-element.45, bf16[1024,512]{0,1:T(8,128)(2,1)S(1)} %get-tuple-element.44), kind=kOutput, calls=%fused_computation.24 | convolution fusion | flops 3226992640 | bytes 8388608 | tf_op jit(solution)/shard_map/tf,cf->tc/dot_general | solution.py:951
  240.5 3.5 convolution_convert_fusion.1
  244.0 6.3 %convolution_convert_fusion.2 = bf16[1536,1024]{1,0:T(8,128)(2,1)} fusion(bf16[1024,512]{0,1:T(8,128)(2,1)S(1)} %get-tuple-element.45, bf16[1024,512]{0,1:T(8,128)(2,1)S(1)} %get-tuple-element.44, f32[1024,1536]{1,0:T(8,128)S(1)} %bitcast.218, f32[1536]{0:T(1024)S(1)} %convert_reduce_fusion, f32[1024]{0:T(1024)S(1)} %add_rsqrt_fusion), kind=kOutput, calls=%fused_computation.23 | convolution fusion | flops 3231711232 | bytes 11544576 | tf_op jit(solution)/shard_map/tc,tf->cf/dot_general | solution.py:63
  250.3 3.0 convolution_convert_fusion.4
  253.2 85.3 %ff_back.1 = (f32[128,1536]{1,0:T(8,128)}, f32[128,1536]{1,0:T(8,128)}, bf16[8,48,1024]{2,1,0:T(8,128)(2,1)}, f32[128,1536]{1,0:T(8,128)}) custom-call(bf16[8,128,1536]{2,1,0:T(8,128)(2,1)} %bitcast.193, bf16[8,128,1536]{2,1,0:T(8,128)(2,1)} %bitcast.194, bf16[4,384,1024]{2,1,0:T(8,128)(2,1)} %bitcast.195, bf16[4,128,1536]{2,1,0:T(8,128)(2,1)} %bitcast.212), custom_call_target="tpu_custom_call" | custom-call | tf_op jit(solution)/shard_map/ff_back/pallas_call | solution.py:699
  338.5 0.8 dynamic-slice.3
  339.3 2.2 multiply_reduce_fusion.2
  341.5 3.1 convert_bitcast_fusion.1
  345.2 1.2 copy.55
  346.4 3.9 convolution_convert_fusion.6
  350.3 1.0 pad_maximum_fusion.6.blocks
  351.3 12.6 %to_columns.1 = bf16[2,192,1024]{2,1,0:T(8,128)(2,1)} custom-call(bf16[8,2,192,128]{3,2,1,0:T(8,128)(2,1)} %pad_maximum_fusion.6.blocks), custom_call_target="tpu_custom_call" | custom-call | tf_op jit(solution)/shard_map/to_columns/pallas_call | solution.py:743
  363.9 1.0 slice.96
  365.0 6.4 %fusion.31 = bf16[1024,128]{0,1:T(8,128)(2,1)S(1)} fusion(f32[1024,1024,2]{1,0,2:T(8,128)} %copy-done.1, f32[2,1024]{1,0:T(2,128)S(1)} %copy-done.31, pred[1024,1024]{0,1:T(8,128)(4,1)} %iota_compare_fusion, bf16[1024,2,96]{0,2,1:T(8,128)(2,1)S(1)} %bitcast.207), kind=kOutput, calls=%fused_computation.58 | convolution fusion | flops 545390592 | bytes 10100736 | tf_op jit(solution)/shard_map/gts,tgd->sd/dot_general | solution.py:986
  371.6 4.3 fusion.1
  375.9 1.5 fusion.30
  377.4 0.7 fusion.25
  378.4 0.8 copy-done.4
  380.0 3.5 convolution_convert_fusion
  383.4 3.3 fusion.15
  386.8 2.0 convolution_convert_fusion.5
  388.8 2.2 copy.83
  391.0 2.1 pad.32.clone
  393.1 61.3 %attn_back.1 = (f32[128,1536]{1,0:T(8,128)}, bf16[8,48,512]{2,1,0:T(8,128)(2,1)}, bf16[8,48,256]{2,1,0:T(8,128)(2,1)}) custom-call(bf16[8,128,1536]{2,1,0:T(8,128)(2,1)} %bitcast.192, bf16[4,384,512]{2,1,0:T(8,128)(2,1)} %bitcast.211, bf16[4,384,256]{2,1,0:T(8,128)(2,1)} %bitcast.197), custom_call_target="tpu_custom_call" | custom-call | tf_op jit(solution)/shard_map/attn_back/pallas_call | solution.py:778
  454.5 0.9 convert.34
  455.4 0.7 fusion.48
  456.3 1.1 multiply_add_fusion
  458.4 12.8 %sum_gains.1 = f32[8,128]{1,0:T(8,128)} custom-call(f32[32,8,128]{2,1,0:T(8,128)} %pad.33.parts), custom_call_target="tpu_custom_call" | custom-call | tf_op jit(solution)/shard_map/sum_gains/pallas_call | solution.py:820
  471.2 1.3 slice_bitcast_fusion.3
  473.0 0.7 reshape.271
  474.2 1.8 reshape_reshape.18
  476.9 1.2 reshape_reshape.19
  478.4 0.8 reshape_squeeze.7
  479.5 0.9 reshape.286
  481.3 1.3 copy.93
  483.4 1.3 copy.92
  484.7 0.9 copy.97
  (143 shorter events, 11.2 us)
Async XLA Ops:
  0.6 4.0 copy-start.26
  0.7 4.2 copy-start.37
  0.7 4.2 copy-start.38
  0.7 5.3 %copy-start.21 = (bf16[48,4096]{1,0:T(8,128)(2,1)S(1)}, bf16[48,4096]{1,0:T(8,128)(2,1)}, u32[]{:S(2)}) copy-start(bf16[48,4096]{1,0:T(8,128)(2,1)} %param.20) | copy-start | bytes 1179652
  2.3 4.0 copy-start.22
  145.3 7.9 %copy-start = (bf16[8,128,1536]{2,1,0:T(8,128)(2,1)S(1)}, bf16[8,128,1536]{2,1,0:T(8,128)(2,1)}, u32[]{:S(2)}) copy-start(bf16[8,128,1536]{2,1,0:T(8,128)(2,1)} %get-tuple-element.24) | copy-start | bytes 9437188
  153.2 2.5 copy-start.30
  162.6 6.6 %copy-start.7 = (f32[1024,4,128]{0,2,1:T(8,128)}, f32[1024,4,128]{0,2,1:T(8,128)S(1)}, u32[]{:S(2)}) copy-start(f32[1024,4,128]{0,2,1:T(8,128)S(1)} %fusion.64) | copy-start | bytes 6291460
  163.5 1.6 copy-start.8
  163.7 0.8 copy-start.3
  163.7 1.0 copy-start.5
  165.2 1.9 copy-start.17
  167.1 3.3 copy-start.1
  167.1 3.3 copy-start.28
  169.1 44.2 %slice-start.2 = ((s8[4718592]{0:T(1024)(128)(4,1)}), s8[4194304]{0:T(1024)(128)(4,1)S(1)}, s32[]{:S(2)}) async-start(s8[4718592]{0:T(1024)(128)(4,1)} %bitcast.179), calls=%async_computation.2 | async-start | bytes 8388608
  170.5 42.9 %slice-start.3 = ((s8[4718592]{0:T(1024)(128)(4,1)}), s8[524288]{0:T(1024)(128)(4,1)S(1)}, s32[]{:S(2)}) async-start(s8[4718592]{0:T(1024)(128)(4,1)} %bitcast.179), calls=%async_computation.3 | async-start | bytes 1048576
  173.1 1.0 copy-start.13
  224.8 19.1 %copy-start.25 = (f32[1536]{0:T(1024)}, f32[1536]{0:T(1024)S(1)}, u32[]{:S(2)}) copy-start(f32[1536]{0:T(1024)S(1)} %convert_reduce_fusion) | copy-start | bytes 18436
  225.6 18.4 %copy-start.33 = (f32[1024]{0:T(1024)}, f32[1024]{0:T(1024)S(1)}, u32[]{:S(2)}) copy-start(f32[1024]{0:T(1024)S(1)} %add_rsqrt_fusion) | copy-start | bytes 12292
  225.6 7.4 %copy-start.34 = (bf16[8,128,1536]{2,1,0:T(8,128)(2,1)S(1)}, bf16[8,128,1536]{2,1,0:T(8,128)(2,1)}, u32[]{:S(2)}) copy-start(bf16[8,128,1536]{2,1,0:T(8,128)(2,1)} %get-tuple-element.27) | copy-start | bytes 9437188
  225.6 7.4 %copy-start.36 = (bf16[4,128,1536]{2,1,0:T(8,128)(2,1)S(1)}, bf16[4,128,1536]{2,1,0:T(8,128)(2,1)}, u32[]{:S(2)}) copy-start(bf16[4,128,1536]{2,1,0:T(8,128)(2,1)} %get-tuple-element.28) | copy-start | bytes 4718596
  232.9 2.5 copy-start.35
  232.9 11.0 %slice-start.4 = ((s8[6291456]{0:T(1024)(128)(4,1)}), s8[4194304]{0:T(1024)(128)(4,1)S(1)}, s32[]{:S(2)}) async-start(s8[6291456]{0:T(1024)(128)(4,1)} %bitcast.217), calls=%async_computation.4 | async-start | bytes 8388608
  235.5 8.5 %slice-start.5 = ((s8[6291456]{0:T(1024)(128)(4,1)}), s8[2097152]{0:T(1024)(128)(4,1)S(1)}, s32[]{:S(2)}) async-start(s8[6291456]{0:T(1024)(128)(4,1)} %bitcast.217), calls=%async_computation.5 | async-start | bytes 4194304
  253.2 88.3 %copy-start.16 = (bf16[128,1536]{1,0:T(8,128)(2,1)S(1)}, bf16[128,1536]{1,0:T(8,128)(2,1)}, u32[]{:S(2)}) copy-start(bf16[128,1536]{1,0:T(8,128)(2,1)} %cotangent.1) | copy-start | bytes 1179652
  338.5 6.0 %copy-start.29 = (f32[2,1024]{1,0:T(2,128)S(1)}, f32[2,1024]{1,0:T(2,128)}, u32[]{:S(2)}) copy-start(f32[2,1024]{1,0:T(2,128)} %copy-done.28) | copy-start | bytes 24580
  350.3 14.6 %copy-start.31 = (f32[2,1024]{1,0:T(2,128)S(1)}, f32[2,1024]{1,0:T(2,128)}, u32[]{:S(2)}) copy-start(f32[2,1024]{1,0:T(2,128)} %log_add_fusion) | copy-start | bytes 24580
  351.3 20.2 %slice-start = ((s8[8388608]{0:T(1024)(128)(4,1)}), s8[4194304]{0:T(1024)(128)(4,1)S(1)}, s32[]{:S(2)}) async-start(s8[8388608]{0:T(1024)(128)(4,1)} %bitcast.176), calls=%async_computation | async-start | bytes 8388608
  364.9 6.4 %copy-start.14 = (f32[1024,2,128]{0,2,1:T(8,128)S(1)}, f32[1024,2,128]{0,2,1:T(8,128)}, u32[]{:S(2)}) copy-start(f32[1024,2,128]{0,2,1:T(8,128)} %copy-done.13) | copy-start | bytes 3145732
  365.0 6.6 %slice-start.1 = ((s8[8388608]{0:T(1024)(128)(4,1)}), s8[4194304]{0:T(1024)(128)(4,1)S(1)}, s32[]{:S(2)}) async-start(s8[8388608]{0:T(1024)(128)(4,1)} %bitcast.176), calls=%async_computation.1 | async-start | bytes 8388608
  365.0 6.6 %copy-start.9 = (pred[1024,1024]{0,1:T(8,128)(4,1)S(1)}, pred[1024,1024]{0,1:T(8,128)(4,1)}, u32[]{:S(2)}) copy-start(pred[1024,1024]{0,1:T(8,128)(4,1)} %iota_compare_fusion) | copy-start | bytes 3145732
  371.5 4.3 copy-start.18
  378.2 1.0 copy-start.4
  378.2 1.2 copy-start.6
  378.4 1.6 copy-start.10
  380.0 3.5 copy-start.32
  383.4 3.3 copy-start.11
  383.4 3.3 copy-start.15
  454.4 1.6 copy-start.12
  454.4 1.9 copy-start.2
  455.3 2.1 copy-start.27
  455.3 17.1 %copy-start.23 = (bf16[8,48,512]{2,1,0:T(8,128)(2,1)S(1)}, bf16[8,48,512]{2,1,0:T(8,128)(2,1)}, u32[]{:S(2)}) copy-start(bf16[8,48,512]{2,1,0:T(8,128)(2,1)} %get-tuple-element.33) | copy-start | bytes 1179652
  473.7 5.5 %copy-start.24 = (bf16[8,48,256]{2,1,0:T(8,128)(2,1)S(1)}, bf16[8,48,256]{2,1,0:T(8,128)(2,1)}, u32[]{:S(2)}) copy-start(bf16[8,48,256]{2,1,0:T(8,128)(2,1)} %get-tuple-element.34) | copy-start | bytes 589828
  474.2 6.2 %copy-start.20 = (bf16[8,48,1024]{2,1,0:T(8,128)(2,1)S(1)}, bf16[8,48,1024]{2,1,0:T(8,128)(2,1)}, u32[]{:S(2)}) copy-start(bf16[8,48,1024]{2,1,0:T(8,128)(2,1)} %get-tuple-element.35) | copy-start | bytes 2359300
  481.3 3.4 copy-start.19

commit v3 on v0

--- a/solution.py
+++ b/solution.py
@@ -1,6 +1,10 @@
+import functools
+
 import jax
 import jax.numpy as jnp
 from jax import lax
+from jax.experimental import pallas as pl
+from jax.experimental.pallas import tpu as pltpu
 from jax.sharding import PartitionSpec as P
 
 QUERY_HEADS = 16
@@ -59,7 +63,7 @@
     return jnp.einsum("tc,tf->cf", left, right, preferred_element_type=jnp.float32)
 
 
-def per_device(
+def blockwise_layer(
     tokens,
     cotangent,
     gain_attn,
@@ -347,9 +351,985 @@
     )
 
 
+CUBE = 8
+BITS = (0, 1, 2)
+HEAD_LANES = 128
+HALF_LANES = 64
+SHARE = 4 * HEAD_LANES
+F32 = jnp.float32
+BF16 = jnp.bfloat16
+
+
+class Here:
+    def __init__(self):
+        dp = lax.axis_index("dp")
+        ctx = lax.axis_index("ctx")
+        self.core = lax.rem(dp, 2)
+        self.far = ctx // 4
+        self.own = (dp // 2, lax.rem(ctx // 2, 2), lax.rem(ctx, 2))
+        self.shard = self.shard_of(self.own)
+        self.at_home = self.own[0] == self.far
+        self.sibling = self.device(self.own, core=1 - self.core)
+        self.across = self.device(self.own, far=1 - self.far)
+
+    def shard_of(self, bits):
+        return bits[0] * 4 + bits[1] * 2 + bits[2]
+
+    def device(self, bits, core=None, far=None):
+        core = self.core if core is None else core
+        far = self.far if far is None else far
+        return (bits[0] * 2 + core, far * 4 + bits[1] * 2 + bits[2])
+
+    def flip(self, *turned, of=None):
+        bits = self.own if of is None else of
+        return tuple(1 - bit if index in turned else bit for index, bit in enumerate(bits))
+
+    def next(self, bit):
+        return self.device(self.flip(bit))
+
+    def others(self):
+        return [
+            self.flip(*[bit for bit in BITS if code >> (2 - bit) & 1]) for code in range(1, CUBE)
+        ]
+
+    def greet(self, partners):
+        barrier = pltpu.get_barrier_semaphore()
+        for partner in partners:
+            pl.semaphore_signal(
+                barrier, inc=1, device_id=partner, device_id_type=pl.DeviceIdType.MESH
+            )
+        pl.semaphore_wait(barrier, len(partners))
+
+    def peers(self):
+        return [self.device(bits) for bits in self.others()]
+
+
+def make_send(source, target, sems, device):
+    return pltpu.make_async_remote_copy(
+        src_ref=source,
+        dst_ref=target,
+        send_sem=sems[0],
+        recv_sem=sems[1],
+        device_id=device,
+        device_id_type=pl.DeviceIdType.MESH,
+    )
+
+
+def send(*operands):
+    copy = make_send(*operands)
+    copy.start()
+    return copy
+
+
+class Sems:
+    def __init__(self, sent, received):
+        self.sent, self.received, self.used = sent, received, 0
+
+    def __call__(self):
+        pair = (self.sent.at[self.used], self.received.at[self.used])
+        self.used += 1
+        return pair
+
+
+def run_all(*generators):
+    live = list(generators)
+    while live:
+        for one in list(live):
+            try:
+                next(one)
+            except StopIteration:
+                live.remove(one)
+
+
+ORDERS = ((0, 1, 2), (1, 2, 0), (2, 0, 1))
+
+
+def gather_cube(here, place_of, order, sems):
+    a, b, c = order
+    to = lambda bits, bit: send(place_of(bits), place_of(bits), sems(), here.next(bit))
+    from_a, from_b = here.flip(a), here.flip(b)
+    a0, b0, c0 = to(here.own, a), to(here.own, b), to(here.own, c)
+    yield
+    a0.wait_recv()
+    b1, c1 = to(from_a, b), to(from_a, c)
+    yield
+    b0.wait_recv()
+    c2 = to(from_b, c)
+    yield
+    b1.wait_recv()
+    c3 = to(here.flip(a, b), c)
+    yield
+    for copy in (c0, c1, c2, c3):
+        copy.wait_recv()
+    for copy in (a0, b0, b1, c0, c1, c2, c3):
+        copy.wait_send()
+
+
+def gather_cube_thirds(here, place_of, sems):
+    return [
+        gather_cube(here, functools.partial(place_of, third=third), order, sems)
+        for third, order in enumerate(ORDERS)
+    ]
+
+
+def total_of(*refs):
+    total = refs[0][...].astype(F32)
+    for ref in refs[1:]:
+        total = total + ref[...].astype(F32)
+    return total
+
+
+def reduce_cube(here, part_of, slots, out, order, sems):
+    c, b, a = order
+    own = here.own
+    sends = []
+
+    def to(bits, slot, bit):
+        sends.append(send(part_of(bits), slots(slot), sems(), here.next(bit)))
+        return sends[-1]
+
+    c0 = to(here.flip(c, b, a), 0, c)
+    c1 = to(here.flip(c, b), 1, c)
+    c2 = to(here.flip(c, a), 2, c)
+    c3 = to(here.flip(c), 3, c)
+    yield
+    c0.wait_recv()
+    spot = part_of(here.flip(b, a))
+    spot[...] = total_of(spot, slots(0)).astype(BF16)
+    b0 = to(here.flip(b, a), 4, b)
+    yield
+    c1.wait_recv()
+    spot = part_of(here.flip(b))
+    spot[...] = total_of(spot, slots(1)).astype(BF16)
+    b1 = to(here.flip(b), 5, b)
+    yield
+    c2.wait_recv()
+    b0.wait_recv()
+    spot = part_of(here.flip(a))
+    spot[...] = total_of(spot, slots(2), slots(4)).astype(BF16)
+    a0 = to(here.flip(a), 6, a)
+    yield
+    c3.wait_recv()
+    b1.wait_recv()
+    a0.wait_recv()
+    out[...] = total_of(part_of(own), slots(3), slots(5), slots(6))
+    yield
+    for copy in sends:
+        copy.wait_send()
+
+
+def reduce_cube_all(here, part, slots, out, sems):
+    width = out.shape[1] // 6
+    streams = []
+    for index in range(6):
+        columns = pl.ds(index * width, width)
+        streams.append(
+            reduce_cube(
+                here,
+                lambda bits, columns=columns: part.at[bits[0], bits[1], bits[2], :, columns],
+                lambda slot, columns=columns: slots.at[slot, :, columns],
+                out.at[:, columns],
+                ORDERS[index // 2],
+                sems,
+            )
+        )
+    return streams
+
+
+def swap_home(here, source, target, relay, local_sem, sems, beyond=None):
+    beyond = target if beyond is None else beyond
+    half = source.shape[1] // 2
+    left, right = pl.ds(0, half), pl.ds(half, half)
+    by_x = here.next(0)
+    local = pltpu.make_async_copy(source, target, local_sem)
+    out_left = make_send(source.at[:, left], relay.at[0], sems(), here.across)
+    out_right = make_send(source.at[:, right], relay.at[1], sems(), by_x)
+    on_left = make_send(relay.at[0], beyond.at[:, left], sems(), by_x)
+    on_right = make_send(relay.at[1], target.at[:, right], sems(), here.across)
+
+    @pl.when(here.at_home)
+    def _():
+        local.start()
+
+    @pl.when(jnp.logical_not(here.at_home))
+    def _():
+        out_left.start()
+        out_right.start()
+
+    yield
+
+    @pl.when(here.at_home)
+    def _():
+        out_left.wait_recv()
+        on_left.start()
+        out_right.wait_recv()
+        on_right.start()
+        local.wait()
+
+    @pl.when(jnp.logical_not(here.at_home))
+    def _():
+        on_left.wait_recv()
+        on_right.wait_recv()
+
+    yield
+
+    @pl.when(here.at_home)
+    def _():
+        on_left.wait_send()
+        on_right.wait_send()
+
+    @pl.when(jnp.logical_not(here.at_home))
+    def _():
+        out_left.wait_send()
+        out_right.wait_send()
+
+
+def spread(here, place_of, sems, ready=()):
+    for copy in ready:
+        copy.wait()
+    over = send(place_of(here.far), place_of(here.far), sems(), here.across)
+    beside = send(place_of(here.far), place_of(here.far), sems(), here.sibling)
+    yield
+    yield
+    yield
+    over.wait_recv()
+    last = send(place_of(1 - here.far), place_of(1 - here.far), sems(), here.sibling)
+    yield
+    beside.wait_recv()
+    last.wait_recv()
+    for copy in (over, beside, last):
+        copy.wait_send()
+
+
+def gather_columns(here, chunks, target, local_sem, sems):
+    x, z, y = here.own
+    place = target.at[x, here.core, here.far, z, y]
+    local = pltpu.make_async_copy(chunks.at[here.shard], place, local_sem)
+    local.start()
+    copies = [
+        send(chunks.at[here.shard_of(bits)], place, sems(), here.device(bits))
+        for bits in here.others()
+    ]
+    yield
+    yield
+    yield from spread(
+        here, lambda far: target.at[:, here.core, far], sems, copies + [local]
+    )
+
+
+def in_step(live):
+    live = list(live)
+    while live:
+        for one in list(live):
+            try:
+                next(one)
+            except StopIteration:
+                live.remove(one)
+        yield
+
+
+ANY = pl.BlockSpec(memory_space=pltpu.MemorySpace.HBM)
+VMEM = pl.BlockSpec(memory_space=pltpu.MemorySpace.VMEM)
+VMEM_BYTES = 56 * 2**20
+
+
+def params(collective_id):
+    return pltpu.CompilerParams(
+        collective_id=collective_id, has_side_effects=True, vmem_limit_bytes=VMEM_BYTES
+    )
+
+
+def dma_sems(count):
+    return [pltpu.SemaphoreType.DMA((count,)), pltpu.SemaphoreType.DMA((count,))]
+
+
+def half_blocks(block):
+    return pltpu.VMEM((2, block[0], block[1] // 2), BF16)
+
+
+QUERY_TILE = 256
+NT = (((1,), (1,)), ((), ()))
+
+
+def dot(left, right):
+    return jnp.dot(left, right, preferred_element_type=F32)
+
+
+def dot_nt(left, right):
+    return lax.dot_general(left, right, NT, preferred_element_type=F32)
+
+
+def rotate(head, cosine, sine):
+    return head * cosine + pltpu.roll(head, HALF_LANES, 1) * sine
+
+
+def scores_of(keys, queries):
+    count = keys.shape[0] - QUERY_TILE
+    parts = []
+    if count > 0:
+        parts.append(dot_nt(keys[:count], queries) * HEAD_SIZE**-0.5)
+    last = dot_nt(keys[count:], queries) * HEAD_SIZE**-0.5
+    key = lax.broadcasted_iota(jnp.int32, last.shape, 0)
+    query = lax.broadcasted_iota(jnp.int32, last.shape, 1)
+    parts.append(jnp.where(key <= query, last, MASK_FILL))
+    return parts
+
+
+def attend_tile(q, k, v_t, o_t, ob, lse, group, tile):
+    rows = pl.ds(tile * QUERY_TILE, QUERY_TILE)
+    count = (tile + 1) * QUERY_TILE
+    parts = scores_of(k[:count, :], q[group, rows, :])
+    top = jnp.max(parts[-1], axis=0, keepdims=True)
+    for part in parts[:-1]:
+        top = jnp.maximum(top, jnp.max(part, axis=0, keepdims=True))
+    total = jnp.zeros_like(top)
+    result = None
+    first = 0
+    for part in parts:
+        expo = jnp.exp(part - top)
+        total = total + jnp.sum(expo, axis=0, keepdims=True)
+        added = dot(v_t[:, first : first + part.shape[0]], expo.astype(BF16))
+        result = added if result is None else result + added
+        first += part.shape[0]
+    result = result / total
+    o_t[group, :, rows] = result
+    ob[group * HEAD_SIZE : (group + 1) * HEAD_SIZE, rows] = result[:HEAD_SIZE].astype(BF16)
+    lse[group, :, rows] = top + jnp.log(total)
+
+
+def front_kernel(
+    tokens, cotangent, qkv, gate_up, down, out, cosine, sine,
+    x_all, ct_all, w_qkv, w_gu, w_d, w_o, ob_all, h1, q, k, v, o_t, lse, gains,
+    v_t, x_relay, ct_relay, local, sent, got,
+):
+    here = Here()
+    sems = Sems(sent, got)
+    here.greet(here.peers() + [here.sibling, here.across])
+    x, z, y = here.own
+    width = tokens.shape[1]
+    block_rows = tokens.shape[0]
+    seq_rows = CUBE * block_rows
+
+    def swapped(source, target, relay, local_sem):
+        third_width = width // 3
+        yield from swap_home(
+            here,
+            source,
+            target.at[here.shard],
+            relay,
+            local_sem,
+            sems,
+            target.at[here.shard_of(here.flip(0))],
+        )
+        yield from in_step(
+            gather_cube_thirds(
+                here,
+                lambda bits, third: target.at[
+                    here.shard_of(bits), :, pl.ds(third * third_width, third_width)
+                ],
+                sems,
+            )
+        )
+
+    def out_gather():
+        third_width = width // 3
+        mine = w_o.at[x, here.core, here.far, z, y]
+        kept = pltpu.make_async_copy(out, mine, local.at[3])
+        kept.start()
+        over = send(out, mine, sems(), here.across)
+        yield
+        kept.wait()
+        over.wait()
+        yield from in_step(
+            gather_cube_thirds(
+                here,
+                lambda bits, third: w_o.at[
+                    bits[0],
+                    here.core,
+                    :,
+                    bits[1],
+                    bits[2],
+                    :,
+                    pl.ds(third * third_width, third_width),
+                ],
+                sems,
+            )
+        )
+        beside = send(w_o.at[:, here.core], w_o.at[:, here.core], sems(), here.sibling)
+        yield
+        beside.wait()
+
+    def down_gather():
+        kept = pltpu.make_async_copy(down, w_d.at[here.core, here.far], local.at[2])
+        kept.start()
+        yield from spread(here, lambda far: w_d.at[here.core, far], sems, [kept])
+
+    get_x = swapped(tokens, x_all, x_relay, local.at[0])
+    get_qkv = gather_columns(here, qkv, w_qkv, local.at[4], sems)
+    get_gu = gather_columns(here, gate_up, w_gu, local.at[5], sems)
+    get_out = out_gather()
+    get_down = down_gather()
+    get_ct = swapped(cotangent, ct_all, ct_relay, local.at[1])
+    next(get_x)
+    next(get_qkv)
+    next(get_out)
+    next(get_x)
+    next(get_x)
+    next(get_qkv)
+    next(get_down)
+    next(get_gu)
+    next(get_ct)
+    run_all(get_x, get_qkv)
+    later = in_step([get_ct, get_gu, get_out, get_down])
+
+    turned = jnp.transpose(
+        w_qkv[:, :, :, :, :, :, 3 * HEAD_LANES :].astype(F32).reshape(width, HEAD_LANES)
+    )
+    gains[...] = turned[HEAD_SIZE : HEAD_SIZE + 8]
+    next(later)
+
+    def norm_block(index, carry):
+        rows = x_all[index].astype(F32)
+        inv_root = lax.rsqrt(jnp.mean(rows * rows, axis=-1, keepdims=True) + NORM_EPS)
+        place = pl.ds(pl.multiple_of(index * block_rows, block_rows), block_rows)
+        h1[place, :] = (rows * inv_root * gains[0:1, :]).astype(BF16)
+        return carry
+
+    lax.fori_loop(0, CUBE, norm_block, 0)
+    next(later)
+
+    def project(index, carry):
+        rows = pl.ds(pl.multiple_of(index * QUERY_TILE, QUERY_TILE), QUERY_TILE)
+        raw = dot(h1[rows, :], w_qkv[...].reshape(width, SHARE))
+        cos_rows, sin_rows = cosine[rows, :], sine[rows, :]
+        heads = [raw[:, lane : lane + HEAD_LANES] for lane in range(0, SHARE, HEAD_LANES)]
+        q[0, rows, :] = rotate(heads[0], cos_rows, sin_rows).astype(BF16)
+        q[1, rows, :] = rotate(heads[1], cos_rows, sin_rows).astype(BF16)
+        k[rows, :] = rotate(heads[2], cos_rows, sin_rows).astype(BF16)
+        v[rows, :] = heads[3].astype(BF16)
+        v_t[:, rows] = jnp.transpose(heads[3]).astype(BF16)
+        return carry
+
+    lax.fori_loop(0, seq_rows // QUERY_TILE, project, 0)
+    next(later)
+
+    ob = ob_all.at[here.shard]
+    row_third = ob.shape[0] // 3
+    streams = []
+    tiles = seq_rows // QUERY_TILE
+    for tile in range(tiles):
+        for group in range(2):
+            attend_tile(q, k, v_t, o_t, ob, lse, group, tile)
+        if tile % 2 == 1:
+            lanes = pl.ds((tile - 1) * QUERY_TILE, 2 * QUERY_TILE)
+            half = in_step(
+                gather_cube_thirds(
+                    here,
+                    lambda bits, third, lanes=lanes: ob_all.at[
+                        here.shard_of(bits), pl.ds(third * row_third, row_third), lanes
+                    ],
+                    sems,
+                )
+            )
+            next(half)
+            streams.append(half)
+        next(later)
+    run_all(*streams, later)
+
+
+def front(tokens, cotangent, qkv, gate_up, down, out, cosine, sine):
+    slots = (2, 2, 2, 2, 2)
+    shape = lambda *dims: jax.ShapeDtypeStruct(dims, BF16)
+    wide = lambda *dims: jax.ShapeDtypeStruct(dims, F32)
+    rows, width = tokens.shape
+    seq_rows = CUBE * rows
+    share = 2 * HEAD_SIZE
+    outs = (
+        shape(CUBE, rows, width),
+        shape(CUBE, rows, width),
+        shape(*slots, *qkv.shape[1:]),
+        shape(*slots, *gate_up.shape[1:]),
+        shape(2, 2, *down.shape),
+        shape(*slots, *out.shape),
+        shape(CUBE, share, seq_rows),
+        shape(seq_rows, width),
+        shape(2, seq_rows, HEAD_LANES),
+        shape(seq_rows, HEAD_LANES),
+        shape(seq_rows, HEAD_LANES),
+        wide(2, HEAD_LANES, seq_rows),
+        wide(2, 1, seq_rows),
+        wide(8, width),
+    )
+    return pl.pallas_call(
+        front_kernel,
+        out_shape=outs,
+        in_specs=[VMEM] * 8,
+        out_specs=(VMEM,) * len(outs),
+        scratch_shapes=[
+            pltpu.VMEM((HEAD_LANES, seq_rows), BF16),
+            half_blocks(tokens.shape),
+            half_blocks(tokens.shape),
+            pltpu.SemaphoreType.DMA((6,)),
+        ]
+        + dma_sems(140),
+        compiler_params=params(1),
+        name="front",
+    )(tokens, cotangent, qkv, gate_up, down, out, cosine, sine)
+
+
+def attend_back_tile(q, k, k_t, v, do_t, o_t, lse, dk, dv, group, tile):
+    rows = pl.ds(tile * QUERY_TILE, QUERY_TILE)
+    count = (tile + 1) * QUERY_TILE
+    q_rows = q[group, rows, :]
+    do_rows = do_t[group * HEAD_SIZE : (group + 1) * HEAD_SIZE, rows]
+    do_rows = jnp.concatenate(
+        [do_rows, jnp.zeros((HEAD_LANES - HEAD_SIZE, QUERY_TILE), BF16)], axis=0
+    )
+    delta = jnp.sum(do_rows.astype(F32) * o_t[group, :, rows], axis=0, keepdims=True)
+    log_total = lse[group, :, rows]
+    dq_t = None
+    first = 0
+    for part in scores_of(k[:count, :], q_rows):
+        keys = slice(first, first + part.shape[0])
+        probs = jnp.exp(part - log_total)
+        d_probs = dot(v[keys, :], do_rows)
+        d_scores = (probs * (d_probs - delta)).astype(BF16)
+        dv[keys, :] += dot_nt(probs.astype(BF16), do_rows)
+        dk[keys, :] += dot(d_scores, q_rows)
+        added = dot(k_t[:, keys], d_scores)
+        dq_t = added if dq_t is None else dq_t + added
+        first += part.shape[0]
+    return jnp.transpose(dq_t) * HEAD_SIZE**-0.5
+
+
+def attn_grads_kernel(q, k, v, do_t, o_t, lse, cosine, sine, d_qkv, k_t, dk, dv):
+    seq_rows = k.shape[0]
+    k_t[...] = jnp.transpose(k[...].astype(F32)).astype(BF16)
+    dk[...] = jnp.zeros_like(dk)
+    dv[...] = jnp.zeros_like(dv)
+    for tile in range(seq_rows // QUERY_TILE):
+        rows = pl.ds(tile * QUERY_TILE, QUERY_TILE)
+        for group in range(2):
+            dq = attend_back_tile(q, k, k_t, v, do_t, o_t, lse, dk, dv, group, tile)
+            d_qkv[rows, group * HEAD_LANES : (group + 1) * HEAD_LANES] = rotate(
+                dq, cosine[rows, :], -sine[rows, :]
+            ).astype(BF16)
+    d_qkv[:, 2 * HEAD_LANES : 3 * HEAD_LANES] = rotate(
+        dk[...] * HEAD_SIZE**-0.5, cosine[...], -sine[...]
+    ).astype(BF16)
+    d_qkv[:, 3 * HEAD_LANES :] = dv[...].astype(BF16)
+
+
+def attn_grads(q, k, v, do_t, o_t, lse, cosine, sine):
+    seq_rows = k.shape[0]
+    return pl.pallas_call(
+        attn_grads_kernel,
+        out_shape=jax.ShapeDtypeStruct((seq_rows, SHARE), BF16),
+        in_specs=[VMEM] * 8,
+        out_specs=VMEM,
+        scratch_shapes=[
+            pltpu.VMEM((HEAD_LANES, seq_rows), BF16),
+            pltpu.VMEM((seq_rows, HEAD_LANES), F32),
+            pltpu.VMEM((seq_rows, HEAD_LANES), F32),
+        ],
+        compiler_params=pltpu.CompilerParams(vmem_limit_bytes=VMEM_BYTES),
+        name="attn_grads",
+    )(q, k, v, do_t, o_t, lse, cosine, sine)
+
+
+def add_rows(total, more, piece):
+    def body(index, carry):
+        rows = pl.ds(pl.multiple_of(index * piece, piece), piece)
+        for block in range(total.shape[0]):
+            total[block, rows, :] = total_of(
+                total.at[block, rows, :], more.at[block, rows, :]
+            ).astype(BF16)
+        return carry
+
+    lax.fori_loop(0, total.shape[1] // piece, body, 0)
+
+
+def reduce_copies(here, part, beside, over, sems, piece):
+    core, far = here.core, here.far
+    first = send(part.at[:, 1 - core, 1 - far], beside.at[0], sems(), here.sibling)
+    second = send(part.at[:, 1 - core, far], beside.at[1], sems(), here.sibling)
+    yield
+    first.wait_recv()
+    add_rows(part.at[:, core, 1 - far], beside.at[0], piece)
+    third = send(part.at[:, core, 1 - far], over, sems(), here.across)
+    second.wait_recv()
+    add_rows(part.at[:, core, far], beside.at[1], piece)
+    yield
+    yield
+    yield
+    third.wait_recv()
+    add_rows(part.at[:, core, far], over, piece)
+    for copy in (first, second, third):
+        copy.wait_send()
+
+
+def scatter_columns(here, part, beside, over, out, local_sem, sems):
+    rows = out.shape[1]
+    yield from reduce_copies(here, part, beside, over, sems, rows)
+
+    def source(bits):
+        place = pl.ds((bits[1] * 2 + bits[2]) * rows, rows)
+        return part.at[bits[0], here.core, here.far, place, :]
+
+    local = pltpu.make_async_copy(source(here.own), out.at[here.shard], local_sem)
+    local.start()
+    copies = [
+        send(source(bits), out.at[here.shard], sems(), here.device(bits)) for bits in here.others()
+    ]
+    yield
+    for copy in copies + [local]:
+        copy.wait()
+
+
+def ff_back_kernel(
+    dh2_part, out_part, gu_part, down_part,
+    dh2, out, gu_rows, down_sum,
+    dh2_slots, out_slots, gu_beside, gu_over, down_beside, down_over, local, sent, got,
+):
+    here = Here()
+    sems = Sems(sent, got)
+    here.greet(here.peers() + [here.sibling, here.across])
+
+    def down_reduce():
+        yield from reduce_copies(here, down_part, down_beside, down_over, sems, 32)
+        down_sum[...] = down_part[0, here.core, here.far].astype(F32)
+
+    run_all(
+        *reduce_cube_all(here, dh2_part, dh2_slots, dh2, sems),
+        scatter_columns(here, gu_part, gu_beside, gu_over, gu_rows, local, sems),
+        down_reduce(),
+        *reduce_cube_all(here, out_part, out_slots, out, sems),
+    )
+
+
+def copy_slots(part):
+    blocks, _, _, rows, share = part.shape
+    return [pltpu.VMEM((2, blocks, rows, share), BF16), pltpu.VMEM((blocks, rows, share), BF16)]
+
+
+def by_owner(part):
+    rows, share = part.shape[3:]
+    return jax.ShapeDtypeStruct((CUBE, rows // 4, share), BF16)
+
+
+def ff_back(dh2_part, out_part, gu_part, down_part):
+    rows, width = dh2_part.shape[3:]
+    own = jax.ShapeDtypeStruct((rows, width), F32)
+    return pl.pallas_call(
+        ff_back_kernel,
+        out_shape=(
+            own,
+            own,
+            by_owner(gu_part),
+            jax.ShapeDtypeStruct(down_part.shape[3:], F32),
+        ),
+        in_specs=[VMEM] * 4,
+        out_specs=(VMEM,) * 4,
+        scratch_shapes=[
+            pltpu.VMEM((CUBE - 1, rows, width), BF16),
+            pltpu.VMEM((CUBE - 1, rows, width), BF16),
+            *copy_slots(gu_part),
+            *copy_slots(down_part),
+            pltpu.SemaphoreType.DMA,
+        ]
+        + dma_sems(100),
+        compiler_params=params(3),
+        name="ff_back",
+    )(dh2_part, out_part, gu_part, down_part)
+
+
+def columns_kernel(blocks, every, local, sent, got):
+    here = Here()
+    sems = Sems(sent, got)
+    here.greet(here.peers())
+    rows = blocks.shape[3]
+    place = every.at[:, :, pl.ds(pl.multiple_of(here.shard * rows, rows), rows)]
+    kept = pltpu.make_async_copy(blocks.at[here.shard], place, local)
+    kept.start()
+    copies = [
+        send(blocks.at[here.shard_of(bits)], place, sems(), here.device(bits))
+        for bits in here.others()
+    ]
+    for copy in copies:
+        copy.wait()
+    kept.wait()
+
+
+def to_columns(blocks):
+    _, pair, share, rows = blocks.shape
+    return pl.pallas_call(
+        columns_kernel,
+        out_shape=jax.ShapeDtypeStruct((pair, share, CUBE * rows), BF16),
+        in_specs=[VMEM],
+        out_specs=VMEM,
+        scratch_shapes=[pltpu.SemaphoreType.DMA] + dma_sems(CUBE - 1),
+        compiler_params=params(4),
+        name="to_columns",
+    )(blocks)
+
+
+def attn_back_kernel(
+    dh1_part, qkv_part, out_part, output,
+    dh1, qkv_rows, out_rows, output_home,
+    slots, qkv_beside, qkv_over, out_beside, out_over, relay, local, sent, got,
+):
+    here = Here()
+    sems = Sems(sent, got)
+    here.greet(here.peers() + [here.sibling, here.across])
+    run_all(
+        *reduce_cube_all(here, dh1_part, slots, dh1, sems),
+        scatter_columns(here, out_part, out_beside, out_over, out_rows, local.at[0], sems),
+        scatter_columns(here, qkv_part, qkv_beside, qkv_over, qkv_rows, local.at[1], sems),
+        swap_home(here, output, output_home, relay, local.at[2], sems),
+    )
+
+
+def attn_back(dh1_part, qkv_part, out_part, output):
+    rows, width = dh1_part.shape[3:]
+    return pl.pallas_call(
+        attn_back_kernel,
+        out_shape=(
+            jax.ShapeDtypeStruct((rows, width), F32),
+            by_owner(qkv_part),
+            by_owner(out_part),
+            jax.ShapeDtypeStruct((rows, width), BF16),
+        ),
+        in_specs=[VMEM] * 4,
+        out_specs=(VMEM,) * 4,
+        scratch_shapes=[
+            pltpu.VMEM((CUBE - 1, rows, width), BF16),
+            *copy_slots(qkv_part),
+            *copy_slots(out_part),
+            half_blocks((rows, width)),
+            pltpu.SemaphoreType.DMA((3,)),
+        ]
+        + dma_sems(80),
+        compiler_params=params(5),
+        name="attn_back",
+    )(dh1_part, qkv_part, out_part, output)
+
+
+def finish_kernel(parts, grad, total, grad_home, every, relay, local, sent, got):
+    here = Here()
+    sems = Sems(sent, got)
+    own = here.device(here.own)
+    mine = own[0] * CUBE + own[1]
+    count = parts.shape[0]
+    others = []
+    for ahead in range(1, count):
+        rank = lax.rem(mine + ahead, count)
+        others.append((rank // CUBE, lax.rem(rank, CUBE)))
+    here.greet(others)
+    every[mine] = parts[mine]
+    swap = swap_home(here, grad, grad_home, relay, local, sems)
+    next(swap)
+    copies = []
+    for other in others:
+        copies.append(send(parts.at[other[0] * CUBE + other[1]], every.at[mine], sems(), other))
+    for _ in swap:
+        pass
+    for copy in copies:
+        copy.wait()
+    total[...] = jnp.sum(every[...], axis=0)
+
+
+def finish(parts, grad):
+    return pl.pallas_call(
+        finish_kernel,
+        out_shape=(
+            jax.ShapeDtypeStruct(parts.shape[1:], F32),
+            jax.ShapeDtypeStruct(grad.shape, BF16),
+        ),
+        in_specs=[VMEM] * 2,
+        out_specs=(VMEM,) * 2,
+        scratch_shapes=[
+            pltpu.VMEM(parts.shape, F32),
+            half_blocks(grad.shape),
+            pltpu.SemaphoreType.DMA,
+        ]
+        + dma_sems(parts.shape[0] + 3),
+        compiler_params=params(6),
+        name="finish",
+    )(parts, grad)
+
+
+def normed(rows, gain):
+    inv_root = lax.rsqrt(jnp.mean(rows * rows, axis=-1, keepdims=True) + NORM_EPS)
+    return inv_root, (rows * inv_root * gain.astype(F32)).astype(BF16)
+
+
+def spaced_head(weight):
+    half = HEAD_SIZE // 2
+    cut = weight.reshape(*weight.shape[:-1], 2, half)
+    cut = jnp.pad(cut, [(0, 0)] * (cut.ndim - 1) + [(0, HALF_LANES - half)])
+    return cut.reshape(*weight.shape[:-1], HEAD_LANES)
+
+
+def packed_head(spaced):
+    half = HEAD_SIZE // 2
+    cut = spaced.reshape(*spaced.shape[:-1], 2, HALF_LANES)[..., :half]
+    return cut.reshape(*spaced.shape[:-1], HEAD_SIZE)
+
+
+def spaced_tables(row_count):
+    half = HEAD_SIZE // 2
+    cosine, sine = rope_tables(0, row_count)
+    pad = ((0, 0), (0, HALF_LANES - half))
+    cosine = jnp.pad(cosine[:, 0], pad)
+    sine = jnp.pad(sine[:, 0], pad)
+    return jnp.concatenate([cosine, cosine], axis=1), jnp.concatenate([-sine, sine], axis=1)
+
+
+def split_layer(
+    tokens,
+    cotangent,
+    gain_attn,
+    w_query,
+    key_weight,
+    value_weight,
+    w_out,
+    gain_ffn,
+    w_gate,
+    w_up,
+    w_down,
+):
+    here = Here()
+    block_rows, width = tokens.shape
+    weight_rows = w_query.shape[0]
+    head_group = QUERY_HEADS // KEY_VALUE_HEADS
+    score_scale = HEAD_SIZE ** (-0.5)
+    query_share = head_group * HEAD_SIZE
+    seq_rows = block_rows * CUBE
+    ff_width = w_gate.shape[1]
+    down_rows = w_down.shape[0]
+    ff_share = 4 * down_rows
+
+    def own(rows):
+        return lax.dynamic_slice_in_dim(rows, here.shard * block_rows, block_rows, 0)
+
+    q_cut = spaced_head(w_query.reshape(weight_rows, CUBE, head_group, HEAD_SIZE))
+    k_cut = spaced_head(key_weight.reshape(weight_rows, CUBE, HEAD_SIZE))
+    gains = jnp.stack([gain_attn, gain_ffn], axis=1)[:, None, :]
+    v_cut = jnp.concatenate(
+        [
+            value_weight.reshape(weight_rows, CUBE, HEAD_SIZE),
+            jnp.broadcast_to(gains, (weight_rows, CUBE, 2)),
+            jnp.zeros((weight_rows, CUBE, HEAD_LANES - HEAD_SIZE - 2), BF16),
+        ],
+        axis=2,
+    )
+    qkv_chunks = jnp.transpose(
+        jnp.concatenate([q_cut.reshape(weight_rows, CUBE, -1), k_cut, v_cut], axis=2), (1, 0, 2)
+    )
+
+    def ff_chunks(weight):
+        cut = weight.reshape(weight_rows, 2, 4, 4, down_rows)
+        return jnp.transpose(cut, (1, 3, 0, 2, 4)).reshape(CUBE, weight_rows, ff_share)
+
+    gu_chunks = jnp.concatenate([ff_chunks(w_gate), ff_chunks(w_up)], axis=2)
+    cosine, sine = spaced_tables(seq_rows)
+    x_all, ct_all, w_qkv, w_gu, w_d, w_o, ob_all, h1, q, k, v, o_t, lse, gains = front(
+        tokens, cotangent, qkv_chunks, gu_chunks, w_down, w_out, cosine, sine
+    )
+    gain_one, gain_two = gains[0], gains[1]
+    x_all = x_all.reshape(seq_rows, width)
+    ct_all = ct_all.reshape(seq_rows, width)
+    w_qkv = w_qkv.reshape(width, SHARE)
+    w_gu = w_gu.reshape(width, 2 * ff_share)
+    w_d = w_d.reshape(ff_share, width)
+    w_o = w_o.reshape(width, width)
+    ob_all = ob_all.reshape(width, seq_rows)
+    inputs = x_all.astype(F32)
+
+    middle = inputs + jnp.einsum("ct,cd->td", ob_all, w_o, preferred_element_type=F32)
+    inv_two, h2 = normed(middle, gain_two)
+    gate_up = jnp.dot(h2, w_gu, preferred_element_type=F32)
+    gate, up = gate_up[:, :ff_share], gate_up[:, ff_share:]
+    sig = jax.nn.sigmoid(gate)
+    silu = gate * sig
+    hidden = (silu * up).astype(BF16)
+    out_part = jnp.dot(hidden, w_d, preferred_element_type=F32).astype(BF16)
+    d_hidden = jnp.einsum("td,fd->tf", ct_all, w_d, preferred_element_type=F32)
+    d_gate = (d_hidden * up * sig * (1.0 + gate * (1.0 - sig))).astype(BF16)
+    d_up = (d_hidden * silu).astype(BF16)
+    d_gu = jnp.concatenate([d_gate, d_up], axis=1)
+    dh2_part = jnp.einsum("tf,cf->tc", d_gu, w_gu, preferred_element_type=F32).astype(BF16)
+    gu_part = row_product(h2, d_gu).astype(BF16)
+    down_part = row_product(hidden, ct_all).astype(BF16)
+    dh2, out_sum, gu_rows, grad_down = ff_back(
+        dh2_part.reshape(2, 2, 2, block_rows, width),
+        out_part.reshape(2, 2, 2, block_rows, width),
+        gu_part.reshape(2, 2, 2, 4 * weight_rows, 2 * ff_share),
+        down_part.reshape(1, 2, 2, down_rows, width),
+    )
+    middle_own = own(middle)
+    output = (middle_own + out_sum).astype(BF16)
+    grad_gain_two, back = norm_back(dh2, middle_own, own(inv_two), gain_two)
+    d_middle = own(ct_all).astype(F32) + back
+
+    da = d_middle.astype(BF16)
+    do_t = jnp.einsum("cd,td->ct", w_o, da, preferred_element_type=F32).astype(BF16)
+    pair = jnp.stack(
+        [
+            do_t.reshape(CUBE, query_share, block_rows),
+            jnp.transpose(da).reshape(CUBE, query_share, block_rows),
+        ],
+        axis=1,
+    )
+    do_da = to_columns(pair)
+    out_part = jnp.einsum("ct,et->ce", ob_all, do_da[1], preferred_element_type=F32).astype(BF16)
+    out_part = jnp.pad(out_part, ((0, 0), (0, 2 * HEAD_LANES - query_share)))
+
+    d_qkv = attn_grads(q, k, v, do_da[0], o_t, lse, cosine, sine)
+    qkv_part = row_product(h1, d_qkv).astype(BF16)
+    dh1_part = jnp.einsum("tq,cq->tc", d_qkv, w_qkv, preferred_element_type=F32).astype(BF16)
+    dh1, qkv_rows, out_rows, output = attn_back(
+        dh1_part.reshape(2, 2, 2, block_rows, width),
+        qkv_part.reshape(2, 2, 2, 4 * weight_rows, SHARE),
+        out_part.reshape(2, 2, 2, 4 * weight_rows, 2 * HEAD_LANES),
+        output,
+    )
+    own_inputs = own(inputs)
+    inv_one, _ = normed(own_inputs, gain_one)
+    grad_gain_one, back = norm_back(dh1, own_inputs, inv_one, gain_one)
+    grad_tokens = d_middle + back
+    gain_parts = jnp.stack([grad_gain_one, grad_gain_two]).reshape(2, width // weight_rows, weight_rows)
+    gain_parts = jnp.pad(
+        jnp.transpose(gain_parts, (1, 0, 2)), ((0, 0), (0, 6), (0, HEAD_LANES - weight_rows))
+    )
+    gain_sums, grad_tokens = finish(gain_parts, grad_tokens.astype(BF16))
+
+    qkv_rows = jnp.transpose(qkv_rows.astype(F32), (1, 0, 2)).reshape(weight_rows, CUBE, 4, HEAD_LANES)
+    out_rows = jnp.transpose(out_rows.astype(F32), (1, 0, 2))[..., :query_share]
+
+    def ff_joined(blocks):
+        cut = blocks.astype(F32).reshape(2, 4, weight_rows, 4, down_rows)
+        return jnp.transpose(cut, (2, 0, 3, 1, 4)).reshape(weight_rows, ff_width)
+
+    return (
+        output,
+        grad_tokens.astype(F32),
+        gain_sums[0, :weight_rows],
+        packed_head(qkv_rows[:, :, :head_group]).reshape(weight_rows, -1),
+        packed_head(qkv_rows[:, :, head_group]).reshape(weight_rows, -1),
+        qkv_rows[:, :, 3, :HEAD_SIZE].reshape(weight_rows, -1),
+        out_rows.reshape(weight_rows, width),
+        gain_sums[1, :weight_rows],
+        ff_joined(gu_rows[:, :, :ff_share]),
+        ff_joined(gu_rows[:, :, ff_share:]),
+        grad_down,
+    )
+
+
 def solution(mesh):
+    heads_split = mesh.shape["dp"] == 4 and mesh.shape["ctx"] == KEY_VALUE_HEADS
     return jax.shard_map(
-        per_device,
+        split_layer if heads_split else blockwise_layer,
         mesh=mesh,
         in_specs=(
             P(("dp", "ctx"), None),

time: 1900 us -> 462 us (0.24)
  waiting for transfers between devices: 1530 us -> 0 us
  Pallas kernels: 0 us -> 364 us
  matrix products: 134 us -> 43.1 us
  blocking collectives: 88.6 us -> 0 us
  starting transfers between devices: 60.9 us -> 0 us
    reduce_scatter x4 -> x0, waiting for transfers between devices: 925 us -> none  [the longest x1 433 us: per_device(): lax.psum_scatter(row_product(normed_two, gate_up_pair), ('dp', 'ctx'), sc...]
    all_gather x8 -> x0, waiting for transfers between devices: 509 us -> none  [the longest x1 94.2 us: per_device(): lax.all_gather(w_gate, ('dp', 'ctx'), axis=0, tiled=True)]
    pallas_call x0 -> x6, Pallas kernels: none -> 364 us  [the longest x1 170 us: front(): pl.pallas_call(front_kernel, out_shape=outs, in_specs=[VMEM] * 8, out_spe...]
    ppermute x16 -> x0, waiting for transfers between devices: 91.5 us -> none  [the longest x8 78.3 us: shifted(): return lax.ppermute(block, axis, route)]
    unnamed x2 -> x0, blocking collectives: 88.6 us -> none
    ppermute x16 -> x0, starting transfers between devices: 60.5 us -> none  [the longest x8 39.3 us: passed_along(): return lax.ppermute(value, axis, pairs)]
    dot_general x21 -> x8, matrix products: 84.3 us -> 29.5 us  [the longest x1 5.63 us: split_layer(): jnp.einsum('ct,cd->td', ob_all, w_o, preferred_element_type=F32)]
    dot_general x4 -> x3, matrix products: 49.6 us -> 13.5 us  [row_product(): jnp.einsum('tc,tf->cf', left, right, preferred_element_type=jnp.float32)]
  transfers between devices with their start and end apart: 28 -> 0, of which waited for: 24 -> 0; matrix products, arithmetic and copies ran while one was open for 7% -> 0% of each run, Pallas kernels for 0% -> 0%
where the time goes in v3:
time: 462 us; the launch traced here: 456 us
  Pallas kernels  364 us (79%)
  matrix products  43.1 us (9%)
  local copies, waits for them, and re-layouts  28.2 us (6%)
  other arithmetic  19.5 us (4%)
    pallas_call x1, Pallas kernels, front(): pl.pallas_call(front_kernel, out_shape=outs, in_specs=[VMEM] * 8, out_spe...  170 us
    pallas_call x1, Pallas kernels, ff_back(): pl.pallas_call(ff_back_kernel, out_shape=(own, own, by_owner(gu_part), ja...  85.5 us
    pallas_call x1, Pallas kernels, attn_back(): pl.pallas_call(attn_back_kernel, out_shape=(jax.ShapeDtypeStruct((rows, w...  64.1 us
    pallas_call x1, Pallas kernels, finish(): pl.pallas_call(finish_kernel, out_shape=(jax.ShapeDtypeStruct(parts.shape...  21.9 us
    pallas_call x1, Pallas kernels, to_columns(): pl.pallas_call(columns_kernel, out_shape=jax.ShapeDtypeStruct((pair, shar...  14.7 us
    dot_general x3, matrix products, row_product(): jnp.einsum('tc,tf->cf', left, right, preferred_element_type=jnp.float32)  13.5 us

profile of v3, /device:TPU:0, one launch (start us, length us, event | category | flops | bytes accessed | tf_op | source)
XLA Modules:
  0.0 456.0 jit_solution(7239450774919985811)
XLA Ops:
  0.7 0.7 pad_maximum_fusion.7
  1.6 1.0 reshape.173
  2.6 1.1 reshape_reshape.17
  4.2 1.4 reshape_reshape.15
  5.6 0.3 copy.34
  5.9 0.4 pad.23
  6.3 0.3 reshape_reshape.16
  6.6 0.9 concatenate.16
  7.5 0.3 reshape.174
  8.1 0.3 reshape.176
  8.7 1.0 pad_maximum_fusion.3.gate_up
  9.7 1.9 multiply_sine_fusion
  11.7 1.3 pad_maximum_fusion.5
  13.0 170.1 %front.1 = (bf16[8,128,1536]{2,1,0:T(8,128)(2,1)}, bf16[8,128,1536]{2,1,0:T(8,128)(2,1)}, bf16[2,2,2,2,2,48,512]{6,5,4,3,2,1,0:T(8,128)(2,1)}, bf16[2,2,2,2,2,48...) custom-call(bf16[128,1536]{1,0:T(8,128)(2,1)} %tokens.1, ...), custom_call_target="tpu_custom_call" | custom-call | tf_op jit(solution)/shard_map/front/pallas_call | solution.py:863
  183.2 0.9 slice_reduce_fusion.1
  184.1 2.9 bitcast_convert_fusion
  187.3 1.8 copy-done.3
  189.1 5.6 %multiply_reduce_fusion = (f32[1024]{0:T(1024)S(1)}, f32[1024,1536]{1,0:T(8,128)S(1)}) fusion(f32[1024,1536]{1,0:T(8,128)S(1)} %bitcast_convert_fusion, bf16[1536,1024]{1,0:T(8,128)(2,1)S(1)} %bitcast.91, bf16[1536,1536]{1,0:T(8,128)(2,1)S(1)} %bitcast.81), kind=kOutput, calls=%fused_computation.1 | convolution fusion | flops 4836555776 | bytes 20451328 | tf_op jit(solution)/shard_map/ct,cd->td/dot_general | solution.py:1249
  194.9 4.1 fusion.6
  199.1 0.4 copy-done.17
  199.4 2.6 multiply_convert_fusion.3
  202.0 5.0 %convolution_convert_fusion.3 = bf16[1024,1536]{1,0:T(8,128)(2,1)} fusion(bf16[1536,1024]{1,0:T(8,128)(2,1)S(1)} %bitcast.106, bf16[1024,512]{0,1:T(8,128)(2,1)S(1)} %get-tuple-element.69, bf16[1024,512]{0,1:T(8,128)(2,1)S(1)} %get-tuple-element.68), kind=kOutput, calls=%fused_computation.6 | convolution fusion | flops 3226992640 | bytes 8388608 | tf_op jit(solution)/shard_map/tf,cf->tc/dot_general | solution.py:1261
  207.0 6.3 %convolution_convert_fusion.2 = bf16[1536,1024]{1,0:T(8,128)(2,1)} fusion(bf16[1024,512]{0,1:T(8,128)(2,1)S(1)} %get-tuple-element.69, bf16[1024,512]{0,1:T(8,128)(2,1)S(1)} %get-tuple-element.68, f32[1024,1536]{1,0:T(8,128)S(1)} %get-tuple-element.80, f32[1536]{0:T(1024)S(1)} %get-tuple-element.64, f32[1024]{0:T(1024)S(1)} %add_rsqrt_fusion), kind=kOutput, calls=%fused_computation.5 | convolution fusion | flops 3231711232 | bytes 11544576 | tf_op jit(solution)/shard_map/tc,tf->cf/dot_general | solution.py:63
  213.3 3.0 convolution_convert_fusion.5
  216.3 3.6 convolution_convert_fusion.1
  219.8 85.5 %ff_back.1 = (f32[128,1536]{1,0:T(8,128)}, f32[128,1536]{1,0:T(8,128)}, bf16[8,48,1024]{2,1,0:T(8,128)(2,1)}, f32[128,1536]{1,0:T(8,128)}) custom-call(bf16[2,2,2,128,1536]{4,3,2,1,0:T(8,128)(2,1)} %bitcast.87, bf16[2,2,2,128,1536]{4,3,2,1,0:T(8,128)(2,1)} %bitcast.89, bf16[2,2,2,192,1024]{4,3,2,1,0:T(8,128)(2,1)} %bitcast.88, ...), custom_call_target="tpu_custom_call" | custom-call | tf_op jit(solution)/shard_map/ff_back/pallas_call | solution.py:1023
  305.4 2.6 multiply_reduce_fusion.2
  308.0 1.5 convert_bitcast_fusion.1
  309.5 1.4 convolution_convert_fusion.7
  310.9 0.2 copy.40
  311.1 1.0 pad_maximum_fusion.4.blocks
  312.1 14.7 %to_columns.1 = bf16[2,192,1024]{2,1,0:T(8,128)(2,1)} custom-call(bf16[8,2,192,128]{3,2,1,0:T(8,128)(2,1)} %pad_maximum_fusion.4.blocks), custom_call_target="tpu_custom_call" | custom-call | tf_op jit(solution)/shard_map/to_columns/pallas_call | solution.py:1065
  326.8 2.3 convolution_convert_fusion.6
  329.1 0.8 slice_bitcast_fusion.do_t
  329.9 7.2 %attn_grads.1 = bf16[1024,512]{1,0:T(8,128)(2,1)} custom-call(bf16[2,1024,128]{2,1,0:T(8,128)(2,1)} %get-tuple-element.35.q, bf16[1024,128]{1,0:T(8,128)(2,1)} %get-tuple-element.36.k, bf16[1024,128]{1,0:T(8,128)(2,1)} %get-tuple-element.37.v, bf16[192,1024]{1,0:T(8,128)(2,1)} %slice_bitcast_fusion.do_t, f32[2,128,1024]{2,1,0:T(8,128)} %get-tuple-element.46.o_t, ...), custom_call_target="tpu_custom_call" | custom-call | tf_op jit(solution)/shard_map/attn_grads/pallas_call | solution.py:925
  337.1 4.3 convolution_convert_fusion.4
  341.5 0.3 copy.51
  341.8 1.0 pad.27.clone
  342.8 5.0 %convolution_convert_fusion = bf16[1024,1536]{1,0:T(8,128)(2,1)} fusion(bf16[1024,512]{1,0:T(8,128)(2,1)S(1)} %copy-done.6, bf16[1536,512]{1,0:T(8,128)(2,1)} %bitcast.107), kind=kOutput, calls=%fused_computation.3 | convolution fusion | flops 1612185600 | bytes 5767168 | tf_op jit(solution)/shard_map/tq,cq->tc/dot_general | solution.py:1290
  347.8 64.1 %attn_back.1 = (f32[128,1536]{1,0:T(8,128)}, bf16[8,48,512]{2,1,0:T(8,128)(2,1)}, bf16[8,48,256]{2,1,0:T(8,128)(2,1)}, bf16[128,1536]{1,0:T(8,128)(2,1)}) custom-call(bf16[2,2,2,128,1536]{4,3,2,1,0:T(8,128)(2,1)} %bitcast.83, bf16[2,2,2,192,512]{4,3,2,1,0:T(8,128)(2,1)} %bitcast.99, bf16[2,2,2,192,256]{4,3,2,1,0:T(8,128)(2,1)} %bitcast.90, ...), custom_call_target="tpu_custom_call" | custom-call | tf_op jit(solution)/shard_map/attn_back/pallas_call | solution.py:1094
  411.9 1.6 multiply_reduce_fusion.1
  413.5 2.4 add_convert_fusion.grad
  416.1 0.7 pad.28.parts
  416.8 21.9 %finish.1 = (f32[8,128]{1,0:T(8,128)}, bf16[128,1536]{1,0:T(8,128)(2,1)}) custom-call(f32[32,8,128]{2,1,0:T(8,128)} %pad.28.parts, bf16[128,1536]{1,0:T(8,128)(2,1)} %add_convert_fusion.grad), custom_call_target="tpu_custom_call" | custom-call | tf_op jit(solution)/shard_map/finish/pallas_call | solution.py:1142
  438.7 1.3 slice_bitcast_fusion.1
  439.9 2.0 convert_element_type.100
  441.9 0.2 copy.46
  442.2 0.9 reshape.206
  443.1 0.3 reshape.204
  443.7 0.8 reshape_squeeze.7
  444.5 0.6 slice_reduce_fusion
  445.2 0.2 reshape_squeeze.6
  445.6 1.2 reshape_reshape.19
  446.8 0.7 reshape.193
  447.5 0.4 copy.49
  447.9 1.8 reshape_reshape.18
  450.0 0.3 reshape.217
  450.2 0.5 copy.48
  450.8 1.2 reshape.210
  452.0 0.3 reshape.215
  452.2 0.5 copy.47
  452.8 1.2 reshape.208
  454.0 0.7 copy.58
  454.7 0.9 copy.59
  (70 shorter events, 2.9 us)
Async XLA Ops:
  0.6 6.9 %copy-start.9 = (bf16[48,4096]{1,0:T(8,128)(2,1)S(1)}, bf16[48,4096]{1,0:T(8,128)(2,1)}, u32[]{:S(2)}) copy-start(bf16[48,4096]{1,0:T(8,128)(2,1)} %param.19) | copy-start | bytes 1179652
  4.2 3.9 copy-start.10
  184.1 3.1 slice-start
  184.1 3.2 slice-start.1
  184.1 5.0 %copy-start.3 = (bf16[8,192,1024]{2,1,0:T(8,128)(2,1)S(1)}, bf16[8,192,1024]{2,1,0:T(8,128)(2,1)}, u32[]{:S(2)}) copy-start(bf16[8,192,1024]{2,1,0:T(8,128)(2,1)} %get-tuple-element.41) | copy-start | bytes 9437188
  187.0 7.7 %copy-start = (f32[1024,1536]{1,0:T(8,128)}, f32[1024,1536]{1,0:T(8,128)S(1)}, u32[]{:S(2)}) copy-start(f32[1024,1536]{1,0:T(8,128)S(1)} %bitcast_convert_fusion) | copy-start | bytes 18874372
  189.1 5.8 %copy-start.16 = (bf16[2,2,2,2,2,48,1024]{6,5,4,3,2,1,0:T(8,128)(2,1)S(1)}, bf16[2,2,2,2,2,48,1024]{6,5,4,3,2,1,0:T(8,128)(2,1)}, u32[]{:S(2)}) copy-start(bf16[2,2,2,2,2,48,1024]{6,5,4,3,2,1,0:T(8,128)(2,1)} %get-tuple-element.44) | copy-start | bytes 9437188
  194.8 12.2 %copy-start.1 = (f32[1024,1536]{1,0:T(8,128)}, f32[1024,1536]{1,0:T(8,128)S(1)}, u32[]{:S(2)}) copy-start(f32[1024,1536]{1,0:T(8,128)S(1)} %get-tuple-element.80) | copy-start | bytes 18874372
  194.9 4.2 copy-start.14
  194.9 4.5 copy-start.17
  305.3 2.6 copy-start.2
  311.1 15.7 %copy-start.4 = (bf16[8,192,1024]{2,1,0:T(8,128)(2,1)S(1)}, bf16[8,192,1024]{2,1,0:T(8,128)(2,1)}, u32[]{:S(2)}) copy-start(bf16[8,192,1024]{2,1,0:T(8,128)(2,1)} %get-tuple-element.41) | copy-start | bytes 9437188
  326.8 2.3 copy-start.5
  329.1 8.0 %copy-start.15 = (bf16[1024,1536]{1,0:T(8,128)(2,1)S(1)}, bf16[1024,1536]{1,0:T(8,128)(2,1)}, u32[]{:S(2)}) copy-start(bf16[1024,1536]{1,0:T(8,128)(2,1)} %get-tuple-element.49) | copy-start | bytes 9437188
  337.1 5.7 %copy-start.6 = (bf16[1024,512]{1,0:T(8,128)(2,1)S(1)}, bf16[1024,512]{1,0:T(8,128)(2,1)}, u32[]{:S(2)}) copy-start(bf16[1024,512]{1,0:T(8,128)(2,1)} %attn_grads.1) | copy-start | bytes 3145732
  411.8 30.0 %copy-start.13 = (bf16[8,48,256]{2,1,0:T(8,128)(2,1)S(1)}, bf16[8,48,256]{2,1,0:T(8,128)(2,1)}, u32[]{:S(2)}) copy-start(bf16[8,48,256]{2,1,0:T(8,128)(2,1)} %get-tuple-element.56) | copy-start | bytes 589828
  413.5 29.5 %copy-start.12 = (bf16[8,48,512]{2,1,0:T(8,128)(2,1)S(1)}, bf16[8,48,512]{2,1,0:T(8,128)(2,1)}, u32[]{:S(2)}) copy-start(bf16[8,48,512]{2,1,0:T(8,128)(2,1)} %get-tuple-element.55) | copy-start | bytes 1179652
  445.0 4.7 %copy-start.8 = (bf16[8,48,1024]{2,1,0:T(8,128)(2,1)S(1)}, bf16[8,48,1024]{2,1,0:T(8,128)(2,1)}, u32[]{:S(2)}) copy-start(bf16[8,48,1024]{2,1,0:T(8,128)(2,1)} %get-tuple-element.57) | copy-start | bytes 2359300
  450.8 3.2 copy-start.11
  452.0 2.7 copy-start.7

commit v4 on v3

--- a/solution.py
+++ b/solution.py
@@ -403,6 +403,10 @@
     def peers(self):
         return [self.device(bits) for bits in self.others()]
 
+    def same_core(self):
+        beyond = [self.device(bits, far=1 - self.far) for bits in self.others() + [self.own]]
+        return self.peers() + beyond
+
 
 def make_send(source, target, sems, device):
     return pltpu.make_async_remote_copy(
@@ -441,7 +445,19 @@
                 live.remove(one)
 
 
+def in_step(live):
+    live = list(live)
+    while live:
+        for one in list(live):
+            try:
+                next(one)
+            except StopIteration:
+                live.remove(one)
+        yield
+
+
 ORDERS = ((0, 1, 2), (1, 2, 0), (2, 0, 1))
+ORDERS_Z_FIRST = ((1, 0, 2), (1, 2, 0))
 
 
 def gather_cube(here, place_of, order, sems):
@@ -465,11 +481,16 @@
         copy.wait_send()
 
 
-def gather_cube_thirds(here, place_of, sems):
-    return [
-        gather_cube(here, functools.partial(place_of, third=third), order, sems)
-        for third, order in enumerate(ORDERS)
-    ]
+def gather_cube_parts(here, place_of, size, orders, sems):
+    step = size // len(orders)
+    return in_step(
+        [
+            gather_cube(
+                here, functools.partial(place_of, part=pl.ds(index * step, step)), order, sems
+            )
+            for index, order in enumerate(orders)
+        ]
+    )
 
 
 def total_of(*refs):
@@ -479,73 +500,87 @@
     return total
 
 
-def reduce_cube(here, part_of, slots, out, order, sems):
-    c, b, a = order
-    own = here.own
-    sends = []
-
-    def to(bits, slot, bit):
-        sends.append(send(part_of(bits), slots(slot), sems(), here.next(bit)))
-        return sends[-1]
-
-    c0 = to(here.flip(c, b, a), 0, c)
-    c1 = to(here.flip(c, b), 1, c)
-    c2 = to(here.flip(c, a), 2, c)
-    c3 = to(here.flip(c), 3, c)
-    yield
-    c0.wait_recv()
-    spot = part_of(here.flip(b, a))
-    spot[...] = total_of(spot, slots(0)).astype(BF16)
-    b0 = to(here.flip(b, a), 4, b)
-    yield
-    c1.wait_recv()
-    spot = part_of(here.flip(b))
-    spot[...] = total_of(spot, slots(1)).astype(BF16)
-    b1 = to(here.flip(b), 5, b)
-    yield
-    c2.wait_recv()
-    b0.wait_recv()
-    spot = part_of(here.flip(a))
-    spot[...] = total_of(spot, slots(2), slots(4)).astype(BF16)
-    a0 = to(here.flip(a), 6, a)
-    yield
-    c3.wait_recv()
-    b1.wait_recv()
-    a0.wait_recv()
-    out[...] = total_of(part_of(own), slots(3), slots(5), slots(6))
-    yield
-    for copy in sends:
-        copy.wait_send()
-
-
-def reduce_cube_all(here, part, slots, out, sems):
-    width = out.shape[1] // 6
-    streams = []
-    for index in range(6):
-        columns = pl.ds(index * width, width)
-        streams.append(
-            reduce_cube(
-                here,
-                lambda bits, columns=columns: part.at[bits[0], bits[1], bits[2], :, columns],
-                lambda slot, columns=columns: slots.at[slot, :, columns],
-                out.at[:, columns],
-                ORDERS[index // 2],
-                sems,
-            )
-        )
-    return streams
+PAIRS = (((0, 1, 2), (0, 1)), ((1, 2), (0, 2)), ((0,), (2,)), ((1,), ()))
+
+
+class ReduceStream:
+    def __init__(self, here, part_of, slots, out, order, sems):
+        self.here, self.part_of, self.slots, self.out = here, part_of, slots, out
+        c, b, a = self.order = order
+        self.first = [(c, b, a), (c, b), (c, a), (c,)]
+        self.copies = [None] * (CUBE - 1)
+        self.sems = [sems() for _ in range(CUBE - 1)]
+        self.made = set()
+
+    def send(self, turned, slot, bit):
+        self.copies[slot] = send(
+            self.part_of(self.here.flip(*turned)),
+            self.slots(slot),
+            self.sems[slot],
+            self.here.next(bit),
+        )
+
+    def add(self, turned, *slots):
+        for slot in slots:
+            self.copies[slot].wait_recv()
+        spot = self.part_of(self.here.flip(*turned))
+        spot[...] = total_of(spot, *[self.slots(slot) for slot in slots]).astype(BF16)
+
+    def after(self, pair):
+        c, b, a = self.order
+        before = set(self.made)
+        self.made |= {frozenset(turned) for turned in PAIRS[pair]}
+        for slot, turned in enumerate(self.first):
+            if frozenset(turned) in self.made - before:
+                self.send(turned, slot, c)
+        if self.copies[4] is None and self.copies[0] is not None and frozenset((b, a)) in self.made:
+            self.add((b, a), 0)
+            self.send((b, a), 4, b)
+        if self.copies[5] is None and self.copies[1] is not None and frozenset((b,)) in self.made:
+            self.add((b,), 1)
+            self.send((b,), 5, b)
+
+    def finish(self):
+        _, b, a = self.order
+        self.add((a,), 2, 4)
+        self.send((a,), 6, a)
+        yield
+        for slot in (3, 5, 6):
+            self.copies[slot].wait_recv()
+        self.out[...] = total_of(
+            self.part_of(self.here.own), self.slots(3), self.slots(5), self.slots(6)
+        )
+        yield
+        for copy in self.copies:
+            copy.wait_send()
+
+
+def reductions(here, part, slots, out, orders, sems):
+    width = out.shape[1] // len(orders)
+    return [
+        ReduceStream(
+            here,
+            lambda bits, columns=columns: part.at[here.shard_of(bits), :, columns],
+            lambda slot, columns=columns: slots.at[slot, :, columns],
+            out.at[:, columns],
+            order,
+            sems,
+        )
+        for columns, order in [
+            (pl.ds(index * width, width), order) for index, order in enumerate(orders)
+        ]
+    ]
 
 
 def swap_home(here, source, target, relay, local_sem, sems, beyond=None):
     beyond = target if beyond is None else beyond
     half = source.shape[1] // 2
     left, right = pl.ds(0, half), pl.ds(half, half)
-    by_x = here.next(0)
+    there = here.device(here.flip(0), far=1 - here.far)
     local = pltpu.make_async_copy(source, target, local_sem)
-    out_left = make_send(source.at[:, left], relay.at[0], sems(), here.across)
-    out_right = make_send(source.at[:, right], relay.at[1], sems(), by_x)
-    on_left = make_send(relay.at[0], beyond.at[:, left], sems(), by_x)
-    on_right = make_send(relay.at[1], target.at[:, right], sems(), here.across)
+    straight = make_send(source.at[:, left], beyond.at[:, left], sems(), there)
+    aside = make_send(source.at[:, right], relay, sems(), here.next(0))
+    onward = make_send(relay, target.at[:, right], sems(), here.across)
 
     @pl.when(here.at_home)
     def _():
@@ -553,35 +588,34 @@
 
     @pl.when(jnp.logical_not(here.at_home))
     def _():
-        out_left.start()
-        out_right.start()
+        aside.start()
+        straight.start()
 
     yield
 
     @pl.when(here.at_home)
     def _():
-        out_left.wait_recv()
-        on_left.start()
-        out_right.wait_recv()
-        on_right.start()
+        aside.wait_recv()
+        onward.start()
+
+    yield
+
+    @pl.when(here.at_home)
+    def _():
         local.wait()
 
     @pl.when(jnp.logical_not(here.at_home))
     def _():
-        on_left.wait_recv()
-        on_right.wait_recv()
+        straight.wait_recv()
+        onward.wait_recv()
+        straight.wait_send()
+        aside.wait_send()
 
     yield
 
     @pl.when(here.at_home)
     def _():
-        on_left.wait_send()
-        on_right.wait_send()
-
-    @pl.when(jnp.logical_not(here.at_home))
-    def _():
-        out_left.wait_send()
-        out_right.wait_send()
+        onward.wait_send()
 
 
 def spread(here, place_of, sems, ready=()):
@@ -589,8 +623,6 @@
         copy.wait()
     over = send(place_of(here.far), place_of(here.far), sems(), here.across)
     beside = send(place_of(here.far), place_of(here.far), sems(), here.sibling)
-    yield
-    yield
     yield
     over.wait_recv()
     last = send(place_of(1 - here.far), place_of(1 - here.far), sems(), here.sibling)
@@ -611,21 +643,9 @@
         for bits in here.others()
     ]
     yield
-    yield
     yield from spread(
         here, lambda far: target.at[:, here.core, far], sems, copies + [local]
     )
-
-
-def in_step(live):
-    live = list(live)
-    while live:
-        for one in list(live):
-            try:
-                next(one)
-            except StopIteration:
-                live.remove(one)
-        yield
 
 
 ANY = pl.BlockSpec(memory_space=pltpu.MemorySpace.HBM)
@@ -644,11 +664,12 @@
 
 
 def half_blocks(block):
-    return pltpu.VMEM((2, block[0], block[1] // 2), BF16)
+    return pltpu.VMEM((block[0], block[1] // 2), BF16)
 
 
 QUERY_TILE = 256
 NT = (((1,), (1,)), ((), ()))
+TN = (((0,), (0,)), ((), ()))
 
 
 def dot(left, right):
@@ -657,6 +678,10 @@
 
 def dot_nt(left, right):
     return lax.dot_general(left, right, NT, preferred_element_type=F32)
+
+
+def dot_tn(left, right):
+    return lax.dot_general(left, right, TN, preferred_element_type=F32)
 
 
 def rotate(head, cosine, sine):
@@ -699,19 +724,18 @@
 
 def front_kernel(
     tokens, cotangent, qkv, gate_up, down, out, cosine, sine,
-    x_all, ct_all, w_qkv, w_gu, w_d, w_o, ob_all, h1, q, k, v, o_t, lse, gains,
-    v_t, x_relay, ct_relay, local, sent, got,
+    w_qkv, w_gu, w_d, w_o, ob_all, h1, q, k, v, o_t, lse, gains, out_part, dh2, x_own, ct_own, y1_own,
+    x_all, ct_all, v_t, hidden, d_gu, dh2_part, slots, x_relay, ct_relay, local, sent, got,
 ):
     here = Here()
     sems = Sems(sent, got)
-    here.greet(here.peers() + [here.sibling, here.across])
+    here.greet(here.same_core() + [here.sibling])
     x, z, y = here.own
     width = tokens.shape[1]
     block_rows = tokens.shape[0]
     seq_rows = CUBE * block_rows
 
-    def swapped(source, target, relay, local_sem):
-        third_width = width // 3
+    def swapped(source, target, relay, local_sem, orders):
         yield from swap_home(
             here,
             source,
@@ -721,18 +745,11 @@
             sems,
             target.at[here.shard_of(here.flip(0))],
         )
-        yield from in_step(
-            gather_cube_thirds(
-                here,
-                lambda bits, third: target.at[
-                    here.shard_of(bits), :, pl.ds(third * third_width, third_width)
-                ],
-                sems,
-            )
+        yield from gather_cube_parts(
+            here, lambda bits, part: target.at[here.shard_of(bits), :, part], width, orders, sems
         )
 
     def out_gather():
-        third_width = width // 3
         mine = w_o.at[x, here.core, here.far, z, y]
         kept = pltpu.make_async_copy(out, mine, local.at[3])
         kept.start()
@@ -740,20 +757,12 @@
         yield
         kept.wait()
         over.wait()
-        yield from in_step(
-            gather_cube_thirds(
-                here,
-                lambda bits, third: w_o.at[
-                    bits[0],
-                    here.core,
-                    :,
-                    bits[1],
-                    bits[2],
-                    :,
-                    pl.ds(third * third_width, third_width),
-                ],
-                sems,
-            )
+        yield from gather_cube_parts(
+            here,
+            lambda bits, part: w_o.at[bits[0], here.core, :, bits[1], bits[2], :, part],
+            width,
+            ORDERS_Z_FIRST,
+            sems,
         )
         beside = send(w_o.at[:, here.core], w_o.at[:, here.core], sems(), here.sibling)
         yield
@@ -764,29 +773,42 @@
         kept.start()
         yield from spread(here, lambda far: w_d.at[here.core, far], sems, [kept])
 
-    get_x = swapped(tokens, x_all, x_relay, local.at[0])
+    get_x = swapped(tokens, x_all, x_relay, local.at[0], ORDERS)
     get_qkv = gather_columns(here, qkv, w_qkv, local.at[4], sems)
     get_gu = gather_columns(here, gate_up, w_gu, local.at[5], sems)
     get_out = out_gather()
     get_down = down_gather()
-    get_ct = swapped(cotangent, ct_all, ct_relay, local.at[1])
-    next(get_x)
-    next(get_qkv)
-    next(get_out)
-    next(get_x)
-    next(get_x)
-    next(get_qkv)
-    next(get_down)
-    next(get_gu)
-    next(get_ct)
+    get_ct = swapped(cotangent, ct_all, ct_relay, local.at[1], ORDERS_Z_FIRST)
+    for step in (
+        get_x,
+        get_qkv,
+        get_out,
+        get_x,
+        get_qkv,
+        get_gu,
+        get_x,
+        get_x,
+        get_ct,
+        get_x,
+        get_ct,
+        get_gu,
+        get_x,
+        get_down,
+        get_x,
+        get_qkv,
+        get_ct,
+        get_out,
+        get_ct,
+    ):
+        next(step)
     run_all(get_x, get_qkv)
-    later = in_step([get_ct, get_gu, get_out, get_down])
+    later = in_step([get_ct, get_out, get_gu, get_down])
 
     turned = jnp.transpose(
         w_qkv[:, :, :, :, :, :, 3 * HEAD_LANES :].astype(F32).reshape(width, HEAD_LANES)
     )
     gains[...] = turned[HEAD_SIZE : HEAD_SIZE + 8]
-    next(later)
+    next(later, None)
 
     def norm_block(index, carry):
         rows = x_all[index].astype(F32)
@@ -796,7 +818,7 @@
         return carry
 
     lax.fori_loop(0, CUBE, norm_block, 0)
-    next(later)
+    next(later, None)
 
     def project(index, carry):
         rows = pl.ds(pl.multiple_of(index * QUERY_TILE, QUERY_TILE), QUERY_TILE)
@@ -811,10 +833,9 @@
         return carry
 
     lax.fori_loop(0, seq_rows // QUERY_TILE, project, 0)
-    next(later)
+    next(later, None)
 
     ob = ob_all.at[here.shard]
-    row_third = ob.shape[0] // 3
     streams = []
     tiles = seq_rows // QUERY_TILE
     for tile in range(tiles):
@@ -822,19 +843,86 @@
             attend_tile(q, k, v_t, o_t, ob, lse, group, tile)
         if tile % 2 == 1:
             lanes = pl.ds((tile - 1) * QUERY_TILE, 2 * QUERY_TILE)
-            half = in_step(
-                gather_cube_thirds(
-                    here,
-                    lambda bits, third, lanes=lanes: ob_all.at[
-                        here.shard_of(bits), pl.ds(third * row_third, row_third), lanes
-                    ],
-                    sems,
-                )
+            half = gather_cube_parts(
+                here,
+                lambda bits, part, lanes=lanes: ob_all.at[here.shard_of(bits), part, lanes],
+                ob.shape[0],
+                ORDERS,
+                sems,
             )
-            next(half)
+            next(half, None)
             streams.append(half)
-        next(later)
+        next(later, None)
     run_all(*streams, later)
+
+    x_own[...] = x_all[here.shard]
+    ct_own[...] = ct_all[here.shard]
+    streams = reductions(here, dh2_part, slots, dh2, ORDERS, sems)
+    for pair, turned in enumerate(PAIRS):
+        shards = [here.shard_of(here.flip(*bits)) for bits in turned]
+        feed_forward(
+            shards, x_all, ct_all, ob_all, w_o, w_gu, w_d, gains, hidden, d_gu, out_part, dh2_part,
+            y1_own if turned[-1] == () else None,
+        )
+        for stream in streams:
+            stream.after(pair)
+    finish = in_step([stream.finish() for stream in streams])
+    next(finish, None)
+
+    def gate_up_grad(index, carry):
+        lanes = pl.ds(pl.multiple_of(index * 4 * HEAD_SIZE, 4 * HEAD_SIZE), 4 * HEAD_SIZE)
+        left = x_all[:, :, lanes].reshape(seq_rows, 4 * HEAD_SIZE)
+        grad = dot_tn(left, d_gu[...]).astype(BF16)
+        w_gu[index // 2, lax.rem(index, 2)] = grad.reshape(w_gu.shape[2:])
+        return carry
+
+    def down_grad(index, carry):
+        lanes = pl.ds(pl.multiple_of(index * HEAD_LANES, HEAD_LANES), HEAD_LANES)
+        grad = dot_tn(hidden[:, lanes], ct_all[...].reshape(seq_rows, width)).astype(BF16)
+        w_d[index // 2, lax.rem(index, 2)] = grad
+        return carry
+
+    lax.fori_loop(0, 4, down_grad, 0)
+    next(finish, None)
+    lax.fori_loop(0, 4, gate_up_grad, 0)
+    for _ in finish:
+        pass
+
+
+def feed_forward(
+    shards, x_all, ct_all, ob_all, w_o, w_gu, w_d, gains, hidden, d_gu, out_part, dh2_part, y1_own
+):
+    _, block_rows, width = x_all.shape
+    share = d_gu.shape[1] // 2
+    pair = lambda ref: jnp.concatenate([ref[shard] for shard in shards], axis=0)
+    rows_of = [
+        pl.ds(pl.multiple_of(shard * block_rows, block_rows), block_rows) for shard in shards
+    ]
+    ob_t = jnp.concatenate([ob_all[:, :, rows].reshape(width, block_rows) for rows in rows_of], axis=1)
+    y1 = pair(x_all).astype(F32) + dot_tn(ob_t, w_o[...].reshape(width, width))
+    inv_root = lax.rsqrt(jnp.mean(y1 * y1, axis=-1, keepdims=True) + NORM_EPS)
+    h2 = (y1 * inv_root * gains[1:2, :]).astype(BF16)
+    if y1_own is not None:
+        y1_own[...] = y1[block_rows:]
+    gate_up = dot(h2, w_gu[...].reshape(width, 2 * share))
+    gate, up = gate_up[:, :share], gate_up[:, share:]
+    sig = 1.0 / (1.0 + jnp.exp(-gate))
+    silu = gate * sig
+    kept = (silu * up).astype(BF16)
+    down = w_d[...].reshape(share, width)
+    d_hidden = dot_nt(pair(ct_all), down)
+    d_gate = (d_hidden * up * sig * (1.0 + gate * (1.0 - sig))).astype(BF16)
+    d_up = (d_hidden * silu).astype(BF16)
+    d_both = jnp.concatenate([d_gate, d_up], axis=1)
+    dh2 = dot_nt(d_both, w_gu[...].reshape(width, 2 * share)).astype(BF16)
+    out = dot(kept, down).astype(BF16)
+    for index, (shard, rows) in enumerate(zip(shards, rows_of)):
+        block = slice(index * block_rows, (index + 1) * block_rows)
+        x_all[shard] = h2[block]
+        hidden[rows, :] = kept[block]
+        d_gu[rows, :] = d_both[block]
+        dh2_part[shard] = dh2[block]
+        out_part[shard] = out[block]
 
 
 def front(tokens, cotangent, qkv, gate_up, down, out, cosine, sine):
@@ -844,9 +932,8 @@
     rows, width = tokens.shape
     seq_rows = CUBE * rows
     share = 2 * HEAD_SIZE
+    ff_share = 4 * down.shape[0]
     outs = (
-        shape(CUBE, rows, width),
-        shape(CUBE, rows, width),
         shape(*slots, *qkv.shape[1:]),
         shape(*slots, *gate_up.shape[1:]),
         shape(2, 2, *down.shape),
@@ -859,6 +946,11 @@
         wide(2, HEAD_LANES, seq_rows),
         wide(2, 1, seq_rows),
         wide(8, width),
+        shape(CUBE, rows, width),
+        wide(rows, width),
+        shape(rows, width),
+        shape(rows, width),
+        wide(rows, width),
     )
     return pl.pallas_call(
         front_kernel,
@@ -866,12 +958,18 @@
         in_specs=[VMEM] * 8,
         out_specs=(VMEM,) * len(outs),
         scratch_shapes=[
+            pltpu.VMEM((CUBE, rows, width), BF16),
+            pltpu.VMEM((CUBE, rows, width), BF16),
             pltpu.VMEM((HEAD_LANES, seq_rows), BF16),
+            pltpu.VMEM((seq_rows, ff_share), BF16),
+            pltpu.VMEM((seq_rows, 2 * ff_share), BF16),
+            pltpu.VMEM((CUBE, rows, width), BF16),
+            pltpu.VMEM((CUBE - 1, rows, width), BF16),
             half_blocks(tokens.shape),
             half_blocks(tokens.shape),
             pltpu.SemaphoreType.DMA((6,)),
         ]
-        + dma_sems(140),
+        + dma_sems(162),
         compiler_params=params(1),
         name="front",
     )(tokens, cotangent, qkv, gate_up, down, out, cosine, sine)
@@ -902,41 +1000,6 @@
     return jnp.transpose(dq_t) * HEAD_SIZE**-0.5
 
 
-def attn_grads_kernel(q, k, v, do_t, o_t, lse, cosine, sine, d_qkv, k_t, dk, dv):
-    seq_rows = k.shape[0]
-    k_t[...] = jnp.transpose(k[...].astype(F32)).astype(BF16)
-    dk[...] = jnp.zeros_like(dk)
-    dv[...] = jnp.zeros_like(dv)
-    for tile in range(seq_rows // QUERY_TILE):
-        rows = pl.ds(tile * QUERY_TILE, QUERY_TILE)
-        for group in range(2):
-            dq = attend_back_tile(q, k, k_t, v, do_t, o_t, lse, dk, dv, group, tile)
-            d_qkv[rows, group * HEAD_LANES : (group + 1) * HEAD_LANES] = rotate(
-                dq, cosine[rows, :], -sine[rows, :]
-            ).astype(BF16)
-    d_qkv[:, 2 * HEAD_LANES : 3 * HEAD_LANES] = rotate(
-        dk[...] * HEAD_SIZE**-0.5, cosine[...], -sine[...]
-    ).astype(BF16)
-    d_qkv[:, 3 * HEAD_LANES :] = dv[...].astype(BF16)
-
-
-def attn_grads(q, k, v, do_t, o_t, lse, cosine, sine):
-    seq_rows = k.shape[0]
-    return pl.pallas_call(
-        attn_grads_kernel,
-        out_shape=jax.ShapeDtypeStruct((seq_rows, SHARE), BF16),
-        in_specs=[VMEM] * 8,
-        out_specs=VMEM,
-        scratch_shapes=[
-            pltpu.VMEM((HEAD_LANES, seq_rows), BF16),
-            pltpu.VMEM((seq_rows, HEAD_LANES), F32),
-            pltpu.VMEM((seq_rows, HEAD_LANES), F32),
-        ],
-        compiler_params=pltpu.CompilerParams(vmem_limit_bytes=VMEM_BYTES),
-        name="attn_grads",
-    )(q, k, v, do_t, o_t, lse, cosine, sine)
-
-
 def add_rows(total, more, piece):
     def body(index, carry):
         rows = pl.ds(pl.multiple_of(index * piece, piece), piece)
@@ -960,8 +1023,6 @@
     second.wait_recv()
     add_rows(part.at[:, core, far], beside.at[1], piece)
     yield
-    yield
-    yield
     third.wait_recv()
     add_rows(part.at[:, core, far], over, piece)
     for copy in (first, second, third):
@@ -986,181 +1047,216 @@
         copy.wait()
 
 
-def ff_back_kernel(
-    dh2_part, out_part, gu_part, down_part,
-    dh2, out, gu_rows, down_sum,
-    dh2_slots, out_slots, gu_beside, gu_over, down_beside, down_over, local, sent, got,
+def copy_slots(part):
+    blocks, _, _, rows, share = part.shape
+    return [pltpu.VMEM((2, blocks, rows, share), BF16), pltpu.VMEM((blocks, rows, share), BF16)]
+
+
+def by_owner(part):
+    rows, share = part.shape[3:]
+    return jax.ShapeDtypeStruct((CUBE, rows // 4, share), BF16)
+
+
+def norm_back_rows(grad_normed, rows, gain):
+    inv_root = lax.rsqrt(jnp.mean(rows * rows, axis=-1, keepdims=True) + NORM_EPS)
+    grad_gain, grad_rows = norm_back(grad_normed, rows, inv_root, gain)
+    return grad_gain.reshape(1, -1), grad_rows
+
+
+def sum_everywhere(here, total, slots, sems):
+    hops = [here.sibling] + [here.next(bit) for bit in BITS] + [here.across]
+    for index, device in enumerate(hops):
+        copy = send(total, slots.at[index], sems(), device)
+        yield
+        copy.wait()
+        total[...] += slots[index]
+
+
+def back_kernel(
+    dh2, x_own, ct_own, y1_own, gains, out_part, gu_part, down_part,
+    w_qkv, w_o, ob_all, h1, q, k, v, o_t, lse, cosine, sine,
+    output_home, grad_home, gu_rows, down_sum, qkv_rows, out_rows, gain_sums,
+    d_middle, pairs, columns, d_qkv, k_t, dk, dv, dh1_part, dh1, dh1_slots, out_sum, out_slots,
+    gu_beside, gu_over, down_beside, down_over, qkv_part, qkv_beside, qkv_over,
+    wo_part, wo_beside, wo_over, own_rows, relay, relay_too, gain_slots, local, sent, got,
 ):
     here = Here()
     sems = Sems(sent, got)
-    here.greet(here.peers() + [here.sibling, here.across])
+    here.greet(here.same_core() + [here.sibling])
+    block_rows, width = dh2.shape
+    seq_rows = CUBE * block_rows
+    share = 2 * HEAD_SIZE
+
+    def half_gu(index):
+        lanes = pl.ds(index * gu_part.shape[4] // 2, gu_part.shape[4] // 2)
+        return scatter_columns(
+            here,
+            gu_part.at[:, :, :, :, lanes],
+            gu_beside.at[:, :, :, lanes],
+            gu_over.at[:, :, lanes],
+            gu_rows.at[:, :, lanes],
+            local.at[index],
+            sems,
+        )
 
     def down_reduce():
         yield from reduce_copies(here, down_part, down_beside, down_over, sems, 32)
         down_sum[...] = down_part[0, here.core, here.far].astype(F32)
 
-    run_all(
-        *reduce_cube_all(here, dh2_part, dh2_slots, dh2, sems),
-        scatter_columns(here, gu_part, gu_beside, gu_over, gu_rows, local, sems),
-        down_reduce(),
-        *reduce_cube_all(here, out_part, out_slots, out, sems),
-    )
-
-
-def copy_slots(part):
-    blocks, _, _, rows, share = part.shape
-    return [pltpu.VMEM((2, blocks, rows, share), BF16), pltpu.VMEM((blocks, rows, share), BF16)]
-
-
-def by_owner(part):
-    rows, share = part.shape[3:]
-    return jax.ShapeDtypeStruct((CUBE, rows // 4, share), BF16)
-
-
-def ff_back(dh2_part, out_part, gu_part, down_part):
-    rows, width = dh2_part.shape[3:]
-    own = jax.ShapeDtypeStruct((rows, width), F32)
+    grads = in_step([half_gu(0), half_gu(1), down_reduce()])
+    next(grads, None)
+
+    y1 = y1_own[...]
+    grad_gain, back = norm_back_rows(dh2[...], y1, gains[1:2, :])
+    gain_sums[...] = jnp.zeros_like(gain_sums)
+    gain_sums[1:2, :] = grad_gain
+    d_middle[...] = ct_own[...].astype(F32) + back
+    da = d_middle[...].astype(BF16)
+    pairs[:, 0] = dot_nt(w_o[...], da).astype(BF16).reshape(CUBE, share, block_rows)
+    pairs[:, 1] = jnp.transpose(d_middle[...]).astype(BF16).reshape(CUBE, share, block_rows)
+    place = columns.at[:, :, pl.ds(pl.multiple_of(here.shard * block_rows, block_rows), block_rows)]
+    kept = pltpu.make_async_copy(pairs.at[here.shard], place, local.at[2])
+    kept.start()
+    copies = [
+        send(pairs.at[here.shard_of(bits)], place, sems(), here.device(bits))
+        for bits in here.others()
+    ]
+    next(grads, None)
+    k_t[...] = jnp.transpose(k[...].astype(F32)).astype(BF16)
+    dk[...] = jnp.zeros_like(dk)
+    dv[...] = jnp.zeros_like(dv)
+    for copy in copies + [kept]:
+        copy.wait()
+
+    sums = reductions(here, out_part, out_slots, out_sum, ORDERS, sems)
+    for tile in range(seq_rows // QUERY_TILE):
+        for stream in sums:
+            stream.after(tile)
+        rows = pl.ds(tile * QUERY_TILE, QUERY_TILE)
+        for group in range(2):
+            dq = attend_back_tile(
+                q, k, k_t, v, columns.at[0], o_t, lse, dk, dv, group, tile
+            )
+            d_qkv[rows, group * HEAD_LANES : (group + 1) * HEAD_LANES] = rotate(
+                dq, cosine[rows, :], -sine[rows, :]
+            ).astype(BF16)
+    d_qkv[:, 2 * HEAD_LANES : 3 * HEAD_LANES] = rotate(
+        dk[...] * HEAD_SIZE**-0.5, cosine[...], -sine[...]
+    ).astype(BF16)
+    d_qkv[:, 3 * HEAD_LANES :] = dv[...].astype(BF16)
+
+    streams = reductions(here, dh1_part, dh1_slots, dh1, ORDERS, sems)
+    for pair, turned in enumerate(PAIRS):
+        shards = [here.shard_of(here.flip(*bits)) for bits in turned]
+        some = jnp.concatenate(
+            [
+                d_qkv[pl.ds(pl.multiple_of(shard * block_rows, block_rows), block_rows), :]
+                for shard in shards
+            ],
+            axis=0,
+        )
+        rows = dot_nt(some, w_qkv[...]).astype(BF16)
+        for index, shard in enumerate(shards):
+            dh1_part[shard] = rows[index * block_rows : (index + 1) * block_rows]
+        for stream in streams:
+            stream.after(pair)
+    finish_out = in_step([stream.finish() for stream in sums])
+    finish = in_step([stream.finish() for stream in streams])
+    next(finish_out, None)
+    next(finish, None)
+
+    def qkv_grad(index, carry):
+        lanes = pl.ds(pl.multiple_of(index * 4 * HEAD_SIZE, 4 * HEAD_SIZE), 4 * HEAD_SIZE)
+        grad = dot_tn(h1[:, lanes], d_qkv[...]).astype(BF16)
+        qkv_part[index // 2, lax.rem(index, 2)] = grad.reshape(qkv_part.shape[2:])
+        return carry
+
+    lax.fori_loop(0, 4, qkv_grad, 0)
+    grads_too = [
+        scatter_columns(here, qkv_part, qkv_beside, qkv_over, qkv_rows, local.at[3], sems)
+    ]
+    next(grads_too[0], None)
+    next(finish_out, None)
+    output = (y1_own[...] + out_sum[...]).astype(BF16)
+    own_rows[0] = output
+    swap_output = swap_home(here, own_rows.at[0], output_home, relay, local.at[4], sems)
+    next(swap_output, None)
+
+    for index in range(4):
+        left = ob_all[2 * index : 2 * index + 2].reshape(2 * share, seq_rows)
+        grad = dot_nt(left, columns[1]).astype(BF16)
+        grad = jnp.concatenate(
+            [grad, jnp.zeros((2 * share, wo_part.shape[4] - share), BF16)], axis=1
+        )
+        wo_part[index // 2, index % 2] = grad.reshape(wo_part.shape[2:])
+    grads_too.append(scatter_columns(here, wo_part, wo_beside, wo_over, out_rows, local.at[5], sems))
+    next(grads_too[1], None)
+    next(grads_too[0], None)
+    for _ in finish:
+        pass
+
+    grad_gain, back = norm_back_rows(dh1[...], x_own[...].astype(F32), gains[0:1, :])
+    gain_sums[0:1, :] = grad_gain
+    own_rows[1] = (d_middle[...] + back).astype(BF16)
+    swap_grad = swap_home(here, own_rows.at[1], grad_home, relay_too, local.at[6], sems)
+    next(swap_grad, None)
+    gain_sum = sum_everywhere(here, gain_sums, gain_slots, sems)
+    next(gain_sum, None)
+    run_all(gain_sum, swap_output, swap_grad, *grads_too, grads, finish_out)
+
+
+def back(*operands):
+    dh2, x_own, _, _, _, out_part, gu_part, down_part = operands[:8]
+    rows, width = dh2.shape
+    seq_rows = CUBE * rows
+    share = 2 * HEAD_SIZE
+    part = lambda lanes: jax.ShapeDtypeStruct((*gu_part.shape[:4], lanes), BF16)
+    qkv_part, wo_part = part(SHARE), part(2 * HEAD_LANES)
+    vmem = lambda like: pltpu.VMEM(like.shape, BF16)
+    wide = lambda *dims: jax.ShapeDtypeStruct(dims, F32)
+    outs = (
+        jax.ShapeDtypeStruct((rows, width), BF16),
+        jax.ShapeDtypeStruct((rows, width), BF16),
+        by_owner(gu_part),
+        wide(*down_part.shape[3:]),
+        by_owner(qkv_part),
+        by_owner(wo_part),
+        wide(8, width),
+    )
     return pl.pallas_call(
-        ff_back_kernel,
-        out_shape=(
-            own,
-            own,
-            by_owner(gu_part),
-            jax.ShapeDtypeStruct(down_part.shape[3:], F32),
-        ),
-        in_specs=[VMEM] * 4,
-        out_specs=(VMEM,) * 4,
+        back_kernel,
+        out_shape=outs,
+        in_specs=[VMEM] * len(operands),
+        out_specs=(VMEM,) * len(outs),
         scratch_shapes=[
+            pltpu.VMEM((rows, width), F32),
+            pltpu.VMEM((CUBE, 2, share, rows), BF16),
+            pltpu.VMEM((2, share, seq_rows), BF16),
+            pltpu.VMEM((seq_rows, SHARE), BF16),
+            pltpu.VMEM((HEAD_LANES, seq_rows), BF16),
+            pltpu.VMEM((seq_rows, HEAD_LANES), F32),
+            pltpu.VMEM((seq_rows, HEAD_LANES), F32),
+            vmem(out_part),
+            pltpu.VMEM((rows, width), F32),
             pltpu.VMEM((CUBE - 1, rows, width), BF16),
+            pltpu.VMEM((rows, width), F32),
             pltpu.VMEM((CUBE - 1, rows, width), BF16),
             *copy_slots(gu_part),
             *copy_slots(down_part),
-            pltpu.SemaphoreType.DMA,
+            vmem(qkv_part),
+            *copy_slots(qkv_part),
+            vmem(wo_part),
+            *copy_slots(wo_part),
+            pltpu.VMEM((2, rows, width), BF16),
+            half_blocks((rows, width)),
+            half_blocks((rows, width)),
+            pltpu.VMEM((5, 8, width), F32),
+            pltpu.SemaphoreType.DMA((7,)),
         ]
-        + dma_sems(100),
-        compiler_params=params(3),
-        name="ff_back",
-    )(dh2_part, out_part, gu_part, down_part)
-
-
-def columns_kernel(blocks, every, local, sent, got):
-    here = Here()
-    sems = Sems(sent, got)
-    here.greet(here.peers())
-    rows = blocks.shape[3]
-    place = every.at[:, :, pl.ds(pl.multiple_of(here.shard * rows, rows), rows)]
-    kept = pltpu.make_async_copy(blocks.at[here.shard], place, local)
-    kept.start()
-    copies = [
-        send(blocks.at[here.shard_of(bits)], place, sems(), here.device(bits))
-        for bits in here.others()
-    ]
-    for copy in copies:
-        copy.wait()
-    kept.wait()
-
-
-def to_columns(blocks):
-    _, pair, share, rows = blocks.shape
-    return pl.pallas_call(
-        columns_kernel,
-        out_shape=jax.ShapeDtypeStruct((pair, share, CUBE * rows), BF16),
-        in_specs=[VMEM],
-        out_specs=VMEM,
-        scratch_shapes=[pltpu.SemaphoreType.DMA] + dma_sems(CUBE - 1),
-        compiler_params=params(4),
-        name="to_columns",
-    )(blocks)
-
-
-def attn_back_kernel(
-    dh1_part, qkv_part, out_part, output,
-    dh1, qkv_rows, out_rows, output_home,
-    slots, qkv_beside, qkv_over, out_beside, out_over, relay, local, sent, got,
-):
-    here = Here()
-    sems = Sems(sent, got)
-    here.greet(here.peers() + [here.sibling, here.across])
-    run_all(
-        *reduce_cube_all(here, dh1_part, slots, dh1, sems),
-        scatter_columns(here, out_part, out_beside, out_over, out_rows, local.at[0], sems),
-        scatter_columns(here, qkv_part, qkv_beside, qkv_over, qkv_rows, local.at[1], sems),
-        swap_home(here, output, output_home, relay, local.at[2], sems),
-    )
-
-
-def attn_back(dh1_part, qkv_part, out_part, output):
-    rows, width = dh1_part.shape[3:]
-    return pl.pallas_call(
-        attn_back_kernel,
-        out_shape=(
-            jax.ShapeDtypeStruct((rows, width), F32),
-            by_owner(qkv_part),
-            by_owner(out_part),
-            jax.ShapeDtypeStruct((rows, width), BF16),
-        ),
-        in_specs=[VMEM] * 4,
-        out_specs=(VMEM,) * 4,
-        scratch_shapes=[
-            pltpu.VMEM((CUBE - 1, rows, width), BF16),
-            *copy_slots(qkv_part),
-            *copy_slots(out_part),
-            half_blocks((rows, width)),
-            pltpu.SemaphoreType.DMA((3,)),
-        ]
-        + dma_sems(80),
-        compiler_params=params(5),
-        name="attn_back",
-    )(dh1_part, qkv_part, out_part, output)
-
-
-def finish_kernel(parts, grad, total, grad_home, every, relay, local, sent, got):
-    here = Here()
-    sems = Sems(sent, got)
-    own = here.device(here.own)
-    mine = own[0] * CUBE + own[1]
-    count = parts.shape[0]
-    others = []
-    for ahead in range(1, count):
-        rank = lax.rem(mine + ahead, count)
-        others.append((rank // CUBE, lax.rem(rank, CUBE)))
-    here.greet(others)
-    every[mine] = parts[mine]
-    swap = swap_home(here, grad, grad_home, relay, local, sems)
-    next(swap)
-    copies = []
-    for other in others:
-        copies.append(send(parts.at[other[0] * CUBE + other[1]], every.at[mine], sems(), other))
-    for _ in swap:
-        pass
-    for copy in copies:
-        copy.wait()
-    total[...] = jnp.sum(every[...], axis=0)
-
-
-def finish(parts, grad):
-    return pl.pallas_call(
-        finish_kernel,
-        out_shape=(
-            jax.ShapeDtypeStruct(parts.shape[1:], F32),
-            jax.ShapeDtypeStruct(grad.shape, BF16),
-        ),
-        in_specs=[VMEM] * 2,
-        out_specs=(VMEM,) * 2,
-        scratch_shapes=[
-            pltpu.VMEM(parts.shape, F32),
-            half_blocks(grad.shape),
-            pltpu.SemaphoreType.DMA,
-        ]
-        + dma_sems(parts.shape[0] + 3),
-        compiler_params=params(6),
-        name="finish",
-    )(parts, grad)
-
-
-def normed(rows, gain):
-    inv_root = lax.rsqrt(jnp.mean(rows * rows, axis=-1, keepdims=True) + NORM_EPS)
-    return inv_root, (rows * inv_root * gain.astype(F32)).astype(BF16)
+        + dma_sems(110),
+        compiler_params=params(2),
+        name="back",
+    )(*operands)
 
 
 def spaced_head(weight):
@@ -1198,7 +1294,6 @@
     w_up,
     w_down,
 ):
-    here = Here()
     block_rows, width = tokens.shape
     weight_rows = w_query.shape[0]
     head_group = QUERY_HEADS // KEY_VALUE_HEADS
@@ -1208,9 +1303,6 @@
     ff_width = w_gate.shape[1]
     down_rows = w_down.shape[0]
     ff_share = 4 * down_rows
-
-    def own(rows):
-        return lax.dynamic_slice_in_dim(rows, here.shard * block_rows, block_rows, 0)
 
     q_cut = spaced_head(w_query.reshape(weight_rows, CUBE, head_group, HEAD_SIZE))
     k_cut = spaced_head(key_weight.reshape(weight_rows, CUBE, HEAD_SIZE))
@@ -1233,76 +1325,20 @@
 
     gu_chunks = jnp.concatenate([ff_chunks(w_gate), ff_chunks(w_up)], axis=2)
     cosine, sine = spaced_tables(seq_rows)
-    x_all, ct_all, w_qkv, w_gu, w_d, w_o, ob_all, h1, q, k, v, o_t, lse, gains = front(
-        tokens, cotangent, qkv_chunks, gu_chunks, w_down, w_out, cosine, sine
-    )
-    gain_one, gain_two = gains[0], gains[1]
-    x_all = x_all.reshape(seq_rows, width)
-    ct_all = ct_all.reshape(seq_rows, width)
+    (
+        w_qkv, gu_part, down_part, w_o, ob_all, h1, q, k, v, o_t, lse, gains,
+        out_part, dh2, x_own, ct_own, y1_own,
+    ) = front(tokens, cotangent, qkv_chunks, gu_chunks, w_down, w_out, cosine, sine)
     w_qkv = w_qkv.reshape(width, SHARE)
-    w_gu = w_gu.reshape(width, 2 * ff_share)
-    w_d = w_d.reshape(ff_share, width)
     w_o = w_o.reshape(width, width)
-    ob_all = ob_all.reshape(width, seq_rows)
-    inputs = x_all.astype(F32)
-
-    middle = inputs + jnp.einsum("ct,cd->td", ob_all, w_o, preferred_element_type=F32)
-    inv_two, h2 = normed(middle, gain_two)
-    gate_up = jnp.dot(h2, w_gu, preferred_element_type=F32)
-    gate, up = gate_up[:, :ff_share], gate_up[:, ff_share:]
-    sig = jax.nn.sigmoid(gate)
-    silu = gate * sig
-    hidden = (silu * up).astype(BF16)
-    out_part = jnp.dot(hidden, w_d, preferred_element_type=F32).astype(BF16)
-    d_hidden = jnp.einsum("td,fd->tf", ct_all, w_d, preferred_element_type=F32)
-    d_gate = (d_hidden * up * sig * (1.0 + gate * (1.0 - sig))).astype(BF16)
-    d_up = (d_hidden * silu).astype(BF16)
-    d_gu = jnp.concatenate([d_gate, d_up], axis=1)
-    dh2_part = jnp.einsum("tf,cf->tc", d_gu, w_gu, preferred_element_type=F32).astype(BF16)
-    gu_part = row_product(h2, d_gu).astype(BF16)
-    down_part = row_product(hidden, ct_all).astype(BF16)
-    dh2, out_sum, gu_rows, grad_down = ff_back(
-        dh2_part.reshape(2, 2, 2, block_rows, width),
-        out_part.reshape(2, 2, 2, block_rows, width),
-        gu_part.reshape(2, 2, 2, 4 * weight_rows, 2 * ff_share),
+    cut = lambda part: part.reshape(2, 2, 2, 4 * weight_rows, -1)
+    output, grad_tokens, gu_rows, grad_down, qkv_rows, out_rows, gain_sums = back(
+        dh2, x_own, ct_own, y1_own, gains, out_part, cut(gu_part),
         down_part.reshape(1, 2, 2, down_rows, width),
-    )
-    middle_own = own(middle)
-    output = (middle_own + out_sum).astype(BF16)
-    grad_gain_two, back = norm_back(dh2, middle_own, own(inv_two), gain_two)
-    d_middle = own(ct_all).astype(F32) + back
-
-    da = d_middle.astype(BF16)
-    do_t = jnp.einsum("cd,td->ct", w_o, da, preferred_element_type=F32).astype(BF16)
-    pair = jnp.stack(
-        [
-            do_t.reshape(CUBE, query_share, block_rows),
-            jnp.transpose(da).reshape(CUBE, query_share, block_rows),
-        ],
-        axis=1,
-    )
-    do_da = to_columns(pair)
-    out_part = jnp.einsum("ct,et->ce", ob_all, do_da[1], preferred_element_type=F32).astype(BF16)
-    out_part = jnp.pad(out_part, ((0, 0), (0, 2 * HEAD_LANES - query_share)))
-
-    d_qkv = attn_grads(q, k, v, do_da[0], o_t, lse, cosine, sine)
-    qkv_part = row_product(h1, d_qkv).astype(BF16)
-    dh1_part = jnp.einsum("tq,cq->tc", d_qkv, w_qkv, preferred_element_type=F32).astype(BF16)
-    dh1, qkv_rows, out_rows, output = attn_back(
-        dh1_part.reshape(2, 2, 2, block_rows, width),
-        qkv_part.reshape(2, 2, 2, 4 * weight_rows, SHARE),
-        out_part.reshape(2, 2, 2, 4 * weight_rows, 2 * HEAD_LANES),
-        output,
-    )
-    own_inputs = own(inputs)
-    inv_one, _ = normed(own_inputs, gain_one)
-    grad_gain_one, back = norm_back(dh1, own_inputs, inv_one, gain_one)
-    grad_tokens = d_middle + back
-    gain_parts = jnp.stack([grad_gain_one, grad_gain_two]).reshape(2, width // weight_rows, weight_rows)
-    gain_parts = jnp.pad(
-        jnp.transpose(gain_parts, (1, 0, 2)), ((0, 0), (0, 6), (0, HEAD_LANES - weight_rows))
-    )
-    gain_sums, grad_tokens = finish(gain_parts, grad_tokens.astype(BF16))
+        w_qkv, w_o, ob_all, h1, q, k, v, o_t, lse, cosine, sine,
+    )
+    rank = lax.axis_index("dp") * lax.axis_size("ctx") + lax.axis_index("ctx")
+    gain_sums = lax.dynamic_slice_in_dim(gain_sums[:2], rank * weight_rows, weight_rows, 1)
 
     qkv_rows = jnp.transpose(qkv_rows.astype(F32), (1, 0, 2)).reshape(weight_rows, CUBE, 4, HEAD_LANES)
     out_rows = jnp.transpose(out_rows.astype(F32), (1, 0, 2))[..., :query_share]
@@ -1314,12 +1350,12 @@
     return (
         output,
         grad_tokens.astype(F32),
-        gain_sums[0, :weight_rows],
+        gain_sums[0],
         packed_head(qkv_rows[:, :, :head_group]).reshape(weight_rows, -1),
         packed_head(qkv_rows[:, :, head_group]).reshape(weight_rows, -1),
         qkv_rows[:, :, 3, :HEAD_SIZE].reshape(weight_rows, -1),
         out_rows.reshape(weight_rows, width),
-        gain_sums[1, :weight_rows],
+        gain_sums[1],
         ff_joined(gu_rows[:, :, :ff_share]),
         ff_joined(gu_rows[:, :, ff_share:]),
         grad_down,

time: 462 us -> 405 us (0.88)
  matrix products: 43.1 us -> 0 us
  other arithmetic: 19.5 us -> 6.67 us
  local copies, waits for them, and re-layouts: 28.2 us -> 19.1 us
  Pallas kernels: 364 us -> 372 us
    dot_general x11 -> x0, matrix products: 43.1 us -> none  [the longest x3 13.5 us: row_product(): jnp.einsum('tc,tf->cf', left, right, preferred_element_type=jnp.float32)]
    pallas_call x1, Pallas kernels: 170 us -> 211 us  [front(): pl.pallas_call(front_kernel, out_shape=outs, in_specs=[VMEM] * 8, out_spe...]
    pallas_call x5 -> x1, Pallas kernels: 193 us -> 160 us  [back(): pl.pallas_call(back_kernel, out_shape=outs, in_specs=[VMEM] * len(operand...]
    convert_element_type x2 -> x0, other arithmetic: 5.34 us -> none  [the longest x1 2.89 us: split_layer(): inputs = x_all.astype(F32)]
where the time goes in v4:
time: 405 us; the launch traced here: 399 us
  Pallas kernels  372 us (92%)
  local copies, waits for them, and re-layouts  19.1 us (5%)
  other arithmetic  6.67 us (2%)
    pallas_call x1, Pallas kernels, front(): pl.pallas_call(front_kernel, out_shape=outs, in_specs=[VMEM] * 8, out_spe...  211 us
    pallas_call x1, Pallas kernels, back(): pl.pallas_call(back_kernel, out_shape=outs, in_specs=[VMEM] * len(operand...  160 us

profile of v4, /device:TPU:0, one launch (start us, length us, event | category | flops | bytes accessed | tf_op | source)
XLA Modules:
  0.0 398.9 jit_solution(5408922013801449407)
XLA Ops:
  0.7 0.0 copy-start.1
  0.7 1.9 multiply_sine_fusion
  2.6 0.1 pad_negate_fusion
  2.6 0.0 copy-start.2
  2.7 1.3 pad_maximum_fusion.1
  4.0 0.0 copy-done.1
  4.0 0.3 reshape.100
  4.3 0.2 copy.49
  4.5 0.2 reshape.101
  4.6 0.0 copy-done.2
  4.6 0.0 copy-start.8
  4.6 0.3 reshape.102
  4.9 0.2 copy.48
  5.1 0.0 copy-start.9
  5.1 0.2 reshape.103
  5.2 0.0 copy-start.10
  5.2 0.0 copy-start.11
  5.3 1.0 pad_maximum_fusion.gate_up
  6.3 0.0 copy-done.7
  6.3 0.4 reshape_reshape.15
  6.7 0.3 copy.32
  6.9 0.4 pad.15
  7.4 0.3 reshape_reshape.16
  7.6 0.0 copy-done.8
  7.6 0.2 reshape_reshape.17
  7.9 0.1 copy.33
  8.0 0.2 pad.16
  8.2 0.1 reshape.98
  8.4 0.0 copy-done.9
  8.4 0.1 reshape.99
  8.5 0.0 copy-done.10
  8.6 0.1 copy.34
  8.7 0.9 concatenate.12
  9.7 211.2 %front.1 = (bf16[2,2,2,2,2,48,512]{6,5,4,3,2,1,0:T(8,128)(2,1)}, bf16[2,2,2,2,2,48,1024]{6,5,4,3,2,1,0:T(8,128)(2,1)}, bf16[2,2,128,1536]{3,2,1,0:T(8,128)(2,1)}...) custom-call(bf16[128,1536]{1,0:T(8,128)(2,1)} %tokens.1, ...), custom_call_target="tpu_custom_call" | custom-call | tf_op jit(solution)/shard_map/front/pallas_call | solution.py:955
  220.8 160.4 %back.1 = (bf16[128,1536]{1,0:T(8,128)(2,1)}, bf16[128,1536]{1,0:T(8,128)(2,1)}, bf16[8,48,1024]{2,1,0:T(8,128)(2,1)}, f32[128,1536]{1,0:T(8,128)}, bf16[8,48,51...) custom-call(f32[128,1536]{1,0:T(8,128)} %get-tuple-element.35.dh2, ...), custom_call_target="tpu_custom_call" | custom-call | tf_op jit(solution)/shard_map/back/pallas_call | solution.py:1226
  381.2 1.3 slice_convert_fusion
  382.6 0.3 reshape.131
  382.8 0.5 copy.42
  383.4 1.2 reshape.124
  384.6 0.3 reshape.133
  384.8 0.5 copy.43
  385.4 1.2 reshape.126
  386.6 0.1 convert_bitcast_fusion
  386.6 0.3 reshape.120
  386.9 0.1 slice.45
  387.1 0.7 reshape.110
  387.8 0.4 copy.44
  388.2 0.0 copy-start.4
  388.2 1.8 reshape_reshape.18
  390.1 0.6 slice_reduce_fusion
  390.6 0.2 reshape_squeeze.6
  390.9 0.1 copy.45
  391.0 1.2 reshape_reshape.19
  392.2 0.2 slice.49
  392.5 0.1 copy.40
  392.5 0.8 reshape_squeeze.7
  393.3 0.2 copy.41
  393.6 0.9 reshape.122
  394.4 1.0 convert_element_type.24
  395.4 0.8 slice.34
  396.2 0.1 constant_dynamic-slice_fusion
  396.3 0.5 slice_bitcast_fusion
  396.8 0.7 copy.52
  397.5 0.9 copy.53
  (19 shorter events, 0.2 us)
Async XLA Ops:
  0.7 3.3 copy-start.1
  2.6 2.0 copy-start.2
  4.0 2.2 copy-start.7
  4.6 3.0 copy-start.8
  5.1 3.3 copy-start.9
  5.2 3.3 copy-start.10
  5.2 3.3 copy-start.11
  383.4 3.2 copy-start.5
  387.8 5.5 %copy-start.6 = (bf16[8,48,256]{2,1,0:T(8,128)(2,1)S(1)}, bf16[8,48,256]{2,1,0:T(8,128)(2,1)}, u32[]{:S(2)}) copy-start(bf16[8,48,256]{2,1,0:T(8,128)(2,1)} %get-tuple-element.56) | copy-start | bytes 589828
  388.2 6.2 %copy-start.4 = (bf16[128,1536]{1,0:T(8,128)(2,1)S(1)}, bf16[128,1536]{1,0:T(8,128)(2,1)}, u32[]{:S(2)}) copy-start(bf16[128,1536]{1,0:T(8,128)(2,1)} %get-tuple-element.53) | copy-start | bytes 1179652
  390.6 6.2 %copy-start.3 = (bf16[128,1536]{1,0:T(8,128)(2,1)S(1)}, bf16[128,1536]{1,0:T(8,128)(2,1)}, u32[]{:S(2)}) copy-start(bf16[128,1536]{1,0:T(8,128)(2,1)} %get-tuple-element.80) | copy-start | bytes 1179652
  390.9 6.7 %copy-start = (f32[128,1536]{1,0:T(8,128)S(1)}, f32[128,1536]{1,0:T(8,128)}, u32[]{:S(2)}) copy-start(f32[128,1536]{1,0:T(8,128)} %get-tuple-element.90) | copy-start | bytes 2359300
